TPU v7x, 32 devices: a whole 2x2x4 slice. The times are simulated.
32 devices in a mesh: slab: 16 (over z, y, x), bal: 2 (over core).
Axes of the slice: x: 2, y: 2, z: 4, core: 2. Of those that a mesh axis runs over, the one named last changes fastest.
Arguments:
- order_parameter: float32 [16, 4, 32, 1024], P('slab', 'bal'), may hold values from -1 to 1
- concentration_excess: float32 [16, 4, 32, 1024], P('slab', 'bal'), may hold values from -1.8 to 1.8
- thermal_subcooling: float32 [16, 4, 32, 1024], P('slab', 'bal'), may hold values from -1.8 to 1.8
- holder_places_prior: int32 [16, 4], replicated, may hold values from 0 to 3, as said below
- holder_places_revised: int32 [16, 4], replicated, may hold values from 0 to 3, as said below
- update_flags: int32 [16, 4], replicated, may hold values 0 or 1
Outputs:
- phase_out: float32 [16, 4, 32, 1024], P('slab', 'bal')
- solute_out: float32 [16, 4, 32, 1024], P('slab', 'bal')
- temperature_out: float32 [16, 4, 32, 1024], P('slab', 'bal')
Inputs may be any that keep to these rules, and one draw needn't show every extreme that they name: `holder_places_prior`: each row is a permutation of the 4 positions of a layer; slot k belongs to the owner of index k // 2 along bal. `holder_places_revised`: each row is a permutation of the layer's positions. In every layer each owner gives exactly 1 of its blocks to other owners and receives exactly 1; every other block keeps its slot.
All inputs are finite; a program needn't handle non-finite values.
Results may differ from a plain program's by a relative error of at most 0.00002.
Values sent between devices are 32-bit elements; how exact they have to be, the bound alone decides.
No kernel may reach another device: no remote copies, remote signals or barrier semaphores. Data moves between devices by JAX's collectives and lax.ppermute only.
A program may use at most 64 MiB of HBM per device.

v0:
```python
import jax
import jax.numpy as jnp
from jax import lax
from jax.sharding import PartitionSpec as P

TILE_SIDE_POINTS = 32
BZ = 4
BLK_DEV = 2
MOVE = 1


RATE = 0.1
ANISO = 0.05
COUPLE = 0.5
DIFF_SOLUTE = 0.08
DIFF_HEAT = 0.15
TINY = 0.0001


def with_halo(block, sides, width):
    for axis, dim in sides:
        count = lax.axis_size(axis)
        forward = [(i, i + 1) for i in range(count - 1)]
        backward = [(target, source) for source, target in forward]
        low = lax.ppermute(
            lax.slice_in_dim(block, block.shape[dim] - width, None, axis=dim), axis, forward
        )
        high = lax.ppermute(lax.slice_in_dim(block, 0, width, axis=dim), axis, backward)
        block = jnp.concatenate([low, block, high], axis=dim)
    return block


def laplace(center, neighbours):
    return (
        neighbours[0]
        + neighbours[1]
        + (neighbours[2] + neighbours[3])
        + (neighbours[4] + neighbours[5])
        - 6.0 * center
    )


def march_forward(phase_now, solute_now, heat_now, near_phase, near_solute, near_heat, active_now):
    slope_x = 0.5 * (near_phase[0] - near_phase[1])
    slope_y = 0.5 * (near_phase[2] - near_phase[3])
    slope_z = 0.5 * (near_phase[4] - near_phase[5])
    sq_x = slope_x * slope_x
    sq_y = slope_y * slope_y
    sq_z = slope_z * slope_z
    slope_sq = sq_x + sq_y + sq_z
    quartic = sq_x * sq_x + sq_y * sq_y + sq_z * sq_z
    fourth_ratio = quartic / (slope_sq * slope_sq + TINY)
    anisotropy = 1.0 - 3.0 * ANISO + 4.0 * ANISO * fourth_ratio
    well_term = 1.0 - phase_now * phase_now
    forcing = (
        phase_now
        - phase_now * phase_now * phase_now
        - COUPLE * well_term * well_term * (solute_now + heat_now)
    )
    phase_new = phase_now + active_now * (
        RATE * (anisotropy * anisotropy * laplace(phase_now, near_phase) + forcing)
    )
    change = phase_new - phase_now
    solute_new = solute_now + DIFF_SOLUTE * laplace(solute_now, near_solute) + 0.5 * change
    heat_new = heat_now + DIFF_HEAT * laplace(heat_now, near_heat) + 0.5 * change
    return (phase_new, solute_new, heat_new)


def face_stack(quantities_bundle):
    stacks = []
    for quantity in quantities_bundle:
        blocks = quantity.shape[0]
        surfaces = [
            quantity[:, 0, :],
            quantity[:, -1, :],
            quantity[:, :, :TILE_SIDE_POINTS].reshape(blocks, -1),
            quantity[:, :, -TILE_SIDE_POINTS:].reshape(blocks, -1),
            quantity[:, :, 0::TILE_SIDE_POINTS].reshape(blocks, -1),
            quantity[:, :, TILE_SIDE_POINTS - 1 :: TILE_SIDE_POINTS].reshape(blocks, -1),
        ]
        stacks.append(jnp.stack(surfaces, axis=1))
    return jnp.stack(stacks, axis=2)


def halo_neighbours(center, border):
    blocks = center.shape[0]
    side = TILE_SIDE_POINTS
    x_padded = jnp.concatenate([border[0][:, None], center, border[1][:, None]], axis=1)
    y_padded = jnp.concatenate(
        [border[2].reshape(blocks, side, side), center, border[3].reshape(blocks, side, side)],
        axis=2,
    )
    x_upper = x_padded[:, 2:]
    x_lower = x_padded[:, :-2]
    y_upper = y_padded[:, :, 2 * side :]
    y_lower = y_padded[:, :, : side * side]
    z_index = lax.broadcasted_iota(jnp.int32, center.shape, 2) % side
    upper_face = jnp.broadcast_to(
        border[5].reshape(blocks, side, side, 1), (blocks, side, side, side)
    ).reshape(center.shape)
    lower_face = jnp.broadcast_to(
        border[4].reshape(blocks, side, side, 1), (blocks, side, side, side)
    ).reshape(center.shape)
    z_upper = jnp.where(z_index == side - 1, upper_face, jnp.roll(center, -1, axis=2))
    z_lower = jnp.where(z_index == 0, lower_face, jnp.roll(center, 1, axis=2))
    return (x_upper, x_lower, y_upper, y_lower, z_upper, z_lower)


def spread(own_faces):
    return lax.all_gather(own_faces, "bal", axis=0, tiled=True)


def ghosts(face_table, slot_lists, positions, own_faces, slab_at, slab_count):
    inverse_low, inverse_mid, inverse_high = slot_lists
    total = face_table.shape[0]
    rows_y = total // BZ
    block_row = positions // BZ
    block_col = positions % BZ
    y_lower = (block_row + rows_y - 1) % rows_y * BZ + block_col
    y_upper = (block_row + 1) % rows_y * BZ + block_col
    z_lower = block_row * BZ + (block_col + BZ - 1) % BZ
    z_upper = block_row * BZ + (block_col + 1) % BZ
    x_edges = jnp.take(face_table[:, 0:2], inverse_mid, axis=0)
    rim_faces = with_halo(x_edges, (("slab", 1),), 1)
    under_face = rim_faces[positions, 0]
    over_face = rim_faces[positions, 3]
    y_faces = (face_table[inverse_mid[y_lower], 3], face_table[inverse_mid[y_upper], 2])
    z_faces = (face_table[inverse_mid[z_lower], 5], face_table[inverse_mid[z_upper], 4])
    under_face = jnp.where(slab_at == 0, own_faces[:, 0], under_face)
    over_face = jnp.where(slab_at == slab_count - 1, own_faces[:, 1], over_face)
    return jnp.stack(
        [under_face, over_face, y_faces[0], y_faces[1], z_faces[0], z_faces[1]], axis=1
    )


def sweep(
    quantities_bundle, positions, own_faces, face_table, slot_lists, active_mid, slab_at, slab_count
):
    border = ghosts(face_table, slot_lists, positions, own_faces, slab_at, slab_count)
    active_now = active_mid[positions][:, None, None]
    near_sets = [
        halo_neighbours(
            quantities_bundle[index], tuple((border[:, side, index] for side in range(6)))
        )
        for index in range(3)
    ]
    return march_forward(
        quantities_bundle[0],
        quantities_bundle[1],
        quantities_bundle[2],
        near_sets[0],
        near_sets[1],
        near_sets[2],
        active_now,
    )


def layer_row(table, which, count):
    return lax.dynamic_slice_in_dim(table, jnp.clip(which, 0, count - 1), 1, 0)[0]


def inverse_of(perm):
    return jnp.argsort(perm)


def body(
    order_parameter,
    concentration_excess,
    thermal_subcooling,
    holder_places_prior,
    holder_places_revised,
    update_flags,
):
    slab_at = lax.axis_index("slab")
    slab_count = lax.axis_size("slab")
    bal_rank = lax.axis_index("bal")
    bal_count = lax.axis_size("bal")
    total = bal_count * BLK_DEV
    quantities_bundle = (order_parameter[0], concentration_excess[0], thermal_subcooling[0])
    active_mid = layer_row(update_flags, slab_at, slab_count).astype(jnp.float32)
    before_mid = layer_row(holder_places_prior, slab_at, slab_count)
    after_mid = layer_row(holder_places_revised, slab_at, slab_count)
    lists_before = tuple(
        (
            inverse_of(layer_row(holder_places_prior, slab_at + shift_by, slab_count))
            for shift_by in (-1, 0, 1)
        )
    )
    lists_after = tuple(
        (
            inverse_of(layer_row(holder_places_revised, slab_at + shift_by, slab_count))
            for shift_by in (-1, 0, 1)
        )
    )
    positions_before = lax.dynamic_slice_in_dim(before_mid, bal_rank * BLK_DEV, BLK_DEV)
    positions_after = lax.dynamic_slice_in_dim(after_mid, bal_rank * BLK_DEV, BLK_DEV)
    own_faces = face_stack(quantities_bundle)
    face_table = spread(own_faces)
    quantities_bundle = sweep(
        quantities_bundle,
        positions_before,
        own_faces,
        face_table,
        lists_before,
        active_mid,
        slab_at,
        slab_count,
    )
    owner_after = inverse_of(after_mid) // BLK_DEV
    slot_owner = jnp.arange(total, dtype=jnp.int32) // BLK_DEV
    leaving = (owner_after[before_mid] != slot_owner).astype(jnp.int32).reshape(bal_count, BLK_DEV)
    order = jnp.argsort(1 - leaving, axis=1, stable=True)[:, :MOVE]
    mover_slots = (jnp.arange(bal_count, dtype=jnp.int32)[:, None] * BLK_DEV + order).reshape(-1)
    mover_positions = before_mid[mover_slots]
    my_order = lax.dynamic_slice_in_dim(order, bal_rank, 1, 0)[0]
    outgoing = tuple((jnp.take(quantity, my_order, axis=0) for quantity in quantities_bundle))
    combined_positions = jnp.concatenate([positions_before, mover_positions], axis=0)
    chosen = jnp.argmax(combined_positions[None, :] == positions_after[:, None], axis=1)
    arrived = (
        lax.all_gather(outgoing[0], "bal", axis=0, tiled=True),
        lax.all_gather(outgoing[1], "bal", axis=0, tiled=True),
        lax.all_gather(outgoing[2], "bal", axis=0, tiled=True),
    )
    quantities_bundle = tuple(
        (
            jnp.take(
                jnp.concatenate([quantities_bundle[index], arrived[index]], axis=0), chosen, axis=0
            )
            for index in range(3)
        )
    )
    own_faces = face_stack(quantities_bundle)
    face_table = spread(own_faces)
    quantities_bundle = sweep(
        quantities_bundle,
        positions_after,
        own_faces,
        face_table,
        lists_after,
        active_mid,
        slab_at,
        slab_count,
    )
    return (quantities_bundle[0][None], quantities_bundle[1][None], quantities_bundle[2][None])


def solution(mesh):
    placed = (
        P("slab", "bal", None, None),
        P("slab", "bal", None, None),
        P("slab", "bal", None, None),
        P(),
        P(),
        P(),
    )
    return jax.shard_map(
        body,
        mesh=mesh,
        in_specs=placed,
        out_specs=(
            P("slab", "bal", None, None),
            P("slab", "bal", None, None),
            P("slab", "bal", None, None),
        ),
        check_vma=False,
    )
```

profile of v0, /device:TPU:8, one launch (start us, length us, event | category | flops | bytes accessed | tf_op | source)
XLA Modules:
  0.0 125.6 jit_solution(14324986880176407615)
XLA Ops:
  2.5 1.3 %slice.425 = f32[2,32,32]{2,1,0:T(8,128)S(1)} slice(f32[2,32,1024]{2,1,0:T(8,128)} %bitcast.223), slice={[0:2:1], [0:32:1], [0:1024:32]} | slice | bytes 16384 | tf_op jit(solution)/shard_map/slice | solution.py:78
  3.8 1.3 %slice.426 = f32[2,32,32]{2,1,0:T(8,128)S(1)} slice(f32[2,32,1024]{2,1,0:T(8,128)} %bitcast.224), slice={[0:2:1], [0:32:1], [31:1024:32]} | slice | bytes 16384 | tf_op jit(solution)/shard_map/slice | solution.py:79
  9.6 2.1 %all_gather.15 = f32[4,6,3,1024]{3,1,2,0:T(8,128)S(1)} all-gather(f32[2,6,3,1024]{3,1,2,0:T(8,128)S(1)} %pad_maximum_fusion.27), channel_id=1, replica_groups=mesh['slab'=16,'bal'=2] {'bal'}, dimensions={0}, use_global_device_ids=true | all-gather | bytes 442368 | tf_op jit(solution)/shard_map/all_gather | solution.py:110
  13.3 3.4 %collective-permute-start = (f32[4,1,3,1024]{3,1,2,0:T(1,128)}, f32[4,1,3,1024]{3,1,2,0:T(1,128)}, u32[]{:S(2)}, u32[]{:S(2)}) collective-permute-start(f32[4,1,3,1024]{3,1,2,0:T(1,128)} %get-tuple-element.119), channel_id=1, source_target_pairs={{0,2},{2,4},{4,6},{6,8},{8,10},{10,12},{12,14},{14,16},{16,18},{18... | collective-permute-start | bytes 147464 | tf_op jit(solution)/shard_map/ppermute | solution.py:25
  16.7 4.2 %collective-permute-start.1 = (f32[4,1,3,1024]{3,1,2,0:T(1,128)}, f32[4,1,3,1024]{3,1,2,0:T(1,128)}, u32[]{:S(2)}, u32[]{:S(2)}) collective-permute-start(f32[4,1,3,1024]{3,1,2,0:T(1,128)} %get-tuple-element.120), channel_id=1, source_target_pairs={{2,0},{4,2},{6,4},{8,6},{10,8},{12,10},{14,12},{16,14},{18,16},{20... | collective-permute-start | bytes 147464 | tf_op jit(solution)/shard_map/ppermute | solution.py:28
  57.8 1.1 broadcast_in_dim.154
  58.9 1.2 reshape.739
  60.8 1.1 broadcast_in_dim.156
  61.8 1.2 reshape.740
  65.8 1.1 broadcast_select_fusion.8
  68.5 2.0 %all_gather.18 = f32[2,32,1024]{2,1,0:T(8,128)S(1)} all-gather(f32[1,32,1024]{2,1,0:T(8,128)S(1)} %dynamic-slice_select_fusion), channel_id=1, replica_groups=mesh['slab'=16,'bal'=2] {'bal'}, dimensions={0}, use_global_device_ids=true | all-gather | bytes 393216 | tf_op jit(solution)/shard_map/all_gather | solution.py:222
  72.1 2.0 %all_gather.17 = f32[2,32,1024]{2,1,0:T(8,128)S(1)} all-gather(f32[1,32,1024]{2,1,0:T(8,128)S(1)} %dynamic-slice_select_fusion.1), channel_id=1, replica_groups=mesh['slab'=16,'bal'=2] {'bal'}, dimensions={0}, use_global_device_ids=true | all-gather | bytes 393216 | tf_op jit(solution)/shard_map/all_gather | solution.py:221
  75.6 2.2 %all_gather.16 = f32[2,32,1024]{2,1,0:T(8,128)S(1)} all-gather(f32[1,32,1024]{2,1,0:T(8,128)S(1)} %dynamic-slice_select_fusion.2), channel_id=1, replica_groups=mesh['slab'=16,'bal'=2] {'bal'}, dimensions={0}, use_global_device_ids=true | all-gather | bytes 393216 | tf_op jit(solution)/shard_map/all_gather | solution.py:220
  82.3 2.1 %all_gather.19 = f32[4,6,3,1024]{3,1,2,0:T(8,128)S(1)} all-gather(f32[2,6,3,1024]{3,1,2,0:T(8,128)S(1)} %pad_maximum_fusion.29), channel_id=1, replica_groups=mesh['slab'=16,'bal'=2] {'bal'}, dimensions={0}, use_global_device_ids=true | all-gather | bytes 442368 | tf_op jit(solution)/shard_map/all_gather | solution.py:110
  90.3 2.0 %collective-permute-start.2 = (f32[4,1,3,1024]{3,1,2,0:T(1,128)}, f32[4,1,3,1024]{3,1,2,0:T(1,128)}, u32[]{:S(2)}, u32[]{:S(2)}) collective-permute-start(f32[4,1,3,1024]{3,1,2,0:T(1,128)} %get-tuple-element.117), channel_id=1, source_target_pairs={{0,2},{2,4},{4,6},{6,8},{8,10},{10,12},{12,14},{14,16},{16,18},{18... | collective-permute-start | bytes 147464 | tf_op jit(solution)/shard_map/ppermute | solution.py:25
  92.3 5.7 %collective-permute-start.3 = (f32[4,1,3,1024]{3,1,2,0:T(1,128)}, f32[4,1,3,1024]{3,1,2,0:T(1,128)}, u32[]{:S(2)}, u32[]{:S(2)}) collective-permute-start(f32[4,1,3,1024]{3,1,2,0:T(1,128)} %get-tuple-element.118), channel_id=1, source_target_pairs={{2,0},{4,2},{6,4},{8,6},{10,8},{12,10},{14,12},{16,14},{18,16},{20... | collective-permute-start | bytes 147464 | tf_op jit(solution)/shard_map/ppermute | solution.py:28
  107.5 1.4 %reshape_squeeze.54 = f32[2,32,32]{2,1,0:T(8,128)} reshape(f32[2,1024]{1,0:T(2,128)} %get-tuple-element.39) | data formatting | bytes 16384 | tf_op jit(solution)/shard_map/reshape;squeeze | solution.py:90
  111.6 1.1 broadcast_in_dim.167
  112.7 1.2 reshape.745
  114.6 1.1 broadcast_in_dim.169
  115.7 1.2 reshape.746
  121.1 1.1 broadcast_select_fusion.7
  123.1 1.4 %fusion.37 = (f32[1,2,32,1024]{3,2,1,0:T(8,128)}, f32[2,32,1024]{2,1,0:T(8,128)S(1)}) fusion(f32[2,32,1024]{2,1,0:T(8,128)S(1)} %get-tuple-element.147, f32[2,32,1024]{2,1,0:T(8,128)S(1)} %reshape.748, f32[2,32,1024]{2,1,0:T(8,128)S(1)} %reshape.747, f32[2,32,32]{2,1,0:T(8,128)S(1)} %copy-done.27, f32[2,32,32]{2,1,0:T(8,128)S(1)} %copy-done.26, ...), kind=kLoop, calls=%fused_computation.75 | loop fusion | flops 4784128 | bytes 3482632 | tf_op jit(solution)/shard_map/broadcast_in_dim | solution.py:244
  124.6 1.0 fusion.30
  (347 shorter events, 78.4 us)
Async XLA Ops:
  0.6 4.4 %copy-start.2 = (f32[1,2,32,1024]{3,2,1,0:T(8,128)S(1)}, f32[1,2,32,1024]{3,2,1,0:T(8,128)}, u32[]{:S(2)}) copy-start(f32[1,2,32,1024]{3,2,1,0:T(8,128)} %param.13) | copy-start | bytes 786436
  1.5 4.3 %copy-start.1 = (f32[1,2,32,1024]{3,2,1,0:T(8,128)S(1)}, f32[1,2,32,1024]{3,2,1,0:T(8,128)}, u32[]{:S(2)}) copy-start(f32[1,2,32,1024]{3,2,1,0:T(8,128)} %param.14) | copy-start | bytes 786436
  9.6 2.1 %copy-start.16 = (f32[2,6,3,1024]{3,1,2,0:T(8,128)}, f32[2,6,3,1024]{3,1,2,0:T(8,128)S(1)}, u32[]{:S(2)}) copy-start(f32[2,6,3,1024]{3,1,2,0:T(8,128)S(1)} %pad_maximum_fusion.27) | copy-start | bytes 442372
  13.3 49.8 %collective-permute-start = (f32[4,1,3,1024]{3,1,2,0:T(1,128)}, f32[4,1,3,1024]{3,1,2,0:T(1,128)}, u32[]{:S(2)}, u32[]{:S(2)}) collective-permute-start(f32[4,1,3,1024]{3,1,2,0:T(1,128)} %get-tuple-element.119), channel_id=1, source_target_pairs={{0,2},{2,4},{4,6},{6,8},{8,10},{10,12},{12,14},{14,16},{16,18},{18... | collective-permute-start | bytes 147464 | tf_op jit(solution)/shard_map/ppermute | solution.py:25
  16.7 46.4 %collective-permute-start.1 = (f32[4,1,3,1024]{3,1,2,0:T(1,128)}, f32[4,1,3,1024]{3,1,2,0:T(1,128)}, u32[]{:S(2)}, u32[]{:S(2)}) collective-permute-start(f32[4,1,3,1024]{3,1,2,0:T(1,128)} %get-tuple-element.120), channel_id=1, source_target_pairs={{2,0},{4,2},{6,4},{8,6},{10,8},{12,10},{14,12},{16,14},{18,16},{20... | collective-permute-start | bytes 147464 | tf_op jit(solution)/shard_map/ppermute | solution.py:28
  64.0 3.0 %copy-start.6 = (f32[2,32,1023]{2,1,0:T(8,128)S(1)}, f32[2,32,1023]{2,1,0:T(8,128)}, u32[]{:S(2)}) copy-start(f32[2,32,1023]{2,1,0:T(8,128)} %get-tuple-element.163) | copy-start | bytes 785668
  64.0 3.0 %copy-start.37 = (f32[2,32,1]{2,1,0:T(8,128)S(1)}, f32[2,32,1]{2,1,0:T(8,128)}, u32[]{:S(2)}) copy-start(f32[2,32,1]{2,1,0:T(8,128)} %get-tuple-element.164) | copy-start | bytes 772
  64.1 3.0 %copy-start.38 = (f32[2,32,1]{2,1,0:T(8,128)S(1)}, f32[2,32,1]{2,1,0:T(8,128)}, u32[]{:S(2)}) copy-start(f32[2,32,1]{2,1,0:T(8,128)} %get-tuple-element.165) | copy-start | bytes 772
  64.2 2.9 %copy-start.5 = (f32[2,32,1023]{2,1,0:T(8,128)S(1)}, f32[2,32,1023]{2,1,0:T(8,128)}, u32[]{:S(2)}) copy-start(f32[2,32,1023]{2,1,0:T(8,128)} %get-tuple-element.162) | copy-start | bytes 785668
  82.3 2.1 %copy-start.17 = (f32[2,6,3,1024]{3,1,2,0:T(8,128)}, f32[2,6,3,1024]{3,1,2,0:T(8,128)S(1)}, u32[]{:S(2)}) copy-start(f32[2,6,3,1024]{3,1,2,0:T(8,128)S(1)} %pad_maximum_fusion.29) | copy-start | bytes 442372
  89.5 9.2 %copy-start.57 = (s32[2]{0:T(128)S(1)}, s32[2]{0:T(128)}, u32[]{:S(2)}) copy-start(s32[2]{0:T(128)} %fusion.100) | copy-start | bytes 28
  90.3 7.8 %copy-start.59 = (s32[2]{0:T(128)S(1)}, s32[2]{0:T(128)}, u32[]{:S(2)}) copy-start(s32[2]{0:T(128)} %fusion.95) | copy-start | bytes 28
  90.3 28.0 %collective-permute-start.2 = (f32[4,1,3,1024]{3,1,2,0:T(1,128)}, f32[4,1,3,1024]{3,1,2,0:T(1,128)}, u32[]{:S(2)}, u32[]{:S(2)}) collective-permute-start(f32[4,1,3,1024]{3,1,2,0:T(1,128)} %get-tuple-element.117), channel_id=1, source_target_pairs={{0,2},{2,4},{4,6},{6,8},{8,10},{10,12},{12,14},{14,16},{16,18},{18... | collective-permute-start | bytes 147464 | tf_op jit(solution)/shard_map/ppermute | solution.py:25
  92.3 26.0 %collective-permute-start.3 = (f32[4,1,3,1024]{3,1,2,0:T(1,128)}, f32[4,1,3,1024]{3,1,2,0:T(1,128)}, u32[]{:S(2)}, u32[]{:S(2)}) collective-permute-start(f32[4,1,3,1024]{3,1,2,0:T(1,128)} %get-tuple-element.118), channel_id=1, source_target_pairs={{2,0},{4,2},{6,4},{8,6},{10,8},{12,10},{14,12},{16,14},{18,16},{20... | collective-permute-start | bytes 147464 | tf_op jit(solution)/shard_map/ppermute | solution.py:28
  119.3 3.0 %copy-start.4 = (f32[2,32,1023]{2,1,0:T(8,128)S(1)}, f32[2,32,1023]{2,1,0:T(8,128)}, u32[]{:S(2)}) copy-start(f32[2,32,1023]{2,1,0:T(8,128)} %get-tuple-element.76) | copy-start | bytes 785668
  119.3 3.0 %copy-start.33 = (f32[2,32,1]{2,1,0:T(8,128)S(1)}, f32[2,32,1]{2,1,0:T(8,128)}, u32[]{:S(2)}) copy-start(f32[2,32,1]{2,1,0:T(8,128)} %get-tuple-element.73) | copy-start | bytes 772
  119.3 3.0 %copy-start.34 = (f32[2,32,1]{2,1,0:T(8,128)S(1)}, f32[2,32,1]{2,1,0:T(8,128)}, u32[]{:S(2)}) copy-start(f32[2,32,1]{2,1,0:T(8,128)} %get-tuple-element.74) | copy-start | bytes 772
  119.5 2.9 %copy-start.3 = (f32[2,32,1023]{2,1,0:T(8,128)S(1)}, f32[2,32,1023]{2,1,0:T(8,128)}, u32[]{:S(2)}) copy-start(f32[2,32,1023]{2,1,0:T(8,128)} %get-tuple-element.75) | copy-start | bytes 785668
  123.0 1.5 %copy-start.7 = (f32[2,32,1024]{2,1,0:T(8,128)S(1)}, f32[2,32,1024]{2,1,0:T(8,128)}, u32[]{:S(2)}) copy-start(f32[2,32,1024]{2,1,0:T(8,128)} %reshape.745) | copy-start | bytes 786436
  123.0 1.5 %copy-start.9 = (f32[2,32,1024]{2,1,0:T(8,128)S(1)}, f32[2,32,1024]{2,1,0:T(8,128)}, u32[]{:S(2)}) copy-start(f32[2,32,1024]{2,1,0:T(8,128)} %reshape.746) | copy-start | bytes 786436
  123.0 1.5 %copy-start.14 = (f32[2,32,1023]{2,1,0:T(8,128)S(1)}, f32[2,32,1023]{2,1,0:T(8,128)}, u32[]{:S(2)}) copy-start(f32[2,32,1023]{2,1,0:T(8,128)} %get-tuple-element.67) | copy-start | bytes 785668
  123.1 1.5 %copy-start.15 = (f32[2,32,1023]{2,1,0:T(8,128)S(1)}, f32[2,32,1023]{2,1,0:T(8,128)}, u32[]{:S(2)}) copy-start(f32[2,32,1023]{2,1,0:T(8,128)} %get-tuple-element.68) | copy-start | bytes 785668
  123.1 1.5 %copy-start.25 = (f32[2,32,32]{2,1,0:T(8,128)S(1)}, f32[2,32,32]{2,1,0:T(8,128)}, u32[]{:S(2)}) copy-start(f32[2,32,32]{2,1,0:T(8,128)} %reshape_squeeze.57) | copy-start | bytes 24580
  123.1 1.5 %copy-start.30 = (f32[2,32,1]{2,1,0:T(8,128)S(1)}, f32[2,32,1]{2,1,0:T(8,128)}, u32[]{:S(2)}) copy-start(f32[2,32,1]{2,1,0:T(8,128)} %get-tuple-element.65) | copy-start | bytes 772
  (46 other events, 42.7 us)
where the time goes:
time: 127 us; the launch traced here: 126 us
  local copies, waits for them, and re-layouts  77.4 us (61%)
  other arithmetic  18.8 us (15%)
  starting transfers between devices  15.4 us (12%)
  blocking collectives  10.3 us (8%)
  between operations  3.66 us (3%)
    ppermute x2, starting transfers between devices, with_halo(): lax.ppermute(lax.slice_in_dim(block, 0, width, axis=dim), axis, backward)  9.96 us
    unnamed x132, local copies, waits for them, and re-layouts  8.27 us
    ppermute x2, starting transfers between devices, with_halo(): lax.ppermute(lax.slice_in_dim(block, block.shape[dim] - width, None, axis...  5.43 us
    broadcast_in_dim x12, local copies, waits for them, and re-layouts, halo_neighbours(): jnp.broadcast_to(border[4].reshape(blocks, side, side, 1), (blocks, side,...  5.24 us
    broadcast_in_dim x12, local copies, waits for them, and re-layouts, halo_neighbours(): jnp.broadcast_to(border[5].reshape(blocks, side, side, 1), (blocks, side,...  5.23 us
    slice x6, local copies, waits for them, and re-layouts, halo_neighbours(): z_lower = jnp.where(z_index == 0, lower_face, jnp.roll(center, 1, axis=2))  4.63 us
    reshape x6, local copies, waits for them, and re-layouts, halo_neighbours(): lower_face = jnp.broadcast_to(border[4].reshape(blocks, side, side, 1), (...  4.37 us
    reshape x6, local copies, waits for them, and re-layouts, halo_neighbours(): upper_face = jnp.broadcast_to(border[5].reshape(blocks, side, side, 1), (...  4.36 us
  transfers between devices with their start and end apart: 4, of which 0 were waited for; matrix products, arithmetic and copies ran while one was open for 45% of the time, Pallas kernels for 0%

commit v1 on v0

v1 whole, which is shorter than its diff:
```python
import functools

import jax
import jax.numpy as jnp
from jax import lax
from jax.experimental import pallas as pl
from jax.experimental.pallas import tpu as pltpu
from jax.sharding import PartitionSpec as P

RATE = 0.1
ANISO = 0.05
COUPLE = 0.5
DIFF_SOLUTE = 0.08
DIFF_HEAT = 0.15
TINY = 0.0001
ROWS, LANES = 8, 128
EDGE = 2
FIELDS = 3
AXES = ("slab", "bal")
VMEM_BYTES = 40 * 2**20


def tiles_of(block):
    blocks, side, cells = block.shape
    split = block.reshape(blocks, side // ROWS, ROWS, cells // LANES, LANES)
    return split.transpose(0, 1, 3, 2, 4).reshape(blocks, side * cells // LANES, LANES)


def block_of(tiles, side):
    blocks, rows, _ = tiles.shape
    columns = rows // side
    split = tiles.reshape(blocks, side // ROWS, columns, ROWS, LANES)
    return split.transpose(0, 1, 3, 2, 4).reshape(blocks, side, columns * LANES)


def plane_rows(x):
    return pl.ds((x // ROWS) * ROWS * ROWS + x % ROWS, ROWS, stride=ROWS)


def lane_ids():
    return lax.broadcasted_iota(jnp.int32, (ROWS, LANES), 1)


class Geometry:
    def __init__(self, side):
        lanes = lane_ids()
        self.side = side
        self.y_last = lanes >= LANES - side
        self.y_first = lanes < side
        self.z_first = lanes % side == 0
        self.z_last = lanes % side == side - 1

    def up(self, plane):
        return pltpu.roll(plane, LANES - self.side, 1)

    def down(self, plane):
        return pltpu.roll(plane, self.side, 1)

    def y_pair(self, up, down):
        upper = jnp.where(self.y_last, pltpu.roll(up, ROWS - 1, 0), up)
        lower = jnp.where(self.y_first, pltpu.roll(down, 1, 0), down)
        return upper, lower

    def z_pair(self, plane, next_down, previous_up):
        upper = pltpu.roll(jnp.where(self.z_first, next_down, plane), LANES - 1, 1)
        lower = pltpu.roll(jnp.where(self.z_last, previous_up, plane), 1, 1)
        return upper, lower


def advance(centers, sums, differences, rate):
    phase, solute, heat = centers
    sum_phase, sum_solute, sum_heat = sums
    squares = [d * d for d in differences]
    square = squares[0] + squares[1] + squares[2]
    quartic = squares[0] * squares[0] + squares[1] * squares[1] + squares[2] * squares[2]
    below = square * square + 16.0 * TINY
    anisotropy = (1.0 - 3.0 * ANISO) + 4.0 * ANISO * (quartic / below)
    well = 1.0 - phase * phase
    forcing = well * (phase - COUPLE * well * (solute + heat))
    change = rate * (anisotropy * anisotropy * (sum_phase - 6.0 * phase) + forcing)
    half = 0.5 * change
    return (
        phase + change,
        (1.0 - 6.0 * DIFF_SOLUTE) * solute + (DIFF_SOLUTE * sum_solute + half),
        (1.0 - 6.0 * DIFF_HEAT) * heat + (DIFF_HEAT * sum_heat + half),
    )


def step_plane(geometry, below, center, above, next_down, previous_up, rate):
    sums, differences = [], None
    for f in range(FIELDS):
        y_upper, y_lower = geometry.y_pair(geometry.up(center[f]), geometry.down(center[f]))
        z_upper, z_lower = geometry.z_pair(center[f], next_down[f], previous_up[f])
        sums.append((above[f] + below[f]) + (y_upper + y_lower) + (z_upper + z_lower))
        if f == 0:
            differences = (above[f] - below[f], y_upper - y_lower, z_upper - z_lower)
    return advance(center, sums, differences, rate)


def step_ring(geometry, load_below, load_center, load_above, rates):
    ring = len(rates)
    centers = [load_center(p) for p in range(ring)]
    ups = [[geometry.up(c) for c in center] for center in centers]
    downs = [[geometry.down(c) for c in center] for center in centers]
    return [
        step_plane(
            geometry,
            load_below(p),
            centers[p],
            load_above(p),
            downs[(p + 1) % ring],
            ups[(p - 1) % ring],
            rates[p],
        )
        for p in range(ring)
    ]


def planes_at(ref, p, x):
    return [ref[f, p, x] for f in range(FIELDS)]


def pack_kernel(side, *refs):
    fields, (even_ref, odd_ref), (tiles, sem) = refs[:FIELDS], refs[FIELDS : FIELDS + 2], refs[FIELDS + 2 :]
    blocks = even_ref.shape[1]
    rows = ROWS * ROWS
    last = side * ROWS - rows
    copies = [
        pltpu.make_async_copy(fields[f].at[:, pl.ds(start, rows)], tiles.at[f, end], sem.at[f, end])
        for f in range(FIELDS)
        for end, start in enumerate((0, last))
    ]
    for copy in copies:
        copy.start()
    parity = lax.rem(lax.axis_index("slab"), 2)
    for copy in copies:
        copy.wait()
    for f in range(FIELDS):
        for b in range(blocks):
            for d in range(EDGE):
                for ref, end in ((even_ref, 1 - parity), (odd_ref, parity)):
                    row = jnp.where(end == 0, d, ROWS - 1 - d)
                    ref[f, b, d] = tiles[f, end, b, pl.ds(row, ROWS, stride=ROWS)]


def inner_kernel(side, blocks, cores, *refs):
    own, other = refs[:FIELDS], refs[FIELDS : 2 * FIELDS]
    before, after, flags = refs[2 * FIELDS : 2 * FIELDS + 3]
    outs = refs[2 * FIELDS + 3 : 3 * FIELDS + 3]
    rim_raw, rim_step, rim_out = refs[3 * FIELDS + 3 : 3 * FIELDS + 6]
    tiles, raw, stepped, result, in_sem, out_sem = refs[3 * FIELDS + 6 :]
    ring = blocks * cores
    layer, core = lax.axis_index("slab"), lax.axis_index("bal")
    copies = []
    for c, source in enumerate((own, other)):
        for f in range(FIELDS):
            copies.append(pltpu.make_async_copy(source[f], tiles.at[c, f], in_sem.at[c, f]))
            copies[-1].start()
    geometry = Geometry(side)
    rates = [jnp.where(flags[p, layer] != 0, jnp.float32(RATE), jnp.float32(0.0)) for p in range(ring)]
    for c in range(cores):
        slot = jnp.where(c == 0, core, cores - 1 - core) * blocks
        for f in range(FIELDS):
            copies[c * FIELDS + f].wait()
            for b in range(blocks):
                p = before[slot + b, layer]

                @pl.loop(0, side, unroll=8)
                def _(x, c=c, f=f, b=b, p=p):
                    raw[f, p, x] = tiles[c, f, b, plane_rows(x)]

    @pl.loop(1, side - 1)
    def _(x):
        new = step_ring(
            geometry,
            lambda p: planes_at(raw, p, x - 1),
            lambda p: planes_at(raw, p, x),
            lambda p: planes_at(raw, p, x + 1),
            rates,
        )
        for p in range(ring):
            for f in range(FIELDS):
                stepped[f, p, x] = new[p][f]

    for end in range(2):
        for d in range(EDGE):
            for f in range(FIELDS):
                for p in range(ring):
                    rim_raw[end, f, p, d] = raw[f, p, d if end == 0 else side - 1 - d]
                    rim_step[end, f, p, d] = stepped[f, p, 1 + d if end == 0 else side - 2 - d]

    places = [after[core * blocks + b, layer] for b in range(blocks)]

    @pl.loop(2, side - 2)
    def _(x):
        for b in range(blocks):
            p = places[b]
            following, previous = lax.rem(p + 1, ring), lax.rem(p + ring - 1, ring)
            new = step_plane(
                geometry,
                planes_at(stepped, p, x - 1),
                planes_at(stepped, p, x),
                planes_at(stepped, p, x + 1),
                [geometry.down(c) for c in planes_at(stepped, following, x)],
                [geometry.up(c) for c in planes_at(stepped, previous, x)],
                jnp.where(flags[p, layer] != 0, jnp.float32(RATE), jnp.float32(0.0)),
            )
            for f in range(FIELDS):
                result[f, b, plane_rows(x)] = new[f]

    rows = ROWS * ROWS
    middle = pl.ds(rows, side * ROWS - 2 * rows)
    copies = []
    for f in range(FIELDS):
        copies.append(pltpu.make_async_copy(result.at[f, :, middle], outs[f].at[:, middle], out_sem.at[f]))
        copies[-1].start()
    for f in range(FIELDS):
        for end in range(2):
            part = pl.ds(end * (side * ROWS - rows), rows)
            rim_out[f, end] = result[f, :, part]
    for copy in copies:
        copy.wait()


def rim_kernel(side, blocks, cores, layers, *refs):
    rim_raw, rim_step, rim_out = refs[:3]
    even, odd, even_other, odd_other = refs[3:7]
    before, after, flags = refs[7:10]
    outs = refs[10 + FIELDS : 10 + 2 * FIELDS]
    halo, stepped, tiles, sem = refs[10 + 2 * FIELDS :]
    ring = blocks * cores
    layer, core = lax.axis_index("slab"), lax.axis_index("bal")
    parity = lax.rem(layer, 2)
    geometry = Geometry(side)
    rows = ROWS * ROWS

    def rate_of(which, p):
        return jnp.where(flags[p, which] != 0, jnp.float32(RATE), jnp.float32(0.0))

    for f in range(FIELDS):
        for end in range(2):
            tiles[f, end] = rim_out[f, end]

    for message, pair in enumerate(((even, even_other), (odd, odd_other))):
        end = (1 - parity) if message == 0 else parity
        beside = layer + 2 * end - 1
        outside = jnp.logical_or(beside < 0, beside >= layers)
        table = jnp.clip(beside, 0, layers - 1)

        @pl.when(jnp.logical_not(outside))
        def _(pair=pair, end=end, table=table):
            for c in range(cores):
                slot = jnp.where(c == 0, core, cores - 1 - core) * blocks
                for b in range(blocks):
                    p = before[slot + b, table]
                    for f in range(FIELDS):
                        for d in range(EDGE):
                            halo[end, f, p, d] = pair[c][f, b, d]

        @pl.when(outside)
        def _(end=end):
            for p in range(ring):
                for f in range(FIELDS):
                    for d in range(EDGE):
                        halo[end, f, p, d] = rim_raw[end, f, p, 0]

    def at(ref, end, p, d):
        return [ref[end, f, p, d] for f in range(FIELDS)]

    places = [after[core * blocks + b, layer] for b in range(blocks)]
    copies = []
    for end in range(2):
        beside = layer + 2 * end - 1
        outside = jnp.logical_or(beside < 0, beside >= layers)
        table = jnp.clip(beside, 0, layers - 1)
        face = step_ring(
            geometry,
            lambda p: at(halo, end, p, 0),
            lambda p: at(rim_raw, end, p, 0),
            lambda p: at(rim_raw, end, p, 1),
            [rate_of(layer, p) for p in range(ring)],
        )
        beyond = step_ring(
            geometry,
            lambda p: at(halo, end, p, 1),
            lambda p: at(halo, end, p, 0),
            lambda p: at(rim_raw, end, p, 0),
            [rate_of(table, p) for p in range(ring)],
        )
        for p in range(ring):
            for f in range(FIELDS):
                stepped[end, f, p, 0] = jnp.where(outside, face[p][f], beyond[p][f])
                stepped[end, f, p, 1] = face[p][f]
                for d in range(EDGE):
                    stepped[end, f, p, 2 + d] = rim_step[end, f, p, d]
        for d in range(EDGE):
            for b in range(blocks):
                p = places[b]
                following, previous = lax.rem(p + 1, ring), lax.rem(p + ring - 1, ring)
                new = step_plane(
                    geometry,
                    at(stepped, end, p, d),
                    at(stepped, end, p, d + 1),
                    at(stepped, end, p, d + 2),
                    [geometry.down(c) for c in at(stepped, end, following, d + 1)],
                    [geometry.up(c) for c in at(stepped, end, previous, d + 1)],
                    rate_of(layer, p),
                )
                row = d if end == 0 else ROWS - 1 - d
                for f in range(FIELDS):
                    tiles[f, end, b, pl.ds(row, ROWS, stride=ROWS)] = new[f]
        for f in range(FIELDS):
            part = pl.ds(end * (side * ROWS - rows), rows)
            copies.append(pltpu.make_async_copy(tiles.at[f, end], outs[f].at[:, part], sem.at[f, end]))
            copies[-1].start()
    for copy in copies:
        copy.wait()


def neighbour_swaps(layers, cores, first):
    pairs = []
    for layer in range(layers):
        partner = layer + 1 if (layer - first) % 2 == 0 else layer - 1
        for core in range(cores):
            here = layer * cores + core
            if 0 <= partner < layers:
                pairs.append((here, partner * cores + core))
            else:
                pairs.append((here, layer * cores + cores - 1 - core))
    return pairs


def body(layers, cores, order_parameter, concentration_excess, thermal_subcooling, before, after, flags):
    blocks, side = order_parameter.shape[1], order_parameter.shape[2]
    ring = blocks * cores
    rows = side * ROWS
    f32 = jnp.float32
    before, after, flags = before.T, after.T, flags.T
    owners = [(s * cores + c, s * cores + cores - 1 - c) for s in range(layers) for c in range(cores)]
    fields = [tiles_of(a[0]) for a in (order_parameter, concentration_excess, thermal_subcooling)]
    others = [lax.ppermute(a, AXES, owners) for a in fields]
    vmem, hbm, smem = (pl.BlockSpec(memory_space=m) for m in (pltpu.VMEM, pl.ANY, pltpu.SMEM))
    message = jax.ShapeDtypeStruct((FIELDS, blocks, EDGE, ROWS, LANES), f32)
    even, odd = pl.pallas_call(
        functools.partial(pack_kernel, side),
        out_shape=(message, message),
        in_specs=[hbm] * FIELDS,
        out_specs=(vmem, vmem),
        scratch_shapes=[
            pltpu.VMEM((FIELDS, 2, blocks, ROWS * ROWS, LANES), f32),
            pltpu.SemaphoreType.DMA((FIELDS, 2)),
        ],
        compiler_params=pltpu.CompilerParams(vmem_limit_bytes=VMEM_BYTES),
        cost_estimate=pl.CostEstimate(flops=0, bytes_accessed=10**6, transcendentals=0),
    )(*fields)
    odd_in = lax.ppermute(odd, AXES, neighbour_swaps(layers, cores, 1))
    even_in = lax.ppermute(even, AXES, neighbour_swaps(layers, cores, 0))
    rim = jax.ShapeDtypeStruct((2, FIELDS, ring, EDGE, ROWS, LANES), f32)
    whole = jax.ShapeDtypeStruct((blocks, rows, LANES), f32)
    rim_tiles = (FIELDS, 2, blocks, ROWS * ROWS, LANES)
    *parts, rim_raw, rim_step, rim_out = pl.pallas_call(
        functools.partial(inner_kernel, side, blocks, cores),
        out_shape=(whole,) * FIELDS + (rim, rim, jax.ShapeDtypeStruct(rim_tiles, f32)),
        in_specs=[hbm] * (2 * FIELDS) + [smem] * 3,
        out_specs=(hbm,) * FIELDS + (vmem,) * 3,
        scratch_shapes=[
            pltpu.VMEM((cores, FIELDS, blocks, rows, LANES), f32),
            pltpu.VMEM((FIELDS, ring, side, ROWS, LANES), f32),
            pltpu.VMEM((FIELDS, ring, side, ROWS, LANES), f32),
            pltpu.VMEM((FIELDS, blocks, rows, LANES), f32),
            pltpu.SemaphoreType.DMA((cores, FIELDS)),
            pltpu.SemaphoreType.DMA((FIELDS,)),
        ],
        compiler_params=pltpu.CompilerParams(vmem_limit_bytes=VMEM_BYTES),
        cost_estimate=pl.CostEstimate(flops=0, bytes_accessed=10**7, transcendentals=0),
    )(*fields, *others, before, after, flags)
    odd_in, even_in, rim_raw = lax.optimization_barrier((odd_in, even_in, rim_raw))
    odd_other = lax.ppermute(odd_in, AXES, owners)
    even_other = lax.ppermute(even_in, AXES, owners)
    results = pl.pallas_call(
        functools.partial(rim_kernel, side, blocks, cores, layers),
        out_shape=(whole,) * FIELDS,
        in_specs=[vmem] * 7 + [smem] * 3 + [hbm] * FIELDS,
        out_specs=(hbm,) * FIELDS,
        input_output_aliases={10 + f: f for f in range(FIELDS)},
        scratch_shapes=[
            pltpu.VMEM((2, FIELDS, ring, EDGE, ROWS, LANES), f32),
            pltpu.VMEM((2, FIELDS, ring, 2 + EDGE, ROWS, LANES), f32),
            pltpu.VMEM(rim_tiles, f32),
            pltpu.SemaphoreType.DMA((FIELDS, 2)),
        ],
        compiler_params=pltpu.CompilerParams(vmem_limit_bytes=VMEM_BYTES),
        cost_estimate=pl.CostEstimate(flops=0, bytes_accessed=10**6, transcendentals=0),
    )(rim_raw, rim_step, rim_out, even_in, odd_in, even_other, odd_other, before, after, flags, *parts)
    return tuple(block_of(r, side)[None] for r in results)


def solution(mesh):
    layers, cores = mesh.shape["slab"], mesh.shape["bal"]
    split, copied = P("slab", "bal", None, None), P()
    return jax.shard_map(
        functools.partial(body, layers, cores),
        mesh=mesh,
        in_specs=(split,) * 3 + (copied,) * 3,
        out_specs=(split,) * 3,
        check_vma=False,
    )
```

time: 127 us -> 27.7 us (0.22)
  the two profiles are of different devices: /device:TPU:8 before, /device:TPU:0 now
where the time goes in v1:
time: 27.7 us; the launch traced here: 27.5 us
  Pallas kernels  16.6 us (60%)
  starting transfers between devices  5.72 us (21%)
  local copies, waits for them, and re-layouts  3.53 us (13%)
  waiting for transfers between devices  0.89 us (3%)
  between operations  0.71 us (3%)
    pallas_call x1, Pallas kernels, body(): pl.pallas_call(functools.partial(inner_kernel, side, blocks, cores), out_...  14.2 us
    ppermute x1, starting transfers between devices, body(): even_in = lax.ppermute(even, AXES, neighbour_swaps(layers, cores, 0))  3.98 us
    unnamed x12, local copies, waits for them, and re-layouts  3.53 us
    pallas_call x1, Pallas kernels, body(): pl.pallas_call(functools.partial(rim_kernel, side, blocks, cores, layers)...  2.11 us
    ppermute x3, starting transfers between devices, body(): others = [lax.ppermute(a, AXES, owners) for a in fields]  1.03 us
    ppermute x1, waiting for transfers between devices, body(): even_other = lax.ppermute(even_in, AXES, owners)  0.72 us
  transfers between devices with their start and end apart: 7, of which 2 were waited for; matrix products, arithmetic and copies ran while one was open for 0% of the time, Pallas kernels for 53%

profile of v1, /device:TPU:0, one launch (start us, length us, event | category | flops | bytes accessed | tf_op | source)
XLA Modules:
  0.0 27.5 jit_solution(11585628743712563277)
XLA Ops:
  0.6 0.5 %collective-permute-start.2 = (f32[2,256,128]{2,1,0:T(8,128)}, f32[2,256,128]{2,1,0:T(8,128)S(1)}, u32[]{:S(2)}, u32[]{:S(2)}) collective-permute-start(f32[2,256,128]{2,1,0:T(8,128)} %bitcast.33), channel_id=1, source_target_pairs={{0,1},{1,0},{2,3},{3,2},{4,5},{5,4},{6,7},{7,6},{8,9},{9,8},{10,11... | collective-permute-start | bytes 786440 | tf_op jit(solution)/shard_map/ppermute | solution.py:341
  1.1 0.1 collective-permute-start.3
  1.2 0.4 %collective-permute-start.4 = (f32[2,256,128]{2,1,0:T(8,128)}, f32[2,256,128]{2,1,0:T(8,128)S(1)}, u32[]{:S(2)}, u32[]{:S(2)}) collective-permute-start(f32[2,256,128]{2,1,0:T(8,128)} %bitcast.39), channel_id=1, source_target_pairs={{0,1},{1,0},{2,3},{3,2},{4,5},{5,4},{6,7},{7,6},{8,9},{9,8},{10,11... | collective-permute-start | bytes 786440 | tf_op jit(solution)/shard_map/ppermute | solution.py:341
  1.7 0.9 %copy-done = f32[1,2,32,1024]{3,2,1,0:T(8,128)S(1)} copy-done((f32[1,2,32,1024]{3,2,1,0:T(8,128)S(1)}, f32[1,2,32,1024]{3,2,1,0:T(8,128)}, u32[]{:S(2)}) %copy-start) | copy-done | bytes 262168
  2.6 0.9 %copy-done.1 = f32[1,2,32,1024]{3,2,1,0:T(8,128)S(1)} copy-done((f32[1,2,32,1024]{3,2,1,0:T(8,128)S(1)}, f32[1,2,32,1024]{3,2,1,0:T(8,128)}, u32[]{:S(2)}) %copy-start.1) | copy-done | bytes 262168
  3.6 0.9 %copy-done.2 = f32[1,2,32,1024]{3,2,1,0:T(8,128)S(1)} copy-done((f32[1,2,32,1024]{3,2,1,0:T(8,128)S(1)}, f32[1,2,32,1024]{3,2,1,0:T(8,128)}, u32[]{:S(2)}) %copy-start.2) | copy-done | bytes 262168
  4.5 0.3 %shard_map.85 = (f32[3,2,2,8,128]{4,3,2,1,0:T(8,128)S(1)}, f32[3,2,2,8,128]{4,3,2,1,0:T(8,128)S(1)}) custom-call(f32[2,256,128]{2,1,0:T(8,128)S(1)} %bitcast.34, f32[2,256,128]{2,1,0:T(8,128)S(1)} %bitcast.37, f32[2,256,128]{2,1,0:T(8,128)S(1)} %bitcast.40), custom_call_target="tpu_custom_call" | custom-call | bytes 1000000 | tf_op jit(solution)/shard_map/pallas_call | solution.py:344
  4.9 0.1 collective-permute-start
  5.0 4.0 %collective-permute-start.1 = (f32[3,2,2,8,128]{4,3,2,1,0:T(8,128)S(1)}, f32[3,2,2,8,128]{4,3,2,1,0:T(8,128)S(1)}, u32[]{:S(2)}, u32[]{:S(2)}) collective-permute-start(f32[3,2,2,8,128]{4,3,2,1,0:T(8,128)S(1)} %get-tuple-element.18), channel_id=1, source_target_pairs={{0,2},{1,3},{2,0},{3,1},{4,6},{5,7},{6,4},{7,5},{8,10},{9,11},{10,... | collective-permute-start | bytes 147464 | tf_op jit(solution)/shard_map/ppermute | solution.py:357
  9.0 0.0 collective-permute-done.2.refs_3_
  9.0 0.0 collective-permute-done.3.refs_4_
  9.0 0.0 collective-permute-done.4.refs_5_
  9.0 0.0 copy-start.4
  9.0 0.0 copy-start.3
  9.0 0.7 %copy-done.4 = s32[16,4]{0,1:T(4,128)S(1)} copy-done((s32[16,4]{0,1:T(4,128)S(1)}, s32[16,4]{0,1:T(4,128)}, u32[]{:S(2)}) %copy-start.4) | copy-done | bytes 280
  9.7 0.0 copy-done.3
  9.7 14.2 %shard_map.86 = (f32[2,256,128]{2,1,0:T(8,128)}, f32[2,256,128]{2,1,0:T(8,128)}, f32[2,256,128]{2,1,0:T(8,128)}, f32[2,3,4,2,8,128]{5,4,3,2,1,0:T(8,128)S(1)}, f...) custom-call(f32[2,256,128]{2,1,0:T(8,128)S(1)} %bitcast.35, f32[2,256,128]{2,1,0:T(8,128)S(1)} %bitcast.38, ...), custom_call_target="tpu_custom_call" | custom-call | bytes 10000000 | tf_op jit(solution)/shard_map/pallas_call | solution.py:361
  23.9 0.0 collective-permute-done.refs_4_
  23.9 0.0 collective-permute-done.1.refs_3_
  23.9 0.1 collective-permute-start.5
  24.0 0.5 %collective-permute-start.6 = (f32[3,2,2,8,128]{4,3,2,1,0:T(8,128)S(1)}, f32[3,2,2,8,128]{4,3,2,1,0:T(8,128)S(1)}, u32[]{:S(2)}, u32[]{:S(2)}) collective-permute-start(f32[3,2,2,8,128]{4,3,2,1,0:T(8,128)S(1)} %collective-permute-done.refs_4_), channel_id=1, source_target_pairs={{0,1},{1,0},{2,3},{3,2},{4,5},{5,4},{6,7},{7,6},{8,9},{9,8},{10,11... | collective-permute-start | bytes 147464 | tf_op jit(solution)/shard_map/ppermute | solution.py:378
  24.5 0.7 %collective-permute-done.5.refs_5_ = f32[3,2,2,8,128]{4,3,2,1,0:T(8,128)S(1)} collective-permute-done((f32[3,2,2,8,128]{4,3,2,1,0:T(8,128)S(1)}, f32[3,2,2,8,128]{4,3,2,1,0:T(8,128)S(1)}, u32[]{:S(2)}, u32[]{:S(2)}) %collective-permute-start.5) | collective-permute-done | bytes 49184 | tf_op jit(solution)/shard_map/ppermute | solution.py:379
  25.2 0.2 collective-permute-done.6.refs_6_
  25.4 2.1 %shard_map.87 = (f32[2,256,128]{2,1,0:T(8,128)}, f32[2,256,128]{2,1,0:T(8,128)}, f32[2,256,128]{2,1,0:T(8,128)}) custom-call(f32[2,3,4,2,8,128]{5,4,3,2,1,0:T(8,128)S(1)} %get-tuple-element.20.refs_0_, f32[2,3,4,2,8,128]{5,4,3,2,1,0:T(8,128)S(1)} %get-tuple-element.21.refs_1_, ...), custom_call_target="tpu_custom_call", output_to_operand_aliasing={{0}: (10, {}), {1}: (11, {}), {2}: (12, {})} | custom-call | bytes 1000000 | tf_op jit(solution)/shard_map/pallas_call | solution.py:380
  (5 shorter events, 0.0 us)
Async XLA Ops:
  0.6 8.4 %collective-permute-start.2 = (f32[2,256,128]{2,1,0:T(8,128)}, f32[2,256,128]{2,1,0:T(8,128)S(1)}, u32[]{:S(2)}, u32[]{:S(2)}) collective-permute-start(f32[2,256,128]{2,1,0:T(8,128)} %bitcast.33), channel_id=1, source_target_pairs={{0,1},{1,0},{2,3},{3,2},{4,5},{5,4},{6,7},{7,6},{8,9},{9,8},{10,11... | collective-permute-start | bytes 786440 | tf_op jit(solution)/shard_map/ppermute | solution.py:341
  1.1 7.8 %collective-permute-start.3 = (f32[2,256,128]{2,1,0:T(8,128)}, f32[2,256,128]{2,1,0:T(8,128)S(1)}, u32[]{:S(2)}, u32[]{:S(2)}) collective-permute-start(f32[2,256,128]{2,1,0:T(8,128)} %bitcast.36), channel_id=1, source_target_pairs={{0,1},{1,0},{2,3},{3,2},{4,5},{5,4},{6,7},{7,6},{8,9},{9,8},{10,11... | collective-permute-start | bytes 786440 | tf_op jit(solution)/shard_map/ppermute | solution.py:341
  1.2 7.8 %collective-permute-start.4 = (f32[2,256,128]{2,1,0:T(8,128)}, f32[2,256,128]{2,1,0:T(8,128)S(1)}, u32[]{:S(2)}, u32[]{:S(2)}) collective-permute-start(f32[2,256,128]{2,1,0:T(8,128)} %bitcast.39), channel_id=1, source_target_pairs={{0,1},{1,0},{2,3},{3,2},{4,5},{5,4},{6,7},{7,6},{8,9},{9,8},{10,11... | collective-permute-start | bytes 786440 | tf_op jit(solution)/shard_map/ppermute | solution.py:341
  1.7 0.9 %copy-start = (f32[1,2,32,1024]{3,2,1,0:T(8,128)S(1)}, f32[1,2,32,1024]{3,2,1,0:T(8,128)}, u32[]{:S(2)}) copy-start(f32[1,2,32,1024]{3,2,1,0:T(8,128)} %param.6) | copy-start | bytes 786436
  2.6 0.9 %copy-start.1 = (f32[1,2,32,1024]{3,2,1,0:T(8,128)S(1)}, f32[1,2,32,1024]{3,2,1,0:T(8,128)}, u32[]{:S(2)}) copy-start(f32[1,2,32,1024]{3,2,1,0:T(8,128)} %param.7) | copy-start | bytes 786436
  3.6 0.9 %copy-start.2 = (f32[1,2,32,1024]{3,2,1,0:T(8,128)S(1)}, f32[1,2,32,1024]{3,2,1,0:T(8,128)}, u32[]{:S(2)}) copy-start(f32[1,2,32,1024]{3,2,1,0:T(8,128)} %param.8) | copy-start | bytes 786436
  4.5 4.5 %copy-start.5 = (s32[16,4]{0,1:T(4,128)S(1)}, s32[16,4]{0,1:T(4,128)}, u32[]{:S(2)}) copy-start(s32[16,4]{0,1:T(4,128)} %param.11) | copy-start | bytes 772
  4.9 19.0 %collective-permute-start = (f32[3,2,2,8,128]{4,3,2,1,0:T(8,128)S(1)}, f32[3,2,2,8,128]{4,3,2,1,0:T(8,128)S(1)}, u32[]{:S(2)}, u32[]{:S(2)}) collective-permute-start(f32[3,2,2,8,128]{4,3,2,1,0:T(8,128)S(1)} %get-tuple-element.17), channel_id=1, source_target_pairs={{0,1},{1,0},{2,4},{3,5},{4,2},{5,3},{6,8},{7,9},{8,6},{9,7},{10,12... | collective-permute-start | bytes 147464 | tf_op jit(solution)/shard_map/ppermute | solution.py:356
  5.0 18.9 %collective-permute-start.1 = (f32[3,2,2,8,128]{4,3,2,1,0:T(8,128)S(1)}, f32[3,2,2,8,128]{4,3,2,1,0:T(8,128)S(1)}, u32[]{:S(2)}, u32[]{:S(2)}) collective-permute-start(f32[3,2,2,8,128]{4,3,2,1,0:T(8,128)S(1)} %get-tuple-element.18), channel_id=1, source_target_pairs={{0,2},{1,3},{2,0},{3,1},{4,6},{5,7},{6,4},{7,5},{8,10},{9,11},{10,... | collective-permute-start | bytes 147464 | tf_op jit(solution)/shard_map/ppermute | solution.py:357
  9.0 0.7 %copy-start.4 = (s32[16,4]{0,1:T(4,128)S(1)}, s32[16,4]{0,1:T(4,128)}, u32[]{:S(2)}) copy-start(s32[16,4]{0,1:T(4,128)} %param.10) | copy-start | bytes 772
  9.0 0.7 %copy-start.3 = (s32[16,4]{0,1:T(4,128)S(1)}, s32[16,4]{0,1:T(4,128)}, u32[]{:S(2)}) copy-start(s32[16,4]{0,1:T(4,128)} %param.9) | copy-start | bytes 772
  23.9 1.3 %collective-permute-start.5 = (f32[3,2,2,8,128]{4,3,2,1,0:T(8,128)S(1)}, f32[3,2,2,8,128]{4,3,2,1,0:T(8,128)S(1)}, u32[]{:S(2)}, u32[]{:S(2)}) collective-permute-start(f32[3,2,2,8,128]{4,3,2,1,0:T(8,128)S(1)} %collective-permute-done.1.refs_3_), channel_id=1, source_target_pairs={{0,1},{1,0},{2,3},{3,2},{4,5},{5,4},{6,7},{7,6},{8,9},{9,8},{10,11... | collective-permute-start | bytes 147464 | tf_op jit(solution)/shard_map/ppermute | solution.py:379
  24.0 1.4 %collective-permute-start.6 = (f32[3,2,2,8,128]{4,3,2,1,0:T(8,128)S(1)}, f32[3,2,2,8,128]{4,3,2,1,0:T(8,128)S(1)}, u32[]{:S(2)}, u32[]{:S(2)}) collective-permute-start(f32[3,2,2,8,128]{4,3,2,1,0:T(8,128)S(1)} %collective-permute-done.refs_4_), channel_id=1, source_target_pairs={{0,1},{1,0},{2,3},{3,2},{4,5},{5,4},{6,7},{7,6},{8,9},{9,8},{10,11... | collective-permute-start | bytes 147464 | tf_op jit(solution)/shard_map/ppermute | solution.py:378

commit v2 on v1

--- a/solution.py
+++ b/solution.py
@@ -17,6 +17,8 @@
 EDGE = 2
 FIELDS = 3
 AXES = ("slab", "bal")
+UNROLL_FIRST = 6
+UNROLL_SECOND = 7
 VMEM_BYTES = 40 * 2**20
 
 
@@ -86,10 +88,10 @@
     )
 
 
-def step_plane(geometry, below, center, above, next_down, previous_up, rate):
+def step_plane(geometry, below, center, above, up, down, next_down, previous_up, rate):
     sums, differences = [], None
     for f in range(FIELDS):
-        y_upper, y_lower = geometry.y_pair(geometry.up(center[f]), geometry.down(center[f]))
+        y_upper, y_lower = geometry.y_pair(up[f], down[f])
         z_upper, z_lower = geometry.z_pair(center[f], next_down[f], previous_up[f])
         sums.append((above[f] + below[f]) + (y_upper + y_lower) + (z_upper + z_lower))
         if f == 0:
@@ -108,6 +110,8 @@
             load_below(p),
             centers[p],
             load_above(p),
+            ups[p],
+            downs[p],
             downs[(p + 1) % ring],
             ups[(p - 1) % ring],
             rates[p],
@@ -118,6 +122,26 @@
 
 def planes_at(ref, p, x):
     return [ref[f, p, x] for f in range(FIELDS)]
+
+
+def rate_of(active):
+    return jnp.where(active != 0, jnp.float32(RATE), jnp.float32(0.0))
+
+
+def start_tables(tables, held, sem):
+    copies = [pltpu.make_async_copy(t, h, sem.at[i]) for i, (t, h) in enumerate(zip(tables, held))]
+    for copy in copies:
+        copy.start()
+    return copies
+
+
+def holders(before, layer, core, blocks, cores):
+    found = [0] * (blocks * cores)
+    for place in range(blocks * cores):
+        owner = core if place < blocks else cores - 1 - core
+        at = before[owner * blocks + place % blocks, layer]
+        found = [jnp.where(at == p, place, found[p]) for p in range(len(found))]
+    return found
 
 
 def pack_kernel(side, *refs):
@@ -143,72 +167,84 @@
                     ref[f, b, d] = tiles[f, end, b, pl.ds(row, ROWS, stride=ROWS)]
 
 
-def inner_kernel(side, blocks, cores, *refs):
-    own, other = refs[:FIELDS], refs[FIELDS : 2 * FIELDS]
-    before, after, flags = refs[2 * FIELDS : 2 * FIELDS + 3]
-    outs = refs[2 * FIELDS + 3 : 3 * FIELDS + 3]
-    rim_raw, rim_step, rim_out = refs[3 * FIELDS + 3 : 3 * FIELDS + 6]
-    tiles, raw, stepped, result, in_sem, out_sem = refs[3 * FIELDS + 6 :]
+def first_kernel(side, blocks, cores, *refs):
+    own, other, tables = refs[:FIELDS], refs[FIELDS : 2 * FIELDS], refs[2 * FIELDS : 2 * FIELDS + 2]
+    raw, stepped = refs[2 * FIELDS + 2 : 2 * FIELDS + 4]
+    tiles, ups, downs, before, flags, sem, own_sem = refs[2 * FIELDS + 4 :]
     ring = blocks * cores
     layer, core = lax.axis_index("slab"), lax.axis_index("bal")
-    copies = []
-    for c, source in enumerate((own, other)):
+    own_copies = [pltpu.make_async_copy(own[f], tiles.at[f], own_sem.at[f]) for f in range(FIELDS)]
+    for copy in own_copies:
+        copy.start()
+    copies = start_tables(tables, (before, flags), sem)
+    geometry = Geometry(side)
+    for c, source in ((1, other), (0, [tiles.at[f] for f in range(FIELDS)])):
         for f in range(FIELDS):
-            copies.append(pltpu.make_async_copy(source[f], tiles.at[c, f], in_sem.at[c, f]))
-            copies[-1].start()
+            if c == 0:
+                own_copies[f].wait()
+            for b in range(blocks):
+                for x in range(side):
+                    plane = source[f][b, plane_rows(x)]
+                    raw[f, c * blocks + b, x] = plane
+                    ups[f, c * blocks + b, x] = geometry.up(plane)
+                    downs[f, c * blocks + b, x] = geometry.down(plane)
+    for copy in copies:
+        copy.wait()
+    places = holders(before, layer, core, blocks, cores)
+    rates = [rate_of(flags[p, layer]) for p in range(ring)]
+
+    @pl.loop(1, side - 1, unroll=UNROLL_FIRST)
+    def _(x):
+        for p in range(ring):
+            here, following, previous = places[p], places[(p + 1) % ring], places[(p - 1) % ring]
+            new = step_plane(
+                geometry,
+                planes_at(raw, here, x - 1),
+                planes_at(raw, here, x),
+                planes_at(raw, here, x + 1),
+                planes_at(ups, here, x),
+                planes_at(downs, here, x),
+                planes_at(downs, following, x),
+                planes_at(ups, previous, x),
+                rates[p],
+            )
+            for f in range(FIELDS):
+                stepped[f, p, x] = new[f]
+
+
+def second_kernel(side, blocks, cores, *refs):
+    stepped, tables, outs, rim_out = refs[0], refs[1:3], refs[3 : 3 + FIELDS], refs[3 + FIELDS]
+    result, after, flags, sem, out_sem = refs[4 + FIELDS :]
+    ring = blocks * cores
+    layer, core = lax.axis_index("slab"), lax.axis_index("bal")
+    copies = start_tables(tables, (after, flags), sem)
     geometry = Geometry(side)
-    rates = [jnp.where(flags[p, layer] != 0, jnp.float32(RATE), jnp.float32(0.0)) for p in range(ring)]
-    for c in range(cores):
-        slot = jnp.where(c == 0, core, cores - 1 - core) * blocks
-        for f in range(FIELDS):
-            copies[c * FIELDS + f].wait()
-            for b in range(blocks):
-                p = before[slot + b, layer]
-
-                @pl.loop(0, side, unroll=8)
-                def _(x, c=c, f=f, b=b, p=p):
-                    raw[f, p, x] = tiles[c, f, b, plane_rows(x)]
-
-    @pl.loop(1, side - 1)
-    def _(x):
-        new = step_ring(
-            geometry,
-            lambda p: planes_at(raw, p, x - 1),
-            lambda p: planes_at(raw, p, x),
-            lambda p: planes_at(raw, p, x + 1),
-            rates,
-        )
-        for p in range(ring):
-            for f in range(FIELDS):
-                stepped[f, p, x] = new[p][f]
-
-    for end in range(2):
-        for d in range(EDGE):
-            for f in range(FIELDS):
-                for p in range(ring):
-                    rim_raw[end, f, p, d] = raw[f, p, d if end == 0 else side - 1 - d]
-                    rim_step[end, f, p, d] = stepped[f, p, 1 + d if end == 0 else side - 2 - d]
-
+    for copy in copies:
+        copy.wait()
     places = [after[core * blocks + b, layer] for b in range(blocks)]
-
-    @pl.loop(2, side - 2)
+    rates = [rate_of(flags[p, layer]) for p in places]
+    rows = ROWS * ROWS
+
+    @pl.loop(2, side - 2, unroll=UNROLL_SECOND)
     def _(x):
         for b in range(blocks):
             p = places[b]
             following, previous = lax.rem(p + 1, ring), lax.rem(p + ring - 1, ring)
+            center = planes_at(stepped, p, x)
             new = step_plane(
                 geometry,
                 planes_at(stepped, p, x - 1),
-                planes_at(stepped, p, x),
+                center,
                 planes_at(stepped, p, x + 1),
+                [geometry.up(c) for c in center],
+                [geometry.down(c) for c in center],
                 [geometry.down(c) for c in planes_at(stepped, following, x)],
                 [geometry.up(c) for c in planes_at(stepped, previous, x)],
-                jnp.where(flags[p, layer] != 0, jnp.float32(RATE), jnp.float32(0.0)),
+                rates[b],
             )
             for f in range(FIELDS):
                 result[f, b, plane_rows(x)] = new[f]
 
-    rows = ROWS * ROWS
     middle = pl.ds(rows, side * ROWS - 2 * rows)
     copies = []
     for f in range(FIELDS):
@@ -223,23 +259,26 @@
 
 
 def rim_kernel(side, blocks, cores, layers, *refs):
-    rim_raw, rim_step, rim_out = refs[:3]
+    raw, inner, rim_out = refs[:3]
     even, odd, even_other, odd_other = refs[3:7]
-    before, after, flags = refs[7:10]
+    tables = refs[7:10]
     outs = refs[10 + FIELDS : 10 + 2 * FIELDS]
-    halo, stepped, tiles, sem = refs[10 + 2 * FIELDS :]
+    halo, stepped, tiles, before, after, flags, table_sem, sem = refs[10 + 2 * FIELDS :]
     ring = blocks * cores
     layer, core = lax.axis_index("slab"), lax.axis_index("bal")
     parity = lax.rem(layer, 2)
+    table_copies = start_tables(tables, (before, after, flags), table_sem)
     geometry = Geometry(side)
     rows = ROWS * ROWS
-
-    def rate_of(which, p):
-        return jnp.where(flags[p, which] != 0, jnp.float32(RATE), jnp.float32(0.0))
-
     for f in range(FIELDS):
         for end in range(2):
             tiles[f, end] = rim_out[f, end]
+    for copy in table_copies:
+        copy.wait()
+    places = holders(before, layer, core, blocks, cores)
+
+    def at_raw(end, p, d):
+        return planes_at(raw, places[p], d if end == 0 else side - 1 - d)
 
     for message, pair in enumerate(((even, even_other), (odd, odd_other))):
         end = (1 - parity) if message == 0 else parity
@@ -259,15 +298,15 @@
 
         @pl.when(outside)
         def _(end=end):
+            x = end * (side - 1)
             for p in range(ring):
                 for f in range(FIELDS):
                     for d in range(EDGE):
-                        halo[end, f, p, d] = rim_raw[end, f, p, 0]
+                        halo[end, f, p, d] = raw[f, places[p], x]
 
     def at(ref, end, p, d):
         return [ref[end, f, p, d] for f in range(FIELDS)]
 
-    places = [after[core * blocks + b, layer] for b in range(blocks)]
     copies = []
     for end in range(2):
         beside = layer + 2 * end - 1
@@ -276,35 +315,39 @@
         face = step_ring(
             geometry,
             lambda p: at(halo, end, p, 0),
-            lambda p: at(rim_raw, end, p, 0),
-            lambda p: at(rim_raw, end, p, 1),
-            [rate_of(layer, p) for p in range(ring)],
+            lambda p: at_raw(end, p, 0),
+            lambda p: at_raw(end, p, 1),
+            [rate_of(flags[p, layer]) for p in range(ring)],
         )
         beyond = step_ring(
             geometry,
             lambda p: at(halo, end, p, 1),
             lambda p: at(halo, end, p, 0),
-            lambda p: at(rim_raw, end, p, 0),
-            [rate_of(table, p) for p in range(ring)],
+            lambda p: at_raw(end, p, 0),
+            [rate_of(flags[p, table]) for p in range(ring)],
         )
         for p in range(ring):
             for f in range(FIELDS):
                 stepped[end, f, p, 0] = jnp.where(outside, face[p][f], beyond[p][f])
                 stepped[end, f, p, 1] = face[p][f]
                 for d in range(EDGE):
-                    stepped[end, f, p, 2 + d] = rim_step[end, f, p, d]
+                    stepped[end, f, p, 2 + d] = inner[f, p, 1 + d if end == 0 else side - 2 - d]
+    for end in range(2):
         for d in range(EDGE):
             for b in range(blocks):
-                p = places[b]
+                p = after[core * blocks + b, layer]
                 following, previous = lax.rem(p + 1, ring), lax.rem(p + ring - 1, ring)
+                center = at(stepped, end, p, d + 1)
                 new = step_plane(
                     geometry,
                     at(stepped, end, p, d),
-                    at(stepped, end, p, d + 1),
+                    center,
                     at(stepped, end, p, d + 2),
+                    [geometry.up(c) for c in center],
+                    [geometry.down(c) for c in center],
                     [geometry.down(c) for c in at(stepped, end, following, d + 1)],
                     [geometry.up(c) for c in at(stepped, end, previous, d + 1)],
-                    rate_of(layer, p),
+                    rate_of(flags[p, layer]),
                 )
                 row = d if end == 0 else ROWS - 1 - d
                 for f in range(FIELDS):
@@ -339,8 +382,11 @@
     owners = [(s * cores + c, s * cores + cores - 1 - c) for s in range(layers) for c in range(cores)]
     fields = [tiles_of(a[0]) for a in (order_parameter, concentration_excess, thermal_subcooling)]
     others = [lax.ppermute(a, AXES, owners) for a in fields]
-    vmem, hbm, smem = (pl.BlockSpec(memory_space=m) for m in (pltpu.VMEM, pl.ANY, pltpu.SMEM))
+    vmem, hbm = (pl.BlockSpec(memory_space=m) for m in (pltpu.VMEM, pltpu.HBM))
+    params = pltpu.CompilerParams(vmem_limit_bytes=VMEM_BYTES)
     message = jax.ShapeDtypeStruct((FIELDS, blocks, EDGE, ROWS, LANES), f32)
+    table = pltpu.SMEM(before.shape, jnp.int32)
+    in_hbm = lambda *arrays: [pltpu.with_memory_space_constraint(a, pltpu.HBM) for a in arrays]
     even, odd = pl.pallas_call(
         functools.partial(pack_kernel, side),
         out_shape=(message, message),
@@ -350,48 +396,56 @@
             pltpu.VMEM((FIELDS, 2, blocks, ROWS * ROWS, LANES), f32),
             pltpu.SemaphoreType.DMA((FIELDS, 2)),
         ],
-        compiler_params=pltpu.CompilerParams(vmem_limit_bytes=VMEM_BYTES),
+        compiler_params=params,
         cost_estimate=pl.CostEstimate(flops=0, bytes_accessed=10**6, transcendentals=0),
-    )(*fields)
+    )(*in_hbm(*fields))
     odd_in = lax.ppermute(odd, AXES, neighbour_swaps(layers, cores, 1))
     even_in = lax.ppermute(even, AXES, neighbour_swaps(layers, cores, 0))
-    rim = jax.ShapeDtypeStruct((2, FIELDS, ring, EDGE, ROWS, LANES), f32)
+    planes = (FIELDS, ring, side, ROWS, LANES)
+    raw, stepped = pl.pallas_call(
+        functools.partial(first_kernel, side, blocks, cores),
+        out_shape=(jax.ShapeDtypeStruct(planes, f32),) * 2,
+        in_specs=[hbm] * FIELDS + [vmem] * FIELDS + [hbm] * 2,
+        out_specs=(vmem, vmem),
+        scratch_shapes=[pltpu.VMEM((FIELDS, blocks, rows, LANES), f32)]
+        + [pltpu.VMEM(planes, f32)] * 2
+        + [table] * 2
+        + [pltpu.SemaphoreType.DMA((2,)), pltpu.SemaphoreType.DMA((FIELDS,))],
+        compiler_params=params,
+        cost_estimate=pl.CostEstimate(flops=0, bytes_accessed=10**7, transcendentals=0),
+    )(*in_hbm(*fields), *others, *in_hbm(before, flags))
+    odd_in, even_in, stepped = lax.optimization_barrier((odd_in, even_in, stepped))
+    odd_other = lax.ppermute(odd_in, AXES, owners)
+    even_other = lax.ppermute(even_in, AXES, owners)
     whole = jax.ShapeDtypeStruct((blocks, rows, LANES), f32)
     rim_tiles = (FIELDS, 2, blocks, ROWS * ROWS, LANES)
-    *parts, rim_raw, rim_step, rim_out = pl.pallas_call(
-        functools.partial(inner_kernel, side, blocks, cores),
-        out_shape=(whole,) * FIELDS + (rim, rim, jax.ShapeDtypeStruct(rim_tiles, f32)),
-        in_specs=[hbm] * (2 * FIELDS) + [smem] * 3,
-        out_specs=(hbm,) * FIELDS + (vmem,) * 3,
-        scratch_shapes=[
-            pltpu.VMEM((cores, FIELDS, blocks, rows, LANES), f32),
-            pltpu.VMEM((FIELDS, ring, side, ROWS, LANES), f32),
-            pltpu.VMEM((FIELDS, ring, side, ROWS, LANES), f32),
-            pltpu.VMEM((FIELDS, blocks, rows, LANES), f32),
-            pltpu.SemaphoreType.DMA((cores, FIELDS)),
-            pltpu.SemaphoreType.DMA((FIELDS,)),
-        ],
-        compiler_params=pltpu.CompilerParams(vmem_limit_bytes=VMEM_BYTES),
+    *parts, rim_out = pl.pallas_call(
+        functools.partial(second_kernel, side, blocks, cores),
+        out_shape=(whole,) * FIELDS + (jax.ShapeDtypeStruct(rim_tiles, f32),),
+        in_specs=[vmem] + [hbm] * 2,
+        out_specs=(hbm,) * FIELDS + (vmem,),
+        scratch_shapes=[pltpu.VMEM((FIELDS, blocks, rows, LANES), f32)]
+        + [table] * 2
+        + [pltpu.SemaphoreType.DMA((2,)), pltpu.SemaphoreType.DMA((FIELDS,))],
+        compiler_params=params,
         cost_estimate=pl.CostEstimate(flops=0, bytes_accessed=10**7, transcendentals=0),
-    )(*fields, *others, before, after, flags)
-    odd_in, even_in, rim_raw = lax.optimization_barrier((odd_in, even_in, rim_raw))
-    odd_other = lax.ppermute(odd_in, AXES, owners)
-    even_other = lax.ppermute(even_in, AXES, owners)
+    )(stepped, *in_hbm(after, flags))
     results = pl.pallas_call(
         functools.partial(rim_kernel, side, blocks, cores, layers),
         out_shape=(whole,) * FIELDS,
-        in_specs=[vmem] * 7 + [smem] * 3 + [hbm] * FIELDS,
+        in_specs=[vmem] * 7 + [hbm] * 3 + [hbm] * FIELDS,
         out_specs=(hbm,) * FIELDS,
         input_output_aliases={10 + f: f for f in range(FIELDS)},
         scratch_shapes=[
             pltpu.VMEM((2, FIELDS, ring, EDGE, ROWS, LANES), f32),
             pltpu.VMEM((2, FIELDS, ring, 2 + EDGE, ROWS, LANES), f32),
             pltpu.VMEM(rim_tiles, f32),
-            pltpu.SemaphoreType.DMA((FIELDS, 2)),
-        ],
-        compiler_params=pltpu.CompilerParams(vmem_limit_bytes=VMEM_BYTES),
+        ]
+        + [table] * 3
+        + [pltpu.SemaphoreType.DMA((3,)), pltpu.SemaphoreType.DMA((FIELDS, 2))],
+        compiler_params=params,
         cost_estimate=pl.CostEstimate(flops=0, bytes_accessed=10**6, transcendentals=0),
-    )(rim_raw, rim_step, rim_out, even_in, odd_in, even_other, odd_other, before, after, flags, *parts)
+    )(raw, stepped, rim_out, even_in, odd_in, even_other, odd_other, *in_hbm(before, after, flags, *parts))
     return tuple(block_of(r, side)[None] for r in results)
 
 

time: 27.7 us -> 18 us (0.65)
  Pallas kernels: 16.6 us -> 11.3 us
  local copies, waits for them, and re-layouts: 3.53 us -> 0 us
  waiting for transfers between devices: 0.89 us -> 0.02 us
    pallas_call x1 -> x2, Pallas kernels: 14.2 us -> 7.66 us  [the longest x1 4.42 us: body(): pl.pallas_call(functools.partial(second_kernel, side, blocks, cores), out...]
    unnamed x12 -> x0, local copies, waits for them, and re-layouts: 3.53 us -> none
    pallas_call x1, Pallas kernels: 0.34 us -> 1.08 us  [body(): pl.pallas_call(functools.partial(pack_kernel, side), out_shape=(message,...]
    ppermute x1, waiting for transfers between devices: 0.72 us -> 0.01 us  [body(): even_other = lax.ppermute(even_in, AXES, owners)]
    pallas_call x1, Pallas kernels: 2.11 us -> 2.53 us  [body(): pl.pallas_call(functools.partial(rim_kernel, side, blocks, cores, layers)...]
  transfers between devices with their start and end apart: 7 -> 7, of which waited for: 2 -> 0; matrix products, arithmetic and copies ran while one was open for 0% -> 0% of each run, Pallas kernels for 53% -> 49%
where the time goes in v2:
time: 18 us; the launch traced here: 17.7 us
  Pallas kernels  11.3 us (63%)
  starting transfers between devices  5.72 us (32%)
  between operations  0.7 us (4%)
    pallas_call x1, Pallas kernels, body(): pl.pallas_call(functools.partial(second_kernel, side, blocks, cores), out...  4.42 us
    ppermute x1, starting transfers between devices, body(): even_in = lax.ppermute(even, AXES, neighbour_swaps(layers, cores, 0))  3.98 us
    pallas_call x1, Pallas kernels, body(): pl.pallas_call(functools.partial(first_kernel, side, blocks, cores), out_...  3.24 us
    pallas_call x1, Pallas kernels, body(): pl.pallas_call(functools.partial(rim_kernel, side, blocks, cores, layers)...  2.53 us
    pallas_call x1, Pallas kernels, body(): pl.pallas_call(functools.partial(pack_kernel, side), out_shape=(message,...  1.08 us
    ppermute x3, starting transfers between devices, body(): others = [lax.ppermute(a, AXES, owners) for a in fields]  1.03 us
    ppermute x1, starting transfers between devices, body(): odd_other = lax.ppermute(odd_in, AXES, owners)  0.5 us
  transfers between devices with their start and end apart: 7, of which 0 were waited for; matrix products, arithmetic and copies ran while one was open for 0% of the time, Pallas kernels for 49%

profile of v2, /device:TPU:0, one launch (start us, length us, event | category | flops | bytes accessed | tf_op | source)
XLA Modules:
  0.0 17.7 jit_solution(1260675850520403939)
XLA Ops:
  0.6 0.5 %collective-permute-start = (f32[2,256,128]{2,1,0:T(8,128)}, f32[2,256,128]{2,1,0:T(8,128)S(1)}, u32[]{:S(2)}, u32[]{:S(2)}) collective-permute-start(f32[2,256,128]{2,1,0:T(8,128)} %bitcast.33), channel_id=1, source_target_pairs={{0,1},{1,0},{2,3},{3,2},{4,5},{5,4},{6,7},{7,6},{8,9},{9,8},{10,11... | collective-permute-start | bytes 786440 | tf_op jit(solution)/shard_map/ppermute | solution.py:384
  1.1 0.1 collective-permute-start.1
  1.2 0.4 %collective-permute-start.2 = (f32[2,256,128]{2,1,0:T(8,128)}, f32[2,256,128]{2,1,0:T(8,128)S(1)}, u32[]{:S(2)}, u32[]{:S(2)}) collective-permute-start(f32[2,256,128]{2,1,0:T(8,128)} %bitcast.39), channel_id=1, source_target_pairs={{0,1},{1,0},{2,3},{3,2},{4,5},{5,4},{6,7},{7,6},{8,9},{9,8},{10,11... | collective-permute-start | bytes 786440 | tf_op jit(solution)/shard_map/ppermute | solution.py:384
  1.7 1.1 %shard_map.86 = (f32[3,2,2,8,128]{4,3,2,1,0:T(8,128)S(1)}, f32[3,2,2,8,128]{4,3,2,1,0:T(8,128)S(1)}) custom-call(f32[2,256,128]{2,1,0:T(8,128)} %bitcast.34, f32[2,256,128]{2,1,0:T(8,128)} %bitcast.37, f32[2,256,128]{2,1,0:T(8,128)} %bitcast.40), custom_call_target="tpu_custom_call" | custom-call | bytes 1000000 | tf_op jit(solution)/shard_map/pallas_call | solution.py:390
  2.7 0.1 collective-permute-start.3
  2.9 4.0 %collective-permute-start.4 = (f32[3,2,2,8,128]{4,3,2,1,0:T(8,128)S(1)}, f32[3,2,2,8,128]{4,3,2,1,0:T(8,128)S(1)}, u32[]{:S(2)}, u32[]{:S(2)}) collective-permute-start(f32[3,2,2,8,128]{4,3,2,1,0:T(8,128)S(1)} %get-tuple-element.19), channel_id=1, source_target_pairs={{0,2},{1,3},{2,0},{3,1},{4,6},{5,7},{6,4},{7,5},{8,10},{9,11},{10,... | collective-permute-start | bytes 147464 | tf_op jit(solution)/shard_map/ppermute | solution.py:403
  6.9 0.0 collective-permute-done.refs_3_
  6.9 0.0 collective-permute-done.1.refs_4_
  6.9 0.0 collective-permute-done.2.refs_5_
  6.9 3.2 %shard_map.85 = (f32[3,4,32,8,128]{4,3,2,1,0:T(8,128)S(1)}, f32[3,4,32,8,128]{4,3,2,1,0:T(8,128)S(1)}) custom-call(f32[2,256,128]{2,1,0:T(8,128)} %bitcast.35, f32[2,256,128]{2,1,0:T(8,128)} %bitcast.38, f32[2,256,128]{2,1,0:T(8,128)} %bitcast.41, f32[2,256,128]{2,1,0:T(8,128)S(1)} %collective-permute-done.refs_3_, ...), custom_call_target="tpu_custom_call" | custom-call | bytes 10000000 | tf_op jit(solution)/shard_map/pallas_call | solution.py:405
  10.1 0.0 collective-permute-done.3.refs_4_
  10.1 0.0 collective-permute-done.4.refs_3_
  10.1 0.1 collective-permute-start.5
  10.2 0.5 %collective-permute-start.6 = (f32[3,2,2,8,128]{4,3,2,1,0:T(8,128)S(1)}, f32[3,2,2,8,128]{4,3,2,1,0:T(8,128)S(1)}, u32[]{:S(2)}, u32[]{:S(2)}) collective-permute-start(f32[3,2,2,8,128]{4,3,2,1,0:T(8,128)S(1)} %collective-permute-done.3.refs_4_), channel_id=1, source_target_pairs={{0,1},{1,0},{2,3},{3,2},{4,5},{5,4},{6,7},{7,6},{8,9},{9,8},{10,11... | collective-permute-start | bytes 147464 | tf_op jit(solution)/shard_map/ppermute | solution.py:418
  10.7 4.4 %shard_map.87 = (f32[2,256,128]{2,1,0:T(8,128)}, f32[2,256,128]{2,1,0:T(8,128)}, f32[2,256,128]{2,1,0:T(8,128)}, f32[3,2,2,64,128]{4,3,2,1,0:T(8,128)S(1)}) custom-call(f32[3,4,32,8,128]{4,3,2,1,0:T(8,128)S(1)} %get-tuple-element.21.refs_0_.refs_1_, s32[4,16]{1,0:T(4,128)} %bitcast.50, s32[4,16]{1,0:T(4,128)} %bitcast.46), custom_call_target="tpu_custom_call" | custom-call | bytes 10000000 | tf_op jit(solution)/shard_map/pallas_call | solution.py:422
  15.1 0.0 collective-permute-done.5.refs_5_
  15.2 0.0 collective-permute-done.6.refs_6_
  15.2 2.5 %shard_map.88 = (f32[2,256,128]{2,1,0:T(8,128)}, f32[2,256,128]{2,1,0:T(8,128)}, f32[2,256,128]{2,1,0:T(8,128)}) custom-call(f32[3,4,32,8,128]{4,3,2,1,0:T(8,128)S(1)} %get-tuple-element.17.refs_0_, f32[3,4,32,8,128]{4,3,2,1,0:T(8,128)S(1)} %get-tuple-element.21.refs_0_.refs_1_, ...), custom_call_target="tpu_custom_call", output_to_operand_aliasing={{0}: (10, {}), {1}: (11, {}), {2}: (12, {})} | custom-call | bytes 1000000 | tf_op jit(solution)/shard_map/pallas_call | solution.py:433
Async XLA Ops:
  0.6 6.2 %collective-permute-start = (f32[2,256,128]{2,1,0:T(8,128)}, f32[2,256,128]{2,1,0:T(8,128)S(1)}, u32[]{:S(2)}, u32[]{:S(2)}) collective-permute-start(f32[2,256,128]{2,1,0:T(8,128)} %bitcast.33), channel_id=1, source_target_pairs={{0,1},{1,0},{2,3},{3,2},{4,5},{5,4},{6,7},{7,6},{8,9},{9,8},{10,11... | collective-permute-start | bytes 786440 | tf_op jit(solution)/shard_map/ppermute | solution.py:384
  1.1 5.7 %collective-permute-start.1 = (f32[2,256,128]{2,1,0:T(8,128)}, f32[2,256,128]{2,1,0:T(8,128)S(1)}, u32[]{:S(2)}, u32[]{:S(2)}) collective-permute-start(f32[2,256,128]{2,1,0:T(8,128)} %bitcast.36), channel_id=1, source_target_pairs={{0,1},{1,0},{2,3},{3,2},{4,5},{5,4},{6,7},{7,6},{8,9},{9,8},{10,11... | collective-permute-start | bytes 786440 | tf_op jit(solution)/shard_map/ppermute | solution.py:384
  1.2 5.6 %collective-permute-start.2 = (f32[2,256,128]{2,1,0:T(8,128)}, f32[2,256,128]{2,1,0:T(8,128)S(1)}, u32[]{:S(2)}, u32[]{:S(2)}) collective-permute-start(f32[2,256,128]{2,1,0:T(8,128)} %bitcast.39), channel_id=1, source_target_pairs={{0,1},{1,0},{2,3},{3,2},{4,5},{5,4},{6,7},{7,6},{8,9},{9,8},{10,11... | collective-permute-start | bytes 786440 | tf_op jit(solution)/shard_map/ppermute | solution.py:384
  2.7 7.4 %collective-permute-start.3 = (f32[3,2,2,8,128]{4,3,2,1,0:T(8,128)S(1)}, f32[3,2,2,8,128]{4,3,2,1,0:T(8,128)S(1)}, u32[]{:S(2)}, u32[]{:S(2)}) collective-permute-start(f32[3,2,2,8,128]{4,3,2,1,0:T(8,128)S(1)} %get-tuple-element.18), channel_id=1, source_target_pairs={{0,1},{1,0},{2,4},{3,5},{4,2},{5,3},{6,8},{7,9},{8,6},{9,7},{10,12... | collective-permute-start | bytes 147464 | tf_op jit(solution)/shard_map/ppermute | solution.py:402
  2.9 7.2 %collective-permute-start.4 = (f32[3,2,2,8,128]{4,3,2,1,0:T(8,128)S(1)}, f32[3,2,2,8,128]{4,3,2,1,0:T(8,128)S(1)}, u32[]{:S(2)}, u32[]{:S(2)}) collective-permute-start(f32[3,2,2,8,128]{4,3,2,1,0:T(8,128)S(1)} %get-tuple-element.19), channel_id=1, source_target_pairs={{0,2},{1,3},{2,0},{3,1},{4,6},{5,7},{6,4},{7,5},{8,10},{9,11},{10,... | collective-permute-start | bytes 147464 | tf_op jit(solution)/shard_map/ppermute | solution.py:403
  10.1 5.0 %collective-permute-start.5 = (f32[3,2,2,8,128]{4,3,2,1,0:T(8,128)S(1)}, f32[3,2,2,8,128]{4,3,2,1,0:T(8,128)S(1)}, u32[]{:S(2)}, u32[]{:S(2)}) collective-permute-start(f32[3,2,2,8,128]{4,3,2,1,0:T(8,128)S(1)} %collective-permute-done.4.refs_3_), channel_id=1, source_target_pairs={{0,1},{1,0},{2,3},{3,2},{4,5},{5,4},{6,7},{7,6},{8,9},{9,8},{10,11... | collective-permute-start | bytes 147464 | tf_op jit(solution)/shard_map/ppermute | solution.py:419
  10.2 4.9 %collective-permute-start.6 = (f32[3,2,2,8,128]{4,3,2,1,0:T(8,128)S(1)}, f32[3,2,2,8,128]{4,3,2,1,0:T(8,128)S(1)}, u32[]{:S(2)}, u32[]{:S(2)}) collective-permute-start(f32[3,2,2,8,128]{4,3,2,1,0:T(8,128)S(1)} %collective-permute-done.3.refs_4_), channel_id=1, source_target_pairs={{0,1},{1,0},{2,3},{3,2},{4,5},{5,4},{6,7},{7,6},{8,9},{9,8},{10,11... | collective-permute-start | bytes 147464 | tf_op jit(solution)/shard_map/ppermute | solution.py:418

commit v3 on v2

v3 whole, which is shorter than its diff:
```python
import functools

import jax
import jax.numpy as jnp
from jax import lax
from jax.experimental import pallas as pl
from jax.experimental.pallas import tpu as pltpu
from jax.sharding import PartitionSpec as P

RATE = 0.1
ANISO = 0.05
COUPLE = 0.5
DIFF_SOLUTE = 0.08
DIFF_HEAT = 0.15
TINY = 0.0001
ROWS, LANES = 8, 128
EDGE = 2
FIELDS = 3
AXES = ("slab", "bal")
SPREAD = 32
CHUNK_FIRST = 15
CHUNK_SECOND = 28
VMEM_BYTES = 40 * 2**20


def tiles_of(block):
    blocks, side, cells = block.shape
    split = block.reshape(blocks, side // ROWS, ROWS, cells // LANES, LANES)
    return split.transpose(0, 1, 3, 2, 4).reshape(blocks, side * cells // LANES, LANES)


def block_of(tiles, side):
    blocks, rows, _ = tiles.shape
    columns = rows // side
    split = tiles.reshape(blocks, side // ROWS, columns, ROWS, LANES)
    return split.transpose(0, 1, 3, 2, 4).reshape(blocks, side, columns * LANES)


def plane_rows(x):
    return pl.ds((x >> 3) * ROWS * ROWS + (x & (ROWS - 1)), ROWS, stride=ROWS)


def lane_ids():
    return lax.broadcasted_iota(jnp.int32, (ROWS, LANES), 1)


class Geometry:
    def __init__(self, side):
        lanes = lane_ids()
        self.side = side
        self.y_last = lanes >= LANES - side
        self.y_first = lanes < side
        self.z_first = lanes % side == 0
        self.z_last = lanes % side == side - 1

    def up(self, plane):
        return pltpu.roll(plane, LANES - self.side, 1)

    def down(self, plane):
        return pltpu.roll(plane, self.side, 1)

    def y_pair(self, up, down):
        upper = jnp.where(self.y_last, pltpu.roll(up, ROWS - 1, 0), up)
        lower = jnp.where(self.y_first, pltpu.roll(down, 1, 0), down)
        return upper, lower

    def z_pair(self, plane, next_down, previous_up):
        upper = pltpu.roll(jnp.where(self.z_first, next_down, plane), LANES - 1, 1)
        lower = pltpu.roll(jnp.where(self.z_last, previous_up, plane), 1, 1)
        return upper, lower


def advance(centers, sums, differences, rate):
    phase, solute, heat = centers
    sum_phase, sum_solute, sum_heat = sums
    squares = [d * d for d in differences]
    square = squares[0] + squares[1] + squares[2]
    quartic = squares[0] * squares[0] + squares[1] * squares[1] + squares[2] * squares[2]
    below = square * square + 16.0 * TINY
    anisotropy = (1.0 - 3.0 * ANISO) + 4.0 * ANISO * (quartic / below)
    well = 1.0 - phase * phase
    forcing = well * (phase - COUPLE * well * (solute + heat))
    change = rate * (anisotropy * anisotropy * (sum_phase - 6.0 * phase) + forcing)
    half = 0.5 * change
    return (
        phase + change,
        (1.0 - 6.0 * DIFF_SOLUTE) * solute + (DIFF_SOLUTE * sum_solute + half),
        (1.0 - 6.0 * DIFF_HEAT) * heat + (DIFF_HEAT * sum_heat + half),
    )


def sides(geometry, center, up, down, next_down, previous_up, phase):
    y_upper, y_lower = geometry.y_pair(up, down)
    z_upper, z_lower = geometry.z_pair(center, next_down, previous_up)
    total = (y_upper + y_lower) + (z_upper + z_lower)
    return (total, y_upper - y_lower, z_upper - z_lower) if phase else (total,)


def keep_sides(geometry, around, b, x, center, up, down, next_down, previous_up):
    for f in range(FIELDS):
        found = sides(geometry, center(f), up(f), down(f), next_down(f), previous_up(f), f == 0)
        for k, value in enumerate(found):
            around[f if k == 0 else FIELDS - 1 + k, b, x] = value


def finish(below, center, above, around, rate):
    sums = [(above[f] + below[f]) + around[f] for f in range(FIELDS)]
    return advance(center, sums, (above[0] - below[0], around[FIELDS], around[FIELDS + 1]), rate)


def step_plane(geometry, below, center, above, up, down, next_down, previous_up, rate):
    around = [
        sides(geometry, center[f], up[f], down[f], next_down[f], previous_up[f], f == 0) for f in range(FIELDS)
    ]
    return finish(below, center, above, [a[0] for a in around] + list(around[0][1:]), rate)


def step_ring(geometry, load_below, load_center, load_above, rates):
    ring = len(rates)
    centers = [load_center(p) for p in range(ring)]
    ups = [[geometry.up(c) for c in center] for center in centers]
    downs = [[geometry.down(c) for c in center] for center in centers]
    return [
        step_plane(
            geometry,
            load_below(p),
            centers[p],
            load_above(p),
            ups[p],
            downs[p],
            downs[(p + 1) % ring],
            ups[(p - 1) % ring],
            rates[p],
        )
        for p in range(ring)
    ]


def planes_at(ref, p, x):
    return [ref[f, p, x] for f in range(FIELDS)]


def rate_of(active):
    return jnp.where(active != 0, jnp.float32(RATE), jnp.float32(0.0))


def start_tables(tables, held, sem):
    copies = [pltpu.make_async_copy(t, h, sem.at[i]) for i, (t, h) in enumerate(zip(tables, held))]
    for copy in copies:
        copy.start()
    return copies


def holders(before, layer, core, blocks, cores):
    found = [0] * (blocks * cores)
    for place in range(blocks * cores):
        owner = core if place < blocks else cores - 1 - core
        at = before[owner * blocks + place % blocks, layer]
        found = [jnp.where(at == p, place, found[p]) for p in range(len(found))]
    return found


def pack_kernel(side, *refs):
    fields, (even_ref, odd_ref), (tiles, sem) = refs[:FIELDS], refs[FIELDS : FIELDS + 2], refs[FIELDS + 2 :]
    blocks = even_ref.shape[1]
    rows = ROWS * ROWS
    last = side * ROWS - rows
    copies = [
        pltpu.make_async_copy(fields[f].at[:, pl.ds(start, rows)], tiles.at[f, end], sem.at[f, end])
        for f in range(FIELDS)
        for end, start in enumerate((0, last))
    ]
    for copy in copies:
        copy.start()
    parity = lax.rem(lax.axis_index("slab"), 2)
    for copy in copies:
        copy.wait()
    for f in range(FIELDS):
        for b in range(blocks):
            for d in range(EDGE):
                for ref, end in ((even_ref, 1 - parity), (odd_ref, parity)):
                    row = jnp.where(end == 0, d, ROWS - 1 - d)
                    ref[f, b, d] = tiles[f, end, b, pl.ds(row, ROWS, stride=ROWS)]


def first_kernel(side, blocks, cores, layers, *refs):
    own, other, tables = refs[:FIELDS], refs[FIELDS : 2 * FIELDS], refs[2 * FIELDS : 2 * FIELDS + 3]
    raw, stepped, places_out, rates_out = refs[2 * FIELDS + 3 : 2 * FIELDS + 7]
    tiles, ups, downs, around, before, after, flags, sem, own_sem = refs[2 * FIELDS + 7 :]
    ring = blocks * cores
    layer, core = lax.axis_index("slab"), lax.axis_index("bal")
    own_copies = [pltpu.make_async_copy(own[f], tiles.at[f], own_sem.at[f]) for f in range(FIELDS)]
    for copy in own_copies:
        copy.start()
    copies = start_tables(tables, (before, after, flags), sem)
    geometry = Geometry(side)
    def spread(c, f, source):
        @pl.loop(0, side // SPREAD)
        def _(r):
            for s in range(SPREAD):
                x = r * SPREAD + s
                for b in range(blocks):
                    plane = source[b, plane_rows(x)]
                    raw[f, c * blocks + b, x] = plane
                    ups[f, c * blocks + b, x] = geometry.up(plane)
                    downs[f, c * blocks + b, x] = geometry.down(plane)

    for f in range(FIELDS):
        spread(1, f, other[f])
    for f in range(FIELDS):
        own_copies[f].wait()
        spread(0, f, tiles.at[f])
    for copy in copies:
        copy.wait()
    places = holders(before, layer, core, blocks, cores)
    rates = [rate_of(flags[p, layer]) for p in range(ring)]

    @pl.loop(0, (side - 2) // CHUNK_FIRST)
    def _(i):
        for x in [1 + i * CHUNK_FIRST + u for u in range(CHUNK_FIRST)]:
            for p in range(ring):
                here, following, previous = places[p], places[(p + 1) % ring], places[(p - 1) % ring]
                keep_sides(
                    geometry,
                    around,
                    p,
                    x,
                    lambda f: raw[f, here, x],
                    lambda f: ups[f, here, x],
                    lambda f: downs[f, here, x],
                    lambda f: downs[f, following, x],
                    lambda f: ups[f, previous, x],
                )
        for x in [1 + i * CHUNK_FIRST + u for u in range(CHUNK_FIRST)]:
            for p in range(ring):
                low, center, high = (planes_at(raw, places[p], x + d) for d in (-1, 0, 1))
                new = finish(low, center, high, [around[k, p, x] for k in range(FIELDS + 2)], rates[p])
                for f in range(FIELDS):
                    stepped[f, p, x] = new[f]

    beside = [jnp.clip(layer + 2 * end - 1, 0, layers - 1) for end in range(2)]
    listed = places + [after[core * blocks + b, layer] for b in range(blocks)]
    for table in beside:
        for c in range(cores):
            slot = jnp.where(c == 0, core, cores - 1 - core) * blocks
            listed += [before[slot + b, table] for b in range(blocks)]
    for k, place in enumerate(listed):
        places_out[k] = jnp.full((ROWS, LANES), place, jnp.int32)
    rates += [rate_of(flags[p, table]) for table in beside for p in range(ring)]
    for k, rate in enumerate(rates):
        rates_out[k] = jnp.full((ROWS, LANES), rate, jnp.float32)


def place_at(ref, k):
    return ref[k][0, 0]


def second_kernel(side, blocks, cores, *refs):
    stepped, places_ref, rates_ref, result, shifted, around = refs
    ring = blocks * cores
    geometry = Geometry(side)
    places = [place_at(places_ref, ring + b) for b in range(blocks)]
    rates = [rates_ref[p] for p in places]

    @pl.loop(0, (side - 4) // CHUNK_SECOND)
    def _(i):
        planes = [2 + i * CHUNK_SECOND + u for u in range(CHUNK_SECOND)]
        for x in planes:
            for b, p in enumerate(places):
                following, previous = (p + 1) & (ring - 1), (p + ring - 1) & (ring - 1)
                for f in range(FIELDS):
                    shifted[0, f, b, x] = geometry.up(stepped[f, p, x])
                    shifted[1, f, b, x] = geometry.down(stepped[f, p, x])
                    shifted[2, f, b, x] = geometry.down(stepped[f, following, x])
                    shifted[3, f, b, x] = geometry.up(stepped[f, previous, x])
        for x in planes:
            for b, p in enumerate(places):
                keep_sides(
                    geometry,
                    around,
                    b,
                    x,
                    lambda f: stepped[f, p, x],
                    lambda f: shifted[0, f, b, x],
                    lambda f: shifted[1, f, b, x],
                    lambda f: shifted[2, f, b, x],
                    lambda f: shifted[3, f, b, x],
                )
        for x in planes:
            for b, p in enumerate(places):
                low, center, high = (planes_at(stepped, p, x + d) for d in (-1, 0, 1))
                new = finish(low, center, high, [around[k, b, x] for k in range(FIELDS + 2)], rates[b])
                for f in range(FIELDS):
                    result[f, b, plane_rows(x)] = new[f]


def rim_kernel(side, blocks, cores, layers, *refs):
    raw, inner, result, places_ref, rates_ref = refs[:5]
    messages = refs[5:9]
    outs = refs[9 : 9 + FIELDS]
    halo, stepped, tiles, sem, middle_sem = refs[9 + FIELDS :]
    ring = blocks * cores
    layer = lax.axis_index("slab")
    parity = lax.rem(layer, 2)
    geometry = Geometry(side)
    rows = ROWS * ROWS
    middle = pl.ds(rows, side * ROWS - 2 * rows)
    copies = [
        pltpu.make_async_copy(result.at[f, :, middle], outs[f].at[:, middle], middle_sem.at[f])
        for f in range(FIELDS)
    ]
    for copy in copies:
        copy.start()
    places = [place_at(places_ref, p) for p in range(ring)]
    targets = [place_at(places_ref, ring + b) for b in range(blocks)]
    for end in range(2):
        from_even = parity == 1 - end
        for c in range(cores):
            for b in range(blocks):
                p = place_at(places_ref, ring + blocks + (end * cores + c) * blocks + b)
                for f in range(FIELDS):
                    for d in range(EDGE):
                        halo[end, f, p, d] = jnp.where(
                            from_even, messages[2 * c][f, b, d], messages[2 * c + 1][f, b, d]
                        )

    def at(ref, end, p, d):
        return [ref[end, f, p, d] for f in range(FIELDS)]

    for end in range(2):
        beside = layer + 2 * end - 1
        outside = jnp.logical_or(beside < 0, beside >= layers)
        raw_face = [planes_at(raw, places[p], end * (side - 1)) for p in range(ring)]
        raw_next = [planes_at(raw, places[p], 1 + end * (side - 3)) for p in range(ring)]
        near = [
            [jnp.where(outside, r, h) for r, h in zip(raw_face[p], at(halo, end, p, 0))]
            for p in range(ring)
        ]
        face = step_ring(
            geometry,
            lambda p: near[p],
            lambda p: raw_face[p],
            lambda p: raw_next[p],
            [rates_ref[p] for p in range(ring)],
        )
        beyond = step_ring(
            geometry,
            lambda p: at(halo, end, p, 1),
            lambda p: near[p],
            lambda p: raw_face[p],
            [rates_ref[ring * (1 + end) + p] for p in range(ring)],
        )
        for p in range(ring):
            for f in range(FIELDS):
                stepped[end, f, p, 0] = jnp.where(outside, face[p][f], beyond[p][f])
                stepped[end, f, p, 1] = face[p][f]
                for d in range(EDGE):
                    stepped[end, f, p, 2 + d] = inner[f, p, 1 + d if end == 0 else side - 2 - d]
    for f in range(FIELDS):
        for end in range(2):
            tiles[f, end] = result[f, :, pl.ds(end * (side * ROWS - rows), rows)]
    for end in range(2):
        for d in range(EDGE):
            for b in range(blocks):
                p = targets[b]
                following, previous = lax.rem(p + 1, ring), lax.rem(p + ring - 1, ring)
                center = at(stepped, end, p, d + 1)
                new = step_plane(
                    geometry,
                    at(stepped, end, p, d),
                    center,
                    at(stepped, end, p, d + 2),
                    [geometry.up(c) for c in center],
                    [geometry.down(c) for c in center],
                    [geometry.down(c) for c in at(stepped, end, following, d + 1)],
                    [geometry.up(c) for c in at(stepped, end, previous, d + 1)],
                    rates_ref[p],
                )
                row = d if end == 0 else ROWS - 1 - d
                for f in range(FIELDS):
                    tiles[f, end, b, pl.ds(row, ROWS, stride=ROWS)] = new[f]
    for end in range(2):
        for f in range(FIELDS):
            part = pl.ds(end * (side * ROWS - rows), rows)
            copies.append(pltpu.make_async_copy(tiles.at[f, end], outs[f].at[:, part], sem.at[f, end]))
            copies[-1].start()
    for copy in copies:
        copy.wait()


def neighbour_swaps(layers, cores, first):
    pairs = []
    for layer in range(layers):
        partner = layer + 1 if (layer - first) % 2 == 0 else layer - 1
        for core in range(cores):
            here = layer * cores + core
            if 0 <= partner < layers:
                pairs.append((here, partner * cores + core))
            else:
                pairs.append((here, layer * cores + cores - 1 - core))
    return pairs


def body(layers, cores, order_parameter, concentration_excess, thermal_subcooling, before, after, flags):
    blocks, side = order_parameter.shape[1], order_parameter.shape[2]
    ring = blocks * cores
    rows = side * ROWS
    f32 = jnp.float32
    before, after, flags = before.T, after.T, flags.T
    owners = [(s * cores + c, s * cores + cores - 1 - c) for s in range(layers) for c in range(cores)]
    fields = [tiles_of(a[0]) for a in (order_parameter, concentration_excess, thermal_subcooling)]
    others = [lax.ppermute(a, AXES, owners) for a in fields]
    vmem, hbm = (pl.BlockSpec(memory_space=m) for m in (pltpu.VMEM, pltpu.HBM))
    params = pltpu.CompilerParams(vmem_limit_bytes=VMEM_BYTES)
    message = jax.ShapeDtypeStruct((FIELDS, blocks, EDGE, ROWS, LANES), f32)
    table = pltpu.SMEM(before.shape, jnp.int32)
    in_hbm = lambda *arrays: [pltpu.with_memory_space_constraint(a, pltpu.HBM) for a in arrays]
    even, odd = pl.pallas_call(
        functools.partial(pack_kernel, side),
        out_shape=(message, message),
        in_specs=[hbm] * FIELDS,
        out_specs=(vmem, vmem),
        scratch_shapes=[
            pltpu.VMEM((FIELDS, 2, blocks, ROWS * ROWS, LANES), f32),
            pltpu.SemaphoreType.DMA((FIELDS, 2)),
        ],
        compiler_params=params,
        cost_estimate=pl.CostEstimate(flops=0, bytes_accessed=10**6, transcendentals=0),
    )(*in_hbm(*fields))
    odd_in = lax.ppermute(odd, AXES, neighbour_swaps(layers, cores, 1))
    even_in = lax.ppermute(even, AXES, neighbour_swaps(layers, cores, 0))
    planes = (FIELDS, ring, side, ROWS, LANES)
    raw, stepped, places, rates = pl.pallas_call(
        functools.partial(first_kernel, side, blocks, cores, layers),
        out_shape=(
            jax.ShapeDtypeStruct(planes, f32),
            jax.ShapeDtypeStruct(planes, f32),
            jax.ShapeDtypeStruct((3 * ring + blocks, ROWS, LANES), jnp.int32),
            jax.ShapeDtypeStruct((3 * ring, ROWS, LANES), f32),
        ),
        in_specs=[hbm] * FIELDS + [vmem] * FIELDS + [hbm] * 3,
        out_specs=(vmem,) * 4,
        scratch_shapes=[pltpu.VMEM((FIELDS, blocks, rows, LANES), f32)]
        + [pltpu.VMEM(planes, f32)] * 2
        + [pltpu.VMEM((FIELDS + 2, ring, side, ROWS, LANES), f32)]
        + [table] * 3
        + [pltpu.SemaphoreType.DMA((3,)), pltpu.SemaphoreType.DMA((FIELDS,))],
        compiler_params=params,
        cost_estimate=pl.CostEstimate(flops=0, bytes_accessed=10**7, transcendentals=0),
    )(*in_hbm(*fields), *others, *in_hbm(before, after, flags))
    odd_in, even_in, stepped = lax.optimization_barrier((odd_in, even_in, stepped))
    odd_other = lax.ppermute(odd_in, AXES, owners)
    even_other = lax.ppermute(even_in, AXES, owners)
    result = pl.pallas_call(
        functools.partial(second_kernel, side, blocks, cores),
        out_shape=jax.ShapeDtypeStruct((FIELDS, blocks, rows, LANES), f32),
        in_specs=[vmem] * 3,
        out_specs=vmem,
        scratch_shapes=[
            pltpu.VMEM((4, FIELDS, blocks, side, ROWS, LANES), f32),
            pltpu.VMEM((FIELDS + 2, blocks, side, ROWS, LANES), f32),
        ],
        compiler_params=params,
        cost_estimate=pl.CostEstimate(flops=0, bytes_accessed=10**7, transcendentals=0),
    )(stepped, places, rates)
    results = pl.pallas_call(
        functools.partial(rim_kernel, side, blocks, cores, layers),
        out_shape=(jax.ShapeDtypeStruct((blocks, rows, LANES), f32),) * FIELDS,
        in_specs=[vmem] * 9,
        out_specs=(hbm,) * FIELDS,
        scratch_shapes=[
            pltpu.VMEM((2, FIELDS, ring, EDGE, ROWS, LANES), f32),
            pltpu.VMEM((2, FIELDS, ring, 2 + EDGE, ROWS, LANES), f32),
            pltpu.VMEM((FIELDS, 2, blocks, ROWS * ROWS, LANES), f32),
            pltpu.SemaphoreType.DMA((FIELDS, 2)),
            pltpu.SemaphoreType.DMA((FIELDS,)),
        ],
        compiler_params=params,
        cost_estimate=pl.CostEstimate(flops=0, bytes_accessed=10**6, transcendentals=0),
    )(raw, stepped, result, places, rates, even_in, odd_in, even_other, odd_other)
    return tuple(block_of(r, side)[None] for r in results)


def solution(mesh):
    layers, cores = mesh.shape["slab"], mesh.shape["bal"]
    split, copied = P("slab", "bal", None, None), P()
    return jax.shard_map(
        functools.partial(body, layers, cores),
        mesh=mesh,
        in_specs=(split,) * 3 + (copied,) * 3,
        out_specs=(split,) * 3,
        check_vma=False,
    )
```

time: 18 us -> 13.9 us (0.77)
  Pallas kernels: 11.3 us -> 7.32 us
    pallas_call x1, Pallas kernels: 4.42 us -> 1.35 us  [body(): pl.pallas_call(functools.partial(second_kernel, side, blocks, cores), out...]
    pallas_call x1, Pallas kernels: 2.53 us -> 1.62 us  [body(): pl.pallas_call(functools.partial(rim_kernel, side, blocks, cores, layers)...]
  transfers between devices with their start and end apart: 7 -> 7, of which waited for: 0 -> 0; matrix products, arithmetic and copies ran while one was open for 0% -> 0% of each run, Pallas kernels for 49% -> 41%
where the time goes in v3:
time: 13.9 us; the launch traced here: 13.8 us
  Pallas kernels  7.32 us (53%)
  starting transfers between devices  5.72 us (41%)
  between operations  0.7 us (5%)
    ppermute x1, starting transfers between devices, body(): even_in = lax.ppermute(even, AXES, neighbour_swaps(layers, cores, 0))  3.98 us
    pallas_call x1, Pallas kernels, body(): pl.pallas_call(functools.partial(first_kernel, side, blocks, cores, layer...  3.28 us
    pallas_call x1, Pallas kernels, body(): pl.pallas_call(functools.partial(rim_kernel, side, blocks, cores, layers)...  1.62 us
    pallas_call x1, Pallas kernels, body(): pl.pallas_call(functools.partial(second_kernel, side, blocks, cores), out...  1.35 us
    pallas_call x1, Pallas kernels, body(): pl.pallas_call(functools.partial(pack_kernel, side), out_shape=(message,...  1.08 us
    ppermute x3, starting transfers between devices, body(): others = [lax.ppermute(a, AXES, owners) for a in fields]  1.03 us
    ppermute x1, starting transfers between devices, body(): odd_other = lax.ppermute(odd_in, AXES, owners)  0.5 us
  transfers between devices with their start and end apart: 7, of which 0 were waited for; matrix products, arithmetic and copies ran while one was open for 0% of the time, Pallas kernels for 41%

profile of v3, /device:TPU:0, one launch (start us, length us, event | category | flops | bytes accessed | tf_op | source)
XLA Modules:
  0.0 13.8 jit_solution(17468856733405346125)
XLA Ops:
  0.6 0.5 %collective-permute-start = (f32[2,256,128]{2,1,0:T(8,128)}, f32[2,256,128]{2,1,0:T(8,128)S(1)}, u32[]{:S(2)}, u32[]{:S(2)}) collective-permute-start(f32[2,256,128]{2,1,0:T(8,128)} %bitcast.33), channel_id=1, source_target_pairs={{0,1},{1,0},{2,3},{3,2},{4,5},{5,4},{6,7},{7,6},{8,9},{9,8},{10,11... | collective-permute-start | bytes 786440 | tf_op jit(solution)/shard_map/ppermute | solution.py:412
  1.1 0.1 collective-permute-start.1
  1.2 0.4 %collective-permute-start.2 = (f32[2,256,128]{2,1,0:T(8,128)}, f32[2,256,128]{2,1,0:T(8,128)S(1)}, u32[]{:S(2)}, u32[]{:S(2)}) collective-permute-start(f32[2,256,128]{2,1,0:T(8,128)} %bitcast.39), channel_id=1, source_target_pairs={{0,1},{1,0},{2,3},{3,2},{4,5},{5,4},{6,7},{7,6},{8,9},{9,8},{10,11... | collective-permute-start | bytes 786440 | tf_op jit(solution)/shard_map/ppermute | solution.py:412
  1.7 1.1 %shard_map.86 = (f32[3,2,2,8,128]{4,3,2,1,0:T(8,128)S(1)}, f32[3,2,2,8,128]{4,3,2,1,0:T(8,128)S(1)}) custom-call(f32[2,256,128]{2,1,0:T(8,128)} %bitcast.34, f32[2,256,128]{2,1,0:T(8,128)} %bitcast.37, f32[2,256,128]{2,1,0:T(8,128)} %bitcast.40), custom_call_target="tpu_custom_call" | custom-call | bytes 1000000 | tf_op jit(solution)/shard_map/pallas_call | solution.py:418
  2.7 0.1 %collective-permute-start.3 = (f32[3,2,2,8,128]{4,3,2,1,0:T(8,128)S(1)}, f32[3,2,2,8,128]{4,3,2,1,0:T(8,128)S(1)}, u32[]{:S(2)}, u32[]{:S(2)}) collective-permute-start(f32[3,2,2,8,128]{4,3,2,1,0:T(8,128)S(1)} %get-tuple-element.16), channel_id=1, source_target_pairs={{0,1},{1,0},{2,4},{3,5},{4,2},{5,3},{6,8},{7,9},{8,6},{9,7},{10,12... | collective-permute-start | bytes 147464 | tf_op jit(solution)/shard_map/ppermute | solution.py:430
  2.9 4.0 %collective-permute-start.4 = (f32[3,2,2,8,128]{4,3,2,1,0:T(8,128)S(1)}, f32[3,2,2,8,128]{4,3,2,1,0:T(8,128)S(1)}, u32[]{:S(2)}, u32[]{:S(2)}) collective-permute-start(f32[3,2,2,8,128]{4,3,2,1,0:T(8,128)S(1)} %get-tuple-element.17), channel_id=1, source_target_pairs={{0,2},{1,3},{2,0},{3,1},{4,6},{5,7},{6,4},{7,5},{8,10},{9,11},{10,... | collective-permute-start | bytes 147464 | tf_op jit(solution)/shard_map/ppermute | solution.py:431
  6.9 0.0 collective-permute-done.refs_3_
  6.9 0.0 collective-permute-done.1.refs_4_
  6.9 0.0 collective-permute-done.2.refs_5_
  6.9 3.3 %shard_map.85 = (f32[3,4,32,8,128]{4,3,2,1,0:T(8,128)S(1)}, f32[3,4,32,8,128]{4,3,2,1,0:T(8,128)S(1)}, s32[14,8,128]{2,1,0:T(8,128)S(1)}, f32[12,8,128]{2,1,0:T(8,128)S(1)}) custom-call(f32[2,256,128]{2,1,0:T(8,128)} %bitcast.35, f32[2,256,128]{2,1,0:T(8,128)} %bitcast.38, f32[2,256,128]{2,1,0:T(8,128)} %bitcast.41, ...), custom_call_target="tpu_custom_call" | custom-call | bytes 10000000 | tf_op jit(solution)/shard_map/pallas_call | solution.py:433
  10.2 0.0 collective-permute-done.3.refs_6_
  10.2 0.0 collective-permute-done.4.refs_5_
  10.2 0.1 collective-permute-start.5
  10.3 0.5 %collective-permute-start.6 = (f32[3,2,2,8,128]{4,3,2,1,0:T(8,128)S(1)}, f32[3,2,2,8,128]{4,3,2,1,0:T(8,128)S(1)}, u32[]{:S(2)}, u32[]{:S(2)}) collective-permute-start(f32[3,2,2,8,128]{4,3,2,1,0:T(8,128)S(1)} %collective-permute-done.3.refs_6_), channel_id=1, source_target_pairs={{0,1},{1,0},{2,3},{3,2},{4,5},{5,4},{6,7},{7,6},{8,9},{9,8},{10,11... | collective-permute-start | bytes 147464 | tf_op jit(solution)/shard_map/ppermute | solution.py:452
  10.8 1.3 %shard_map.87.refs_2_ = f32[3,2,256,128]{3,2,1,0:T(8,128)S(1)} custom-call(f32[3,4,32,8,128]{4,3,2,1,0:T(8,128)S(1)} %get-tuple-element.19.refs_0_.refs_1_, s32[14,8,128]{2,1,0:T(8,128)S(1)} %get-tuple-element.20.refs_1_.refs_3_, f32[12,8,128]{2,1,0:T(8,128)S(1)} %get-tuple-element.21.refs_2_.refs_4_), custom_call_target="tpu_custom_call" | custom-call | bytes 10000000 | tf_op jit(solution)/shard_map/pallas_call | solution.py:454
  12.1 0.0 collective-permute-done.5.refs_7_
  12.1 0.0 collective-permute-done.6.refs_8_
  12.1 1.6 %shard_map.88 = (f32[2,256,128]{2,1,0:T(8,128)}, f32[2,256,128]{2,1,0:T(8,128)}, f32[2,256,128]{2,1,0:T(8,128)}) custom-call(f32[3,4,32,8,128]{4,3,2,1,0:T(8,128)S(1)} %get-tuple-element.15.refs_0_, f32[3,4,32,8,128]{4,3,2,1,0:T(8,128)S(1)} %get-tuple-element.19.refs_0_.refs_1_, f32[3,2,256,128]{3,2,1,0:T(8,128)S(1)} %shard_map.87.refs_2_, ...), custom_call_target="tpu_custom_call" | custom-call | bytes 1000000 | tf_op jit(solution)/shard_map/pallas_call | solution.py:466
Async XLA Ops:
  0.6 6.2 %collective-permute-start = (f32[2,256,128]{2,1,0:T(8,128)}, f32[2,256,128]{2,1,0:T(8,128)S(1)}, u32[]{:S(2)}, u32[]{:S(2)}) collective-permute-start(f32[2,256,128]{2,1,0:T(8,128)} %bitcast.33), channel_id=1, source_target_pairs={{0,1},{1,0},{2,3},{3,2},{4,5},{5,4},{6,7},{7,6},{8,9},{9,8},{10,11... | collective-permute-start | bytes 786440 | tf_op jit(solution)/shard_map/ppermute | solution.py:412
  1.1 5.7 %collective-permute-start.1 = (f32[2,256,128]{2,1,0:T(8,128)}, f32[2,256,128]{2,1,0:T(8,128)S(1)}, u32[]{:S(2)}, u32[]{:S(2)}) collective-permute-start(f32[2,256,128]{2,1,0:T(8,128)} %bitcast.36), channel_id=1, source_target_pairs={{0,1},{1,0},{2,3},{3,2},{4,5},{5,4},{6,7},{7,6},{8,9},{9,8},{10,11... | collective-permute-start | bytes 786440 | tf_op jit(solution)/shard_map/ppermute | solution.py:412
  1.2 5.6 %collective-permute-start.2 = (f32[2,256,128]{2,1,0:T(8,128)}, f32[2,256,128]{2,1,0:T(8,128)S(1)}, u32[]{:S(2)}, u32[]{:S(2)}) collective-permute-start(f32[2,256,128]{2,1,0:T(8,128)} %bitcast.39), channel_id=1, source_target_pairs={{0,1},{1,0},{2,3},{3,2},{4,5},{5,4},{6,7},{7,6},{8,9},{9,8},{10,11... | collective-permute-start | bytes 786440 | tf_op jit(solution)/shard_map/ppermute | solution.py:412
  2.7 7.4 %collective-permute-start.3 = (f32[3,2,2,8,128]{4,3,2,1,0:T(8,128)S(1)}, f32[3,2,2,8,128]{4,3,2,1,0:T(8,128)S(1)}, u32[]{:S(2)}, u32[]{:S(2)}) collective-permute-start(f32[3,2,2,8,128]{4,3,2,1,0:T(8,128)S(1)} %get-tuple-element.16), channel_id=1, source_target_pairs={{0,1},{1,0},{2,4},{3,5},{4,2},{5,3},{6,8},{7,9},{8,6},{9,7},{10,12... | collective-permute-start | bytes 147464 | tf_op jit(solution)/shard_map/ppermute | solution.py:430
  2.9 7.3 %collective-permute-start.4 = (f32[3,2,2,8,128]{4,3,2,1,0:T(8,128)S(1)}, f32[3,2,2,8,128]{4,3,2,1,0:T(8,128)S(1)}, u32[]{:S(2)}, u32[]{:S(2)}) collective-permute-start(f32[3,2,2,8,128]{4,3,2,1,0:T(8,128)S(1)} %get-tuple-element.17), channel_id=1, source_target_pairs={{0,2},{1,3},{2,0},{3,1},{4,6},{5,7},{6,4},{7,5},{8,10},{9,11},{10,... | collective-permute-start | bytes 147464 | tf_op jit(solution)/shard_map/ppermute | solution.py:431
  10.2 1.9 %collective-permute-start.5 = (f32[3,2,2,8,128]{4,3,2,1,0:T(8,128)S(1)}, f32[3,2,2,8,128]{4,3,2,1,0:T(8,128)S(1)}, u32[]{:S(2)}, u32[]{:S(2)}) collective-permute-start(f32[3,2,2,8,128]{4,3,2,1,0:T(8,128)S(1)} %collective-permute-done.4.refs_5_), channel_id=1, source_target_pairs={{0,1},{1,0},{2,3},{3,2},{4,5},{5,4},{6,7},{7,6},{8,9},{9,8},{10,11... | collective-permute-start | bytes 147464 | tf_op jit(solution)/shard_map/ppermute | solution.py:453
  10.3 1.9 %collective-permute-start.6 = (f32[3,2,2,8,128]{4,3,2,1,0:T(8,128)S(1)}, f32[3,2,2,8,128]{4,3,2,1,0:T(8,128)S(1)}, u32[]{:S(2)}, u32[]{:S(2)}) collective-permute-start(f32[3,2,2,8,128]{4,3,2,1,0:T(8,128)S(1)} %collective-permute-done.3.refs_6_), channel_id=1, source_target_pairs={{0,1},{1,0},{2,3},{3,2},{4,5},{5,4},{6,7},{7,6},{8,9},{9,8},{10,11... | collective-permute-start | bytes 147464 | tf_op jit(solution)/shard_map/ppermute | solution.py:452

commit v4 on v3

v4 whole, which is shorter than its diff:
```python
import functools

import jax
import jax.numpy as jnp
from jax import lax
from jax.experimental import pallas as pl
from jax.experimental.pallas import tpu as pltpu
from jax.sharding import PartitionSpec as P

RATE = 0.1
ANISO = 0.05
COUPLE = 0.5
DIFF_SOLUTE = 0.08
DIFF_HEAT = 0.15
TINY = 0.0001
ROWS, LANES = 8, 128
EDGE = 2
FIELDS = 3
AXES = ("slab", "bal")
CHUNK_FIRST = 4
SHIFTED_EARLY = 1
CHUNK_SECOND = 28
VMEM_BYTES = 40 * 2**20


def tiles_of(block):
    blocks, side, cells = block.shape
    split = block.reshape(blocks, side // ROWS, ROWS, cells // LANES, LANES)
    return split.transpose(0, 1, 3, 2, 4).reshape(blocks, side * cells // LANES, LANES)


def tile_grid(block):
    blocks, side, cells = block.shape
    split = block.reshape(blocks, side // ROWS, ROWS, cells // LANES, LANES)
    return split.transpose(0, 1, 3, 2, 4)


def block_of(tiles, side):
    blocks, rows, _ = tiles.shape
    columns = rows // side
    split = tiles.reshape(blocks, side // ROWS, columns, ROWS, LANES)
    return split.transpose(0, 1, 3, 2, 4).reshape(blocks, side, columns * LANES)


def plane_rows(x):
    return pl.ds((x >> 3) * ROWS * ROWS + (x & (ROWS - 1)), ROWS, stride=ROWS)


def lane_ids():
    return lax.broadcasted_iota(jnp.int32, (ROWS, LANES), 1)


class Geometry:
    def __init__(self, side):
        lanes = lane_ids()
        self.side = side
        self.y_last = lanes >= LANES - side
        self.y_first = lanes < side
        self.z_first = lanes % side == 0
        self.z_last = lanes % side == side - 1

    def up(self, plane):
        return pltpu.roll(plane, LANES - self.side, 1)

    def down(self, plane):
        return pltpu.roll(plane, self.side, 1)

    def y_pair(self, up, down):
        upper = jnp.where(self.y_last, pltpu.roll(up, ROWS - 1, 0), up)
        lower = jnp.where(self.y_first, pltpu.roll(down, 1, 0), down)
        return upper, lower

    def z_pair(self, plane, next_down, previous_up):
        upper = pltpu.roll(jnp.where(self.z_first, next_down, plane), LANES - 1, 1)
        lower = pltpu.roll(jnp.where(self.z_last, previous_up, plane), 1, 1)
        return upper, lower


def advance(centers, sums, differences, rate):
    phase, solute, heat = centers
    sum_phase, sum_solute, sum_heat = sums
    squares = [d * d for d in differences]
    square = squares[0] + squares[1] + squares[2]
    quartic = squares[0] * squares[0] + squares[1] * squares[1] + squares[2] * squares[2]
    below = square * square + 16.0 * TINY
    anisotropy = (1.0 - 3.0 * ANISO) + 4.0 * ANISO * (quartic / below)
    well = 1.0 - phase * phase
    forcing = well * (phase - COUPLE * well * (solute + heat))
    change = rate * (anisotropy * anisotropy * (sum_phase - 6.0 * phase) + forcing)
    half = 0.5 * change
    return (
        phase + change,
        (1.0 - 6.0 * DIFF_SOLUTE) * solute + (DIFF_SOLUTE * sum_solute + half),
        (1.0 - 6.0 * DIFF_HEAT) * heat + (DIFF_HEAT * sum_heat + half),
    )


def sides(geometry, center, up, down, next_down, previous_up, phase):
    y_upper, y_lower = geometry.y_pair(up, down)
    z_upper, z_lower = geometry.z_pair(center, next_down, previous_up)
    total = (y_upper + y_lower) + (z_upper + z_lower)
    return (total, y_upper - y_lower, z_upper - z_lower) if phase else (total,)


def keep_sides(geometry, around, b, x, center, up, down, next_down, previous_up):
    for f in range(FIELDS):
        found = sides(geometry, center(f), up(f), down(f), next_down(f), previous_up(f), f == 0)
        for k, value in enumerate(found):
            around[f if k == 0 else FIELDS - 1 + k, b, x] = value


def finish(below, center, above, around, rate):
    sums = [(above[f] + below[f]) + around[f] for f in range(FIELDS)]
    return advance(center, sums, (above[0] - below[0], around[FIELDS], around[FIELDS + 1]), rate)


def planes_at(ref, p, x):
    return [ref[f, p, x] for f in range(FIELDS)]


def rate_of(active):
    return jnp.where(active != 0, jnp.float32(RATE), jnp.float32(0.0))


def start_tables(tables, held, sem):
    copies = [pltpu.make_async_copy(t, h, sem.at[i]) for i, (t, h) in enumerate(zip(tables, held))]
    for copy in copies:
        copy.start()
    return copies


def holders(before, layer, core, blocks, cores):
    found = [0] * (blocks * cores)
    for place in range(blocks * cores):
        owner = core if place < blocks else cores - 1 - core
        at = before[owner * blocks + place % blocks, layer]
        found = [jnp.where(at == p, place, found[p]) for p in range(len(found))]
    return found


def pack_kernel(side, *refs):
    grids, (even_ref, odd_ref, sem) = refs[:FIELDS], refs[FIELDS:]

    def faces(upper_ref, lower_ref):
        return [
            pltpu.make_async_copy(grids[f].at[:, row // ROWS, :, row % ROWS, :], ref.at[f, :, d], sem.at[f, end, d])
            for f in range(FIELDS)
            for d in range(EDGE)
            for end, ref, row in ((0, lower_ref, d), (1, upper_ref, side - 1 - d))
        ]

    is_even = lax.rem(lax.axis_index("slab"), 2) == 0

    @pl.when(is_even)
    def _():
        for copy in faces(even_ref, odd_ref):
            copy.start()

    @pl.when(jnp.logical_not(is_even))
    def _():
        for copy in faces(odd_ref, even_ref):
            copy.start()

    for copy in faces(even_ref, odd_ref):
        copy.wait()


def spread(geometry, planes, slots, own, others, raw, ups, downs):
    blocks = own.shape[1]
    for x in planes:
        for f in range(FIELDS):
            for k in slots:
                source = own.at[f] if k < blocks else others[f]
                plane = source[k % blocks, plane_rows(x)]
                raw[f, k, x] = plane
                ups[f, k, x] = geometry.up(plane)
                downs[f, k, x] = geometry.down(plane)


def early_kernel(side, blocks, cores, *refs):
    fields, others = refs[:FIELDS], refs[FIELDS : 2 * FIELDS]
    raw, ups, downs, own, own_sem = refs[2 * FIELDS :]

    @pl.when(lax.axis_index("slab") == 0)
    def _():
        own_copies = [pltpu.make_async_copy(fields[f], own.at[f], own_sem.at[f]) for f in range(FIELDS)]
        for copy in own_copies:
            copy.start()
        geometry = Geometry(side)
        spread(geometry, range(side), range(blocks, blocks * cores), own, others, raw, ups, downs)
        for copy in own_copies:
            copy.wait()
        spread(geometry, range(side), range(blocks), own, others, raw, ups, downs)


def first_kernel(side, blocks, cores, layers, *refs):
    fields, others, tables = refs[:FIELDS], refs[FIELDS : 2 * FIELDS], refs[2 * FIELDS : 2 * FIELDS + 3]
    outs, scratch = refs[2 * FIELDS + 6 : 2 * FIELDS + 15], refs[2 * FIELDS + 15 :]
    raw, ups, downs, stepped, next_ups, next_downs, face_around, places_out, rates_out = outs
    own, around, before, after, flags, own_sem, table_sem = scratch
    ring = blocks * cores
    layer, core = lax.axis_index("slab"), lax.axis_index("bal")
    is_spread = layer == 0
    own_copies = [pltpu.make_async_copy(fields[f], own.at[f], own_sem.at[f]) for f in range(FIELDS)]

    @pl.when(jnp.logical_not(is_spread))
    def _():
        for copy in own_copies:
            copy.start()

    table_copies = start_tables(tables, (before, after, flags), table_sem)
    geometry = Geometry(side)

    @pl.when(jnp.logical_not(is_spread))
    def _():
        spread(geometry, range(side), range(blocks, ring), own, others, raw, ups, downs)
        for copy in own_copies:
            copy.wait()
        spread(geometry, range(CHUNK_FIRST), range(blocks), own, others, raw, ups, downs)

    for copy in table_copies:
        copy.wait()
    beside = [jnp.clip(layer + 2 * end - 1, 0, layers - 1) for end in range(2)]
    places = holders(before, layer, core, blocks, cores)
    listed = places + [after[core * blocks + b, layer] for b in range(blocks)]
    for table in beside:
        for c in range(cores):
            slot = jnp.where(c == 0, core, cores - 1 - core) * blocks
            listed += [before[slot + b, table] for b in range(blocks)]
    for k, place in enumerate(listed):
        places_out[k] = jnp.full((ROWS, LANES), place, jnp.int32)
    rates = [rate_of(flags[p, table]) for table in [layer] + beside for p in range(ring)]
    for k, rate in enumerate(rates):
        rates_out[k] = jnp.full((ROWS, LANES), rate, jnp.float32)

    def gather(planes):
        for x in planes:
            face = x in (0, side - 1)
            for p in range(ring):
                here, following, previous = places[p], places[(p + 1) % ring], places[(p - 1) % ring]
                keep_sides(
                    geometry,
                    face_around if face else around,
                    p,
                    x // (side - 1) if face else x,
                    lambda f: raw[f, here, x],
                    lambda f: ups[f, here, x],
                    lambda f: downs[f, here, x],
                    lambda f: downs[f, following, x],
                    lambda f: ups[f, previous, x],
                )

    def calculate(planes):
        for x in planes:
            for p in range(ring):
                low, center, high = (planes_at(raw, places[p], x + d) for d in (-1, 0, 1))
                new = finish(low, center, high, [around[k, p, x] for k in range(FIELDS + 2)], rates[p])
                for f in range(FIELDS):
                    stepped[f, p, x] = new[f]
                    if f < SHIFTED_EARLY:
                        next_ups[f, p, x] = geometry.up(new[f])
                        next_downs[f, p, x] = geometry.down(new[f])

    def steps(spread_too):
        count = side // CHUNK_FIRST
        for c in range(count):
            planes = range(c * CHUNK_FIRST, (c + 1) * CHUNK_FIRST)
            gather(planes)
            if spread_too and c + 1 < count:
                ahead = [x + CHUNK_FIRST for x in planes]
                spread(geometry, ahead, range(blocks), own, others, raw, ups, downs)
            calculate([x for x in planes if 0 < x < side - 1])

    pl.when(is_spread)(lambda: steps(False))
    pl.when(jnp.logical_not(is_spread))(lambda: steps(True))


def place_at(ref, k):
    return ref[k][0, 0]


def second_kernel(side, blocks, cores, *refs):
    stepped, ups, downs, places_ref, rates_ref, result, rim_around, shifted, around = refs
    ring = blocks * cores
    geometry = Geometry(side)
    places = [place_at(places_ref, ring + b) for b in range(blocks)]
    rates = [rates_ref[p] for p in places]

    rounds = [(p, (p + 1) & (ring - 1), (p + ring - 1) & (ring - 1)) for p in places]

    def shift(x):
        for b, (p, following, previous) in enumerate(rounds):
            for f in range(SHIFTED_EARLY, FIELDS):
                shifted[0, f, b, x] = geometry.up(stepped[f, p, x])
                shifted[1, f, b, x] = geometry.down(stepped[f, p, x])
                shifted[2, f, b, x] = geometry.down(stepped[f, following, x])
                shifted[3, f, b, x] = geometry.up(stepped[f, previous, x])

    def gather(x, target, at):
        for b, (p, following, previous) in enumerate(rounds):
            keep_sides(
                geometry,
                target,
                b,
                at,
                lambda f: stepped[f, p, x],
                lambda f: ups[f, p, x] if f < SHIFTED_EARLY else shifted[0, f, b, x],
                lambda f: downs[f, p, x] if f < SHIFTED_EARLY else shifted[1, f, b, x],
                lambda f: downs[f, following, x] if f < SHIFTED_EARLY else shifted[2, f, b, x],
                lambda f: ups[f, previous, x] if f < SHIFTED_EARLY else shifted[3, f, b, x],
            )

    @pl.loop(0, (side - 4) // CHUNK_SECOND)
    def _(i):
        planes = [2 + i * CHUNK_SECOND + u for u in range(CHUNK_SECOND)]
        for x in planes:
            shift(x)
        for x in planes:
            gather(x, around, x)
        for x in planes:
            for b, p in enumerate(places):
                low, center, high = (planes_at(stepped, p, x + d) for d in (-1, 0, 1))
                new = finish(low, center, high, [around[k, b, x] for k in range(FIELDS + 2)], rates[b])
                for f in range(FIELDS):
                    result[f, b, plane_rows(x)] = new[f]

    for end in range(2):
        shift(1 + end * (side - 3))
    for end in range(2):
        gather(1 + end * (side - 3), rim_around, end)


def rim_kernel(side, blocks, cores, layers, *refs):
    raw, inner, result, face_around, rim_around, places_ref, rates_ref = refs[:7]
    messages = refs[7:11]
    outs = refs[11 : 11 + FIELDS]
    halo, faces, shifted, around, tiles, sem, middle_sem = refs[11 + FIELDS :]
    ring = blocks * cores
    layer = lax.axis_index("slab")
    parity = lax.rem(layer, 2)
    geometry = Geometry(side)
    rows = ROWS * ROWS
    middle = pl.ds(rows, side * ROWS - 2 * rows)
    copies = [
        pltpu.make_async_copy(result.at[f, :, middle], outs[f].at[:, middle], middle_sem.at[f])
        for f in range(FIELDS)
    ]
    for copy in copies:
        copy.start()
    places = [place_at(places_ref, p) for p in range(ring)]
    targets = [place_at(places_ref, ring + b) for b in range(blocks)]
    beside = [layer + 2 * end - 1 for end in range(2)]
    outside = [jnp.logical_or(b < 0, b >= layers) for b in beside]
    ends = range(2)

    def at_face(end, p, d):
        return planes_at(raw, places[p], d if end == 0 else side - 1 - d)

    for end in ends:
        from_even = parity == 1 - end
        for c in range(cores):
            for b in range(blocks):
                p = place_at(places_ref, ring + blocks + (end * cores + c) * blocks + b)
                for f in range(FIELDS):
                    for d in range(EDGE):
                        halo[end, f, p, d] = jnp.where(
                            from_even, messages[2 * c][f, b, d], messages[2 * c + 1][f, b, d]
                        )
    for f in range(FIELDS):
        for end in ends:
            tiles[f, end] = result[f, :, pl.ds(end * (side * ROWS - rows), rows)]
    for end in ends:
        for p in range(ring):
            for f in range(FIELDS):
                near = jnp.where(outside[end], at_face(end, p, 0)[f], halo[end, f, p, 0])
                halo[end, f, p, 0] = near
                shifted[0, end, f, p] = geometry.up(near)
                shifted[1, end, f, p] = geometry.down(near)
    for end in ends:
        for p in range(ring):
            new = finish(
                [halo[end, f, p, 0] for f in range(FIELDS)],
                at_face(end, p, 0),
                at_face(end, p, 1),
                [face_around[k, p, end] for k in range(FIELDS + 2)],
                rates_ref[p],
            )
            for f in range(FIELDS):
                faces[end, f, p, 1] = new[f]
    for end in ends:
        for p in range(ring):
            keep_sides(
                geometry,
                around,
                p,
                end,
                lambda f: halo[end, f, p, 0],
                lambda f: shifted[0, end, f, p],
                lambda f: shifted[1, end, f, p],
                lambda f: shifted[1, end, f, (p + 1) % ring],
                lambda f: shifted[0, end, f, (p - 1) % ring],
            )
    rounds = [(p, (p + 1) & (ring - 1), (p + ring - 1) & (ring - 1)) for p in targets]
    for end in ends:
        for b, (p, following, previous) in enumerate(rounds):
            for f in range(FIELDS):
                shifted[2, end, f, 4 * b] = geometry.up(faces[end, f, p, 1])
                shifted[2, end, f, 4 * b + 1] = geometry.down(faces[end, f, p, 1])
                shifted[2, end, f, 4 * b + 2] = geometry.down(faces[end, f, following, 1])
                shifted[2, end, f, 4 * b + 3] = geometry.up(faces[end, f, previous, 1])
    for end in ends:
        for p in range(ring):
            new = finish(
                [halo[end, f, p, 1] for f in range(FIELDS)],
                [halo[end, f, p, 0] for f in range(FIELDS)],
                at_face(end, p, 0),
                [around[k, p, end] for k in range(FIELDS + 2)],
                rates_ref[ring * (1 + end) + p],
            )
            for f in range(FIELDS):
                faces[end, f, p, 0] = jnp.where(outside[end], faces[end, f, p, 1], new[f])
    for end in ends:
        for b, (p, following, previous) in enumerate(rounds):
            keep_sides(
                geometry,
                around,
                ring + b,
                end,
                lambda f: faces[end, f, p, 1],
                lambda f: shifted[2, end, f, 4 * b],
                lambda f: shifted[2, end, f, 4 * b + 1],
                lambda f: shifted[2, end, f, 4 * b + 2],
                lambda f: shifted[2, end, f, 4 * b + 3],
            )
    for end in ends:
        for b, p in enumerate(targets):
            outer, face = ([faces[end, f, p, d] for f in range(FIELDS)] for d in range(2))
            first, second = (planes_at(inner, p, d if end == 0 else side - 1 - d) for d in (1, 2))
            news = (
                finish(outer, face, first, [around[k, ring + b, end] for k in range(FIELDS + 2)], rates_ref[p]),
                finish(face, first, second, [rim_around[k, b, end] for k in range(FIELDS + 2)], rates_ref[p]),
            )
            for d in range(EDGE):
                row = d if end == 0 else ROWS - 1 - d
                for f in range(FIELDS):
                    tiles[f, end, b, pl.ds(row, ROWS, stride=ROWS)] = news[d][f]
        for f in range(FIELDS):
            part = pl.ds(end * (side * ROWS - rows), rows)
            copies.append(pltpu.make_async_copy(tiles.at[f, end], outs[f].at[:, part], sem.at[f, end]))
            copies[-1].start()
    for copy in copies:
        copy.wait()


def neighbour_swaps(layers, cores, first):
    pairs = []
    for layer in range(layers):
        partner = layer + 1 if (layer - first) % 2 == 0 else layer - 1
        for core in range(cores):
            here = layer * cores + core
            if 0 <= partner < layers:
                pairs.append((here, partner * cores + core))
            else:
                pairs.append((here, layer * cores + cores - 1 - core))
    return pairs


def body(layers, cores, order_parameter, concentration_excess, thermal_subcooling, before, after, flags):
    blocks, side = order_parameter.shape[1], order_parameter.shape[2]
    ring = blocks * cores
    rows = side * ROWS
    f32 = jnp.float32
    before, after, flags = before.T, after.T, flags.T
    owners = [(s * cores + c, s * cores + cores - 1 - c) for s in range(layers) for c in range(cores)]
    fields = [tiles_of(a[0]) for a in (order_parameter, concentration_excess, thermal_subcooling)]
    others = [lax.ppermute(a, AXES, owners) for a in fields]
    vmem, hbm = (pl.BlockSpec(memory_space=m) for m in (pltpu.VMEM, pltpu.HBM))
    params = pltpu.CompilerParams(vmem_limit_bytes=VMEM_BYTES)
    message = jax.ShapeDtypeStruct((FIELDS, blocks, EDGE, ROWS, LANES), f32)
    table = pltpu.SMEM(before.shape, jnp.int32)
    in_hbm = lambda *arrays: [pltpu.with_memory_space_constraint(a, pltpu.HBM) for a in arrays]
    grids = [tile_grid(a[0]) for a in (order_parameter, concentration_excess, thermal_subcooling)]
    even, odd = pl.pallas_call(
        functools.partial(pack_kernel, side),
        out_shape=(message, message),
        in_specs=[hbm] * FIELDS,
        out_specs=(vmem,) * 2,
        scratch_shapes=[pltpu.SemaphoreType.DMA((FIELDS, 2, EDGE))],
        compiler_params=params,
        cost_estimate=pl.CostEstimate(flops=0, bytes_accessed=10**6, transcendentals=0),
    )(*in_hbm(*grids))
    planes = (FIELDS, ring, side, ROWS, LANES)
    kept = FIELDS + 2
    three = (jax.ShapeDtypeStruct(planes, f32),) * 3
    own_scratch = pltpu.VMEM((FIELDS, blocks, rows, LANES), f32)
    odd_in = lax.ppermute(odd, AXES, neighbour_swaps(layers, cores, 1))
    early = pl.pallas_call(
        functools.partial(early_kernel, side, blocks, cores),
        out_shape=three,
        in_specs=[hbm] * FIELDS + [vmem] * FIELDS,
        out_specs=(vmem,) * 3,
        scratch_shapes=[own_scratch, pltpu.SemaphoreType.DMA((FIELDS,))],
        compiler_params=params,
        cost_estimate=pl.CostEstimate(flops=0, bytes_accessed=10**6, transcendentals=0),
    )(*in_hbm(*fields), *others)
    even, *early = lax.optimization_barrier((even, *early))
    even_in = lax.ppermute(even, AXES, neighbour_swaps(layers, cores, 0))
    raw, _, _, stepped, ups, downs, face_around, places, rates = pl.pallas_call(
        functools.partial(first_kernel, side, blocks, cores, layers),
        out_shape=three * 2
        + (
            jax.ShapeDtypeStruct((kept, ring, 2, ROWS, LANES), f32),
            jax.ShapeDtypeStruct((3 * ring + blocks, ROWS, LANES), jnp.int32),
            jax.ShapeDtypeStruct((3 * ring, ROWS, LANES), f32),
        ),
        in_specs=[hbm] * FIELDS + [vmem] * FIELDS + [hbm] * 3 + [vmem] * 3,
        out_specs=(vmem,) * 9,
        input_output_aliases={2 * FIELDS + 3 + k: k for k in range(3)},
        scratch_shapes=[own_scratch, pltpu.VMEM((kept, ring, side, ROWS, LANES), f32)]
        + [table] * 3
        + [pltpu.SemaphoreType.DMA((FIELDS,)), pltpu.SemaphoreType.DMA((3,))],
        compiler_params=params,
        cost_estimate=pl.CostEstimate(flops=0, bytes_accessed=10**7, transcendentals=0),
    )(*in_hbm(*fields), *others, *in_hbm(before, after, flags), *early)
    odd_in, even_in, stepped = lax.optimization_barrier((odd_in, even_in, stepped))
    odd_other = lax.ppermute(odd_in, AXES, owners)
    even_other = lax.ppermute(even_in, AXES, owners)
    result, rim_around = pl.pallas_call(
        functools.partial(second_kernel, side, blocks, cores),
        out_shape=(
            jax.ShapeDtypeStruct((FIELDS, blocks, rows, LANES), f32),
            jax.ShapeDtypeStruct((kept, blocks, 2, ROWS, LANES), f32),
        ),
        in_specs=[vmem] * 5,
        out_specs=(vmem,) * 2,
        scratch_shapes=[
            pltpu.VMEM((4, FIELDS, blocks, side, ROWS, LANES), f32),
            pltpu.VMEM((kept, blocks, side, ROWS, LANES), f32),
        ],
        compiler_params=params,
        cost_estimate=pl.CostEstimate(flops=0, bytes_accessed=10**7, transcendentals=0),
    )(stepped, ups, downs, places, rates)
    results = pl.pallas_call(
        functools.partial(rim_kernel, side, blocks, cores, layers),
        out_shape=(jax.ShapeDtypeStruct((blocks, rows, LANES), f32),) * FIELDS,
        in_specs=[vmem] * 11,
        out_specs=(hbm,) * FIELDS,
        scratch_shapes=[
            pltpu.VMEM((2, FIELDS, ring, EDGE, ROWS, LANES), f32),
            pltpu.VMEM((2, FIELDS, ring, 2, ROWS, LANES), f32),
            pltpu.VMEM((3, 2, FIELDS, max(ring, 4 * blocks), ROWS, LANES), f32),
            pltpu.VMEM((kept, ring + blocks, 2, ROWS, LANES), f32),
            pltpu.VMEM((FIELDS, 2, blocks, ROWS * ROWS, LANES), f32),
            pltpu.SemaphoreType.DMA((FIELDS, 2)),
            pltpu.SemaphoreType.DMA((FIELDS,)),
        ],
        compiler_params=params,
        cost_estimate=pl.CostEstimate(flops=0, bytes_accessed=10**6, transcendentals=0),
    )(raw, stepped, result, face_around, rim_around, places, rates, even_in, odd_in, even_other, odd_other)
    return tuple(block_of(r, side)[None] for r in results)


def solution(mesh):
    layers, cores = mesh.shape["slab"], mesh.shape["bal"]
    split, copied = P("slab", "bal", None, None), P()
    return jax.shard_map(
        functools.partial(body, layers, cores),
        mesh=mesh,
        in_specs=(split,) * 3 + (copied,) * 3,
        out_specs=(split,) * 3,
        check_vma=False,
    )
```

time: 13.9 us -> 13 us (0.935)
  starting transfers between devices: 5.72 us -> 3.46 us
  waiting for transfers between devices: 0.02 us -> 0.9 us
  Pallas kernels: 7.32 us -> 7.73 us
    ppermute x1, starting transfers between devices: 3.98 us -> 1.78 us  [body(): even_in = lax.ppermute(even, AXES, neighbour_swaps(layers, cores, 0))]
    pallas_call x0 -> x1, Pallas kernels: none -> 1.81 us  [body(): pl.pallas_call(functools.partial(early_kernel, side, blocks, cores), out_...]
    pallas_call x1, Pallas kernels: 3.28 us -> 2.58 us  [body(): pl.pallas_call(functools.partial(first_kernel, side, blocks, cores, layer...]
    ppermute x3, waiting for transfers between devices: 0.01 us -> 0.51 us  [body(): others = [lax.ppermute(a, AXES, owners) for a in fields]]
    ppermute x1, waiting for transfers between devices: 0.01 us -> 0.39 us  [body(): even_in = lax.ppermute(even, AXES, neighbour_swaps(layers, cores, 0))]
    pallas_call x1, Pallas kernels: 1.62 us -> 1.24 us  [body(): pl.pallas_call(functools.partial(rim_kernel, side, blocks, cores, layers)...]
    pallas_call x1, Pallas kernels: 1.35 us -> 1.16 us  [body(): pl.pallas_call(functools.partial(second_kernel, side, blocks, cores), out...]
  transfers between devices with their start and end apart: 7 -> 7, of which waited for: 0 -> 3; matrix products, arithmetic and copies ran while one was open for 0% -> 0% of each run, Pallas kernels for 41% -> 51%
where the time goes in v4:
time: 13 us; the launch traced here: 12.8 us
  Pallas kernels  7.73 us (59%)
  starting transfers between devices  3.46 us (27%)
  waiting for transfers between devices  0.9 us (7%)
  between operations  0.69 us (5%)
    pallas_call x1, Pallas kernels, body(): pl.pallas_call(functools.partial(first_kernel, side, blocks, cores, layer...  2.58 us
    pallas_call x1, Pallas kernels, body(): pl.pallas_call(functools.partial(early_kernel, side, blocks, cores), out_...  1.81 us
    ppermute x1, starting transfers between devices, body(): even_in = lax.ppermute(even, AXES, neighbour_swaps(layers, cores, 0))  1.78 us
    pallas_call x1, Pallas kernels, body(): pl.pallas_call(functools.partial(rim_kernel, side, blocks, cores, layers)...  1.24 us
    pallas_call x1, Pallas kernels, body(): pl.pallas_call(functools.partial(second_kernel, side, blocks, cores), out...  1.16 us
    ppermute x3, starting transfers between devices, body(): others = [lax.ppermute(a, AXES, owners) for a in fields]  1.03 us
    pallas_call x1, Pallas kernels, body(): pl.pallas_call(functools.partial(pack_kernel, side), out_shape=(message,...  0.95 us
    ppermute x3, waiting for transfers between devices, body(): others = [lax.ppermute(a, AXES, owners) for a in fields]  0.51 us
  transfers between devices with their start and end apart: 7, of which 3 were waited for; matrix products, arithmetic and copies ran while one was open for 0% of the time, Pallas kernels for 51%

profile of v4, /device:TPU:0, one launch (start us, length us, event | category | flops | bytes accessed | tf_op | source)
XLA Modules:
  0.0 12.8 jit_solution(5911704131729150904)
XLA Ops:
  0.6 0.5 %collective-permute-start = (f32[2,256,128]{2,1,0:T(8,128)}, f32[2,256,128]{2,1,0:T(8,128)S(1)}, u32[]{:S(2)}, u32[]{:S(2)}) collective-permute-start(f32[2,256,128]{2,1,0:T(8,128)} %bitcast.33), channel_id=1, source_target_pairs={{0,1},{1,0},{2,3},{3,2},{4,5},{5,4},{6,7},{7,6},{8,9},{9,8},{10,11... | collective-permute-start | bytes 786440 | tf_op jit(solution)/shard_map/ppermute | solution.py:476
  1.1 0.1 collective-permute-start.1
  1.2 0.4 %collective-permute-start.2 = (f32[2,256,128]{2,1,0:T(8,128)}, f32[2,256,128]{2,1,0:T(8,128)S(1)}, u32[]{:S(2)}, u32[]{:S(2)}) collective-permute-start(f32[2,256,128]{2,1,0:T(8,128)} %bitcast.41), channel_id=1, source_target_pairs={{0,1},{1,0},{2,3},{3,2},{4,5},{5,4},{6,7},{7,6},{8,9},{9,8},{10,11... | collective-permute-start | bytes 786440 | tf_op jit(solution)/shard_map/ppermute | solution.py:476
  1.7 0.9 %shard_map.85 = (f32[3,2,2,8,128]{4,3,2,1,0:T(8,128)S(1)}, f32[3,2,2,8,128]{4,3,2,1,0:T(8,128)S(1)}) custom-call(f32[2,4,8,8,128]{4,3,2,1,0:T(8,128)} %bitcast.34, f32[2,4,8,8,128]{4,3,2,1,0:T(8,128)} %bitcast.38, f32[2,4,8,8,128]{4,3,2,1,0:T(8,128)} %bitcast.42), custom_call_target="tpu_custom_call" | custom-call | bytes 1000000 | tf_op jit(solution)/shard_map/pallas_call | solution.py:483
  2.6 0.1 %collective-permute-start.3 = (f32[3,2,2,8,128]{4,3,2,1,0:T(8,128)S(1)}, f32[3,2,2,8,128]{4,3,2,1,0:T(8,128)S(1)}, u32[]{:S(2)}, u32[]{:S(2)}) collective-permute-start(f32[3,2,2,8,128]{4,3,2,1,0:T(8,128)S(1)} %get-tuple-element.35), channel_id=1, source_target_pairs={{0,1},{1,0},{2,4},{3,5},{4,2},{5,3},{6,8},{7,9},{8,6},{9,7},{10,12... | collective-permute-start | bytes 147464 | tf_op jit(solution)/shard_map/ppermute | solution.py:496
  2.8 0.0 collective-permute-done.refs_3_
  2.8 0.1 %collective-permute-done.1.refs_4_ = f32[2,256,128]{2,1,0:T(8,128)S(1)} collective-permute-done((f32[2,256,128]{2,1,0:T(8,128)}, f32[2,256,128]{2,1,0:T(8,128)S(1)}, u32[]{:S(2)}, u32[]{:S(2)}) %collective-permute-start.1) | collective-permute-done | bytes 262176 | tf_op jit(solution)/shard_map/ppermute | solution.py:476
  2.9 0.4 %collective-permute-done.2.refs_5_ = f32[2,256,128]{2,1,0:T(8,128)S(1)} collective-permute-done((f32[2,256,128]{2,1,0:T(8,128)}, f32[2,256,128]{2,1,0:T(8,128)S(1)}, u32[]{:S(2)}, u32[]{:S(2)}) %collective-permute-start.2) | collective-permute-done | bytes 262176 | tf_op jit(solution)/shard_map/ppermute | solution.py:476
  3.3 1.8 %shard_map.86 = (f32[3,4,32,8,128]{4,3,2,1,0:T(8,128)S(1)}, f32[3,4,32,8,128]{4,3,2,1,0:T(8,128)S(1)}, f32[3,4,32,8,128]{4,3,2,1,0:T(8,128)S(1)}) custom-call(f32[2,256,128]{2,1,0:T(8,128)} %bitcast.35, f32[2,256,128]{2,1,0:T(8,128)} %bitcast.39, f32[2,256,128]{2,1,0:T(8,128)} %bitcast.43, f32[2,256,128]{2,1,0:T(8,128)S(1)} %collective-permute-done.refs_3_, ...), custom_call_target="tpu_custom_call" | custom-call | bytes 1000000 | tf_op jit(solution)/shard_map/pallas_call | solution.py:497
  5.1 1.8 %collective-permute-start.4 = (f32[3,2,2,8,128]{4,3,2,1,0:T(8,128)S(1)}, f32[3,2,2,8,128]{4,3,2,1,0:T(8,128)S(1)}, u32[]{:S(2)}, u32[]{:S(2)}) collective-permute-start(f32[3,2,2,8,128]{4,3,2,1,0:T(8,128)S(1)} %get-tuple-element.36), channel_id=1, source_target_pairs={{0,2},{1,3},{2,0},{3,1},{4,6},{5,7},{6,4},{7,5},{8,10},{9,11},{10,... | collective-permute-start | bytes 147464 | tf_op jit(solution)/shard_map/ppermute | solution.py:507
  6.9 2.6 %shard_map.87 = (f32[3,4,32,8,128]{4,3,2,1,0:T(8,128)S(1)}, f32[3,4,32,8,128]{4,3,2,1,0:T(8,128)S(1)}, f32[3,4,32,8,128]{4,3,2,1,0:T(8,128)S(1)}, f32[3,4,32,8,1...) custom-call(f32[2,256,128]{2,1,0:T(8,128)} %bitcast.36, ...), custom_call_target="tpu_custom_call", output_to_operand_aliasing={{0}: (9, {}), {1}: (10, {}), {2}: (11, {})} | custom-call | bytes 10000000 | tf_op jit(solution)/shard_map/pallas_call | solution.py:508
  9.5 0.0 collective-permute-done.3.refs_8_
  9.5 0.4 %collective-permute-done.4.refs_7_ = f32[3,2,2,8,128]{4,3,2,1,0:T(8,128)S(1)} collective-permute-done((f32[3,2,2,8,128]{4,3,2,1,0:T(8,128)S(1)}, f32[3,2,2,8,128]{4,3,2,1,0:T(8,128)S(1)}, u32[]{:S(2)}, u32[]{:S(2)}) %collective-permute-start.4) | collective-permute-done | bytes 49184 | tf_op jit(solution)/shard_map/ppermute | solution.py:507
  9.9 0.0 collective-permute-start.5
  9.9 0.5 %collective-permute-start.6 = (f32[3,2,2,8,128]{4,3,2,1,0:T(8,128)S(1)}, f32[3,2,2,8,128]{4,3,2,1,0:T(8,128)S(1)}, u32[]{:S(2)}, u32[]{:S(2)}) collective-permute-start(f32[3,2,2,8,128]{4,3,2,1,0:T(8,128)S(1)} %collective-permute-done.3.refs_8_), channel_id=1, source_target_pairs={{0,1},{1,0},{2,3},{3,2},{4,5},{5,4},{6,7},{7,6},{8,9},{9,8},{10,11... | collective-permute-start | bytes 147464 | tf_op jit(solution)/shard_map/ppermute | solution.py:526
  10.4 1.2 %shard_map.88 = (f32[3,2,256,128]{3,2,1,0:T(8,128)S(1)}, f32[5,2,2,8,128]{4,3,2,1,0:T(8,128)S(1)}) custom-call(f32[3,4,32,8,128]{4,3,2,1,0:T(8,128)S(1)} %get-tuple-element.38.refs_0_.refs_1_, f32[3,4,32,8,128]{4,3,2,1,0:T(8,128)S(1)} %get-tuple-element.39.refs_1_, f32[3,4,32,8,128]{4,3,2,1,0:T(8,128)S(1)} %get-tuple-element.40.refs_2_, ...), custom_call_target="tpu_custom_call" | custom-call | bytes 10000000 | tf_op jit(solution)/shard_map/pallas_call | solution.py:528
  11.5 0.0 collective-permute-done.5.refs_9_
  11.5 0.0 collective-permute-done.6.refs_10_
  11.6 1.2 %shard_map.89 = (f32[2,256,128]{2,1,0:T(8,128)}, f32[2,256,128]{2,1,0:T(8,128)}, f32[2,256,128]{2,1,0:T(8,128)}) custom-call(f32[3,4,32,8,128]{4,3,2,1,0:T(8,128)S(1)} %get-tuple-element.34.refs_0_, f32[3,4,32,8,128]{4,3,2,1,0:T(8,128)S(1)} %get-tuple-element.38.refs_0_.refs_1_, f32[3,2,256,128]{3,2,1,0:T(8,128)S(1)} %get-tuple-element.43.refs_2_, ...), custom_call_target="tpu_custom_call" | custom-call | bytes 1000000 | tf_op jit(solution)/shard_map/pallas_call | solution.py:543
Async XLA Ops:
  0.6 2.1 %collective-permute-start = (f32[2,256,128]{2,1,0:T(8,128)}, f32[2,256,128]{2,1,0:T(8,128)S(1)}, u32[]{:S(2)}, u32[]{:S(2)}) collective-permute-start(f32[2,256,128]{2,1,0:T(8,128)} %bitcast.33), channel_id=1, source_target_pairs={{0,1},{1,0},{2,3},{3,2},{4,5},{5,4},{6,7},{7,6},{8,9},{9,8},{10,11... | collective-permute-start | bytes 786440 | tf_op jit(solution)/shard_map/ppermute | solution.py:476
  1.1 1.7 %collective-permute-start.1 = (f32[2,256,128]{2,1,0:T(8,128)}, f32[2,256,128]{2,1,0:T(8,128)S(1)}, u32[]{:S(2)}, u32[]{:S(2)}) collective-permute-start(f32[2,256,128]{2,1,0:T(8,128)} %bitcast.37), channel_id=1, source_target_pairs={{0,1},{1,0},{2,3},{3,2},{4,5},{5,4},{6,7},{7,6},{8,9},{9,8},{10,11... | collective-permute-start | bytes 786440 | tf_op jit(solution)/shard_map/ppermute | solution.py:476
  1.2 2.0 %collective-permute-start.2 = (f32[2,256,128]{2,1,0:T(8,128)}, f32[2,256,128]{2,1,0:T(8,128)S(1)}, u32[]{:S(2)}, u32[]{:S(2)}) collective-permute-start(f32[2,256,128]{2,1,0:T(8,128)} %bitcast.41), channel_id=1, source_target_pairs={{0,1},{1,0},{2,3},{3,2},{4,5},{5,4},{6,7},{7,6},{8,9},{9,8},{10,11... | collective-permute-start | bytes 786440 | tf_op jit(solution)/shard_map/ppermute | solution.py:476
  2.6 6.8 %collective-permute-start.3 = (f32[3,2,2,8,128]{4,3,2,1,0:T(8,128)S(1)}, f32[3,2,2,8,128]{4,3,2,1,0:T(8,128)S(1)}, u32[]{:S(2)}, u32[]{:S(2)}) collective-permute-start(f32[3,2,2,8,128]{4,3,2,1,0:T(8,128)S(1)} %get-tuple-element.35), channel_id=1, source_target_pairs={{0,1},{1,0},{2,4},{3,5},{4,2},{5,3},{6,8},{7,9},{8,6},{9,7},{10,12... | collective-permute-start | bytes 147464 | tf_op jit(solution)/shard_map/ppermute | solution.py:496
  5.1 4.8 %collective-permute-start.4 = (f32[3,2,2,8,128]{4,3,2,1,0:T(8,128)S(1)}, f32[3,2,2,8,128]{4,3,2,1,0:T(8,128)S(1)}, u32[]{:S(2)}, u32[]{:S(2)}) collective-permute-start(f32[3,2,2,8,128]{4,3,2,1,0:T(8,128)S(1)} %get-tuple-element.36), channel_id=1, source_target_pairs={{0,2},{1,3},{2,0},{3,1},{4,6},{5,7},{6,4},{7,5},{8,10},{9,11},{10,... | collective-permute-start | bytes 147464 | tf_op jit(solution)/shard_map/ppermute | solution.py:507
  9.9 1.7 %collective-permute-start.5 = (f32[3,2,2,8,128]{4,3,2,1,0:T(8,128)S(1)}, f32[3,2,2,8,128]{4,3,2,1,0:T(8,128)S(1)}, u32[]{:S(2)}, u32[]{:S(2)}) collective-permute-start(f32[3,2,2,8,128]{4,3,2,1,0:T(8,128)S(1)} %collective-permute-done.4.refs_7_), channel_id=1, source_target_pairs={{0,1},{1,0},{2,3},{3,2},{4,5},{5,4},{6,7},{7,6},{8,9},{9,8},{10,11... | collective-permute-start | bytes 147464 | tf_op jit(solution)/shard_map/ppermute | solution.py:527
  9.9 1.7 %collective-permute-start.6 = (f32[3,2,2,8,128]{4,3,2,1,0:T(8,128)S(1)}, f32[3,2,2,8,128]{4,3,2,1,0:T(8,128)S(1)}, u32[]{:S(2)}, u32[]{:S(2)}) collective-permute-start(f32[3,2,2,8,128]{4,3,2,1,0:T(8,128)S(1)} %collective-permute-done.3.refs_8_), channel_id=1, source_target_pairs={{0,1},{1,0},{2,3},{3,2},{4,5},{5,4},{6,7},{7,6},{8,9},{9,8},{10,11... | collective-permute-start | bytes 147464 | tf_op jit(solution)/shard_map/ppermute | solution.py:526

commit v5 on v4

--- a/solution.py
+++ b/solution.py
@@ -18,7 +18,7 @@
 FIELDS = 3
 AXES = ("slab", "bal")
 CHUNK_FIRST = 4
-SHIFTED_EARLY = 1
+SHIFTED_EARLY = 2
 CHUNK_SECOND = 28
 VMEM_BYTES = 40 * 2**20
 
@@ -27,12 +27,6 @@
     blocks, side, cells = block.shape
     split = block.reshape(blocks, side // ROWS, ROWS, cells // LANES, LANES)
     return split.transpose(0, 1, 3, 2, 4).reshape(blocks, side * cells // LANES, LANES)
-
-
-def tile_grid(block):
-    blocks, side, cells = block.shape
-    split = block.reshape(blocks, side // ROWS, ROWS, cells // LANES, LANES)
-    return split.transpose(0, 1, 3, 2, 4)
 
 
 def block_of(tiles, side):
@@ -138,100 +132,57 @@
     return found
 
 
-def pack_kernel(side, *refs):
-    grids, (even_ref, odd_ref, sem) = refs[:FIELDS], refs[FIELDS:]
-
-    def faces(upper_ref, lower_ref):
-        return [
-            pltpu.make_async_copy(grids[f].at[:, row // ROWS, :, row % ROWS, :], ref.at[f, :, d], sem.at[f, end, d])
-            for f in range(FIELDS)
-            for d in range(EDGE)
-            for end, ref, row in ((0, lower_ref, d), (1, upper_ref, side - 1 - d))
-        ]
-
-    is_even = lax.rem(lax.axis_index("slab"), 2) == 0
-
-    @pl.when(is_even)
-    def _():
-        for copy in faces(even_ref, odd_ref):
-            copy.start()
-
-    @pl.when(jnp.logical_not(is_even))
-    def _():
-        for copy in faces(odd_ref, even_ref):
-            copy.start()
-
-    for copy in faces(even_ref, odd_ref):
-        copy.wait()
-
-
-def spread(geometry, planes, slots, own, others, raw, ups, downs):
-    blocks = own.shape[1]
-    for x in planes:
-        for f in range(FIELDS):
-            for k in slots:
-                source = own.at[f] if k < blocks else others[f]
-                plane = source[k % blocks, plane_rows(x)]
-                raw[f, k, x] = plane
-                ups[f, k, x] = geometry.up(plane)
-                downs[f, k, x] = geometry.down(plane)
-
-
-def early_kernel(side, blocks, cores, *refs):
-    fields, others = refs[:FIELDS], refs[FIELDS : 2 * FIELDS]
-    raw, ups, downs, own, own_sem = refs[2 * FIELDS :]
-
-    @pl.when(lax.axis_index("slab") == 0)
-    def _():
-        own_copies = [pltpu.make_async_copy(fields[f], own.at[f], own_sem.at[f]) for f in range(FIELDS)]
-        for copy in own_copies:
-            copy.start()
-        geometry = Geometry(side)
-        spread(geometry, range(side), range(blocks, blocks * cores), own, others, raw, ups, downs)
-        for copy in own_copies:
-            copy.wait()
-        spread(geometry, range(side), range(blocks), own, others, raw, ups, downs)
-
-
-def first_kernel(side, blocks, cores, layers, *refs):
-    fields, others, tables = refs[:FIELDS], refs[FIELDS : 2 * FIELDS], refs[2 * FIELDS : 2 * FIELDS + 3]
-    outs, scratch = refs[2 * FIELDS + 6 : 2 * FIELDS + 15], refs[2 * FIELDS + 15 :]
-    raw, ups, downs, stepped, next_ups, next_downs, face_around, places_out, rates_out = outs
-    own, around, before, after, flags, own_sem, table_sem = scratch
+def pack_kernel(side, blocks, cores, layers, *refs):
+    fields, tables = refs[:FIELDS], refs[FIELDS : FIELDS + 3]
+    even_ref, odd_ref, own, places_out, rates_out = refs[FIELDS + 3 : FIELDS + 8]
+    before, after, flags, own_sem, table_sem = refs[FIELDS + 8 :]
     ring = blocks * cores
     layer, core = lax.axis_index("slab"), lax.axis_index("bal")
-    is_spread = layer == 0
     own_copies = [pltpu.make_async_copy(fields[f], own.at[f], own_sem.at[f]) for f in range(FIELDS)]
-
-    @pl.when(jnp.logical_not(is_spread))
-    def _():
-        for copy in own_copies:
-            copy.start()
-
-    table_copies = start_tables(tables, (before, after, flags), table_sem)
-    geometry = Geometry(side)
-
-    @pl.when(jnp.logical_not(is_spread))
-    def _():
-        spread(geometry, range(side), range(blocks, ring), own, others, raw, ups, downs)
-        for copy in own_copies:
-            copy.wait()
-        spread(geometry, range(CHUNK_FIRST), range(blocks), own, others, raw, ups, downs)
-
-    for copy in table_copies:
+    for copy in own_copies:
+        copy.start()
+    copies = start_tables(tables, (before, after, flags), table_sem)
+    for copy in copies:
         copy.wait()
     beside = [jnp.clip(layer + 2 * end - 1, 0, layers - 1) for end in range(2)]
-    places = holders(before, layer, core, blocks, cores)
-    listed = places + [after[core * blocks + b, layer] for b in range(blocks)]
+    listed = holders(before, layer, core, blocks, cores)
+    listed += [after[core * blocks + b, layer] for b in range(blocks)]
     for table in beside:
         for c in range(cores):
-            slot = jnp.where(c == 0, core, cores - 1 - core) * blocks
+            slot = jnp.where(c == 0, cores - 1 - core, core) * blocks
             listed += [before[slot + b, table] for b in range(blocks)]
     for k, place in enumerate(listed):
         places_out[k] = jnp.full((ROWS, LANES), place, jnp.int32)
     rates = [rate_of(flags[p, table]) for table in [layer] + beside for p in range(ring)]
     for k, rate in enumerate(rates):
         rates_out[k] = jnp.full((ROWS, LANES), rate, jnp.float32)
+    is_even = lax.rem(layer, 2) == 0
+    for f in range(FIELDS):
+        own_copies[f].wait()
+        for b in range(blocks):
+            for d in range(EDGE):
+                lower, upper = own[f, b, plane_rows(d)], own[f, b, plane_rows(side - 1 - d)]
+                even_ref[f, b, d] = jnp.where(is_even, upper, lower)
+                odd_ref[f, b, d] = jnp.where(is_even, lower, upper)
+
+
+def first_kernel(side, blocks, cores, *refs):
+    own, other, places_ref, rates_ref = refs[:4]
+    raw, stepped, next_ups, next_downs, face_around, ups, downs, around = refs[4:]
+    ring = blocks * cores
+    geometry = Geometry(side)
+    places = [place_at(places_ref, p) for p in range(ring)]
+    rates = [rates_ref[p] for p in range(ring)]
+
+    def spread(planes):
+        for x in planes:
+            for f in range(FIELDS):
+                for k in range(ring):
+                    source = own if k < blocks else other
+                    plane = source[f, k % blocks, plane_rows(x)]
+                    raw[f, k, x] = plane
+                    ups[f, k, x] = geometry.up(plane)
+                    downs[f, k, x] = geometry.down(plane)
 
     def gather(planes):
         for x in planes:
@@ -261,18 +212,14 @@
                         next_ups[f, p, x] = geometry.up(new[f])
                         next_downs[f, p, x] = geometry.down(new[f])
 
-    def steps(spread_too):
-        count = side // CHUNK_FIRST
-        for c in range(count):
-            planes = range(c * CHUNK_FIRST, (c + 1) * CHUNK_FIRST)
-            gather(planes)
-            if spread_too and c + 1 < count:
-                ahead = [x + CHUNK_FIRST for x in planes]
-                spread(geometry, ahead, range(blocks), own, others, raw, ups, downs)
-            calculate([x for x in planes if 0 < x < side - 1])
-
-    pl.when(is_spread)(lambda: steps(False))
-    pl.when(jnp.logical_not(is_spread))(lambda: steps(True))
+    count = side // CHUNK_FIRST
+    spread(range(CHUNK_FIRST))
+    for c in range(count):
+        planes = range(c * CHUNK_FIRST, (c + 1) * CHUNK_FIRST)
+        gather(planes)
+        if c + 1 < count:
+            spread([x + CHUNK_FIRST for x in planes])
+        calculate([x for x in planes if 0 < x < side - 1])
 
 
 def place_at(ref, k):
@@ -332,9 +279,9 @@
 
 def rim_kernel(side, blocks, cores, layers, *refs):
     raw, inner, result, face_around, rim_around, places_ref, rates_ref = refs[:7]
-    messages = refs[7:11]
-    outs = refs[11 : 11 + FIELDS]
-    halo, faces, shifted, around, tiles, sem, middle_sem = refs[11 + FIELDS :]
+    messages = refs[7:9]
+    outs = refs[9 : 9 + FIELDS]
+    halo, faces, shifted, around, tiles, sem, middle_sem = refs[9 + FIELDS :]
     ring = blocks * cores
     layer = lax.axis_index("slab")
     parity = lax.rem(layer, 2)
@@ -357,15 +304,13 @@
         return planes_at(raw, places[p], d if end == 0 else side - 1 - d)
 
     for end in ends:
-        from_even = parity == 1 - end
+        message = jnp.where(parity == 1 - end, 0, 1)
         for c in range(cores):
             for b in range(blocks):
                 p = place_at(places_ref, ring + blocks + (end * cores + c) * blocks + b)
                 for f in range(FIELDS):
                     for d in range(EDGE):
-                        halo[end, f, p, d] = jnp.where(
-                            from_even, messages[2 * c][f, b, d], messages[2 * c + 1][f, b, d]
-                        )
+                        halo[end, f, p, d] = messages[c][message, f, b, d]
     for f in range(FIELDS):
         for end in ends:
             tiles[f, end] = result[f, :, pl.ds(end * (side * ROWS - rows), rows)]
@@ -459,7 +404,7 @@
         for core in range(cores):
             here = layer * cores + core
             if 0 <= partner < layers:
-                pairs.append((here, partner * cores + core))
+                pairs.append((here, partner * cores + cores - 1 - core))
             else:
                 pairs.append((here, layer * cores + cores - 1 - core))
     return pairs
@@ -473,58 +418,43 @@
     before, after, flags = before.T, after.T, flags.T
     owners = [(s * cores + c, s * cores + cores - 1 - c) for s in range(layers) for c in range(cores)]
     fields = [tiles_of(a[0]) for a in (order_parameter, concentration_excess, thermal_subcooling)]
-    others = [lax.ppermute(a, AXES, owners) for a in fields]
     vmem, hbm = (pl.BlockSpec(memory_space=m) for m in (pltpu.VMEM, pltpu.HBM))
     params = pltpu.CompilerParams(vmem_limit_bytes=VMEM_BYTES)
     message = jax.ShapeDtypeStruct((FIELDS, blocks, EDGE, ROWS, LANES), f32)
     table = pltpu.SMEM(before.shape, jnp.int32)
     in_hbm = lambda *arrays: [pltpu.with_memory_space_constraint(a, pltpu.HBM) for a in arrays]
-    grids = [tile_grid(a[0]) for a in (order_parameter, concentration_excess, thermal_subcooling)]
-    even, odd = pl.pallas_call(
-        functools.partial(pack_kernel, side),
-        out_shape=(message, message),
-        in_specs=[hbm] * FIELDS,
-        out_specs=(vmem,) * 2,
-        scratch_shapes=[pltpu.SemaphoreType.DMA((FIELDS, 2, EDGE))],
+    numbers = (
+        jax.ShapeDtypeStruct((3 * ring + blocks, ROWS, LANES), jnp.int32),
+        jax.ShapeDtypeStruct((3 * ring, ROWS, LANES), f32),
+    )
+    even, odd, own, places, rates = pl.pallas_call(
+        functools.partial(pack_kernel, side, blocks, cores, layers),
+        out_shape=(message, message, jax.ShapeDtypeStruct((FIELDS, blocks, rows, LANES), f32)) + numbers,
+        in_specs=[hbm] * (FIELDS + 3),
+        out_specs=(vmem,) * 5,
+        scratch_shapes=[table] * 3
+        + [pltpu.SemaphoreType.DMA((FIELDS,)), pltpu.SemaphoreType.DMA((3,))],
         compiler_params=params,
         cost_estimate=pl.CostEstimate(flops=0, bytes_accessed=10**6, transcendentals=0),
-    )(*in_hbm(*grids))
+    )(*in_hbm(*fields, before, after, flags))
+    other = lax.ppermute(own, AXES, owners)
+    odd_in = lax.ppermute(odd, AXES, neighbour_swaps(layers, cores, 1))
+    even_in = lax.ppermute(even, AXES, neighbour_swaps(layers, cores, 0))
     planes = (FIELDS, ring, side, ROWS, LANES)
     kept = FIELDS + 2
-    three = (jax.ShapeDtypeStruct(planes, f32),) * 3
-    own_scratch = pltpu.VMEM((FIELDS, blocks, rows, LANES), f32)
-    odd_in = lax.ppermute(odd, AXES, neighbour_swaps(layers, cores, 1))
-    early = pl.pallas_call(
-        functools.partial(early_kernel, side, blocks, cores),
-        out_shape=three,
-        in_specs=[hbm] * FIELDS + [vmem] * FIELDS,
-        out_specs=(vmem,) * 3,
-        scratch_shapes=[own_scratch, pltpu.SemaphoreType.DMA((FIELDS,))],
-        compiler_params=params,
-        cost_estimate=pl.CostEstimate(flops=0, bytes_accessed=10**6, transcendentals=0),
-    )(*in_hbm(*fields), *others)
-    even, *early = lax.optimization_barrier((even, *early))
-    even_in = lax.ppermute(even, AXES, neighbour_swaps(layers, cores, 0))
-    raw, _, _, stepped, ups, downs, face_around, places, rates = pl.pallas_call(
-        functools.partial(first_kernel, side, blocks, cores, layers),
-        out_shape=three * 2
-        + (
-            jax.ShapeDtypeStruct((kept, ring, 2, ROWS, LANES), f32),
-            jax.ShapeDtypeStruct((3 * ring + blocks, ROWS, LANES), jnp.int32),
-            jax.ShapeDtypeStruct((3 * ring, ROWS, LANES), f32),
-        ),
-        in_specs=[hbm] * FIELDS + [vmem] * FIELDS + [hbm] * 3 + [vmem] * 3,
-        out_specs=(vmem,) * 9,
-        input_output_aliases={2 * FIELDS + 3 + k: k for k in range(3)},
-        scratch_shapes=[own_scratch, pltpu.VMEM((kept, ring, side, ROWS, LANES), f32)]
-        + [table] * 3
-        + [pltpu.SemaphoreType.DMA((FIELDS,)), pltpu.SemaphoreType.DMA((3,))],
+    raw, stepped, ups, downs, face_around = pl.pallas_call(
+        functools.partial(first_kernel, side, blocks, cores),
+        out_shape=(jax.ShapeDtypeStruct(planes, f32),) * 4
+        + (jax.ShapeDtypeStruct((kept, ring, 2, ROWS, LANES), f32),),
+        in_specs=[vmem] * 4,
+        out_specs=(vmem,) * 5,
+        scratch_shapes=[pltpu.VMEM(planes, f32)] * 2 + [pltpu.VMEM((kept, ring, side, ROWS, LANES), f32)],
         compiler_params=params,
         cost_estimate=pl.CostEstimate(flops=0, bytes_accessed=10**7, transcendentals=0),
-    )(*in_hbm(*fields), *others, *in_hbm(before, after, flags), *early)
+    )(own, other, places, rates)
     odd_in, even_in, stepped = lax.optimization_barrier((odd_in, even_in, stepped))
-    odd_other = lax.ppermute(odd_in, AXES, owners)
-    even_other = lax.ppermute(even_in, AXES, owners)
+    arrived = jnp.stack([even_in, odd_in])
+    passed_on = lax.ppermute(arrived, AXES, owners)
     result, rim_around = pl.pallas_call(
         functools.partial(second_kernel, side, blocks, cores),
         out_shape=(
@@ -543,7 +473,7 @@
     results = pl.pallas_call(
         functools.partial(rim_kernel, side, blocks, cores, layers),
         out_shape=(jax.ShapeDtypeStruct((blocks, rows, LANES), f32),) * FIELDS,
-        in_specs=[vmem] * 11,
+        in_specs=[vmem] * 9,
         out_specs=(hbm,) * FIELDS,
         scratch_shapes=[
             pltpu.VMEM((2, FIELDS, ring, EDGE, ROWS, LANES), f32),
@@ -556,7 +486,7 @@
         ],
         compiler_params=params,
         cost_estimate=pl.CostEstimate(flops=0, bytes_accessed=10**6, transcendentals=0),
-    )(raw, stepped, result, face_around, rim_around, places, rates, even_in, odd_in, even_other, odd_other)
+    )(raw, stepped, result, face_around, rim_around, places, rates, arrived, passed_on)
     return tuple(block_of(r, side)[None] for r in results)
 
 

time: 13 us -> 11.9 us (0.915)
  Pallas kernels: 7.73 us -> 6.21 us
  starting transfers between devices: 3.46 us -> 4.71 us
  waiting for transfers between devices: 0.9 us -> 0.12 us
    ppermute x1, starting transfers between devices: 1.78 us -> 3.7 us  [body(): even_in = lax.ppermute(even, AXES, neighbour_swaps(layers, cores, 0))]
    pallas_call x3 -> x2, Pallas kernels: 5.33 us -> 4.03 us  [the longest x1 2.86 us: body(): pl.pallas_call(functools.partial(first_kernel, side, blocks, cores), out_...]
    ppermute x5 -> x2, starting transfers between devices: 1.54 us -> 0.93 us  [the longest x1 0.52 us: body(): other = lax.ppermute(own, AXES, owners)]
    ppermute x5 -> x2, waiting for transfers between devices: 0.52 us -> 0.01 us  [the longest x1 0.01 us: body(): passed_on = lax.ppermute(arrived, AXES, owners)]
    ppermute x1, waiting for transfers between devices: 0.39 us -> 0.11 us  [body(): even_in = lax.ppermute(even, AXES, neighbour_swaps(layers, cores, 0))]
    pallas_call x1, Pallas kernels: 1.16 us -> 0.95 us  [body(): pl.pallas_call(functools.partial(second_kernel, side, blocks, cores), out...]
  transfers between devices with their start and end apart: 7 -> 4, of which waited for: 3 -> 1; matrix products, arithmetic and copies ran while one was open for 0% -> 0% of each run, Pallas kernels for 51% -> 33%
where the time goes in v5:
time: 11.9 us; the launch traced here: 11.7 us
  Pallas kernels  6.21 us (52%)
  starting transfers between devices  4.71 us (40%)
  between operations  0.66 us (6%)
  waiting for transfers between devices  0.12 us (1%)
    ppermute x1, starting transfers between devices, body(): even_in = lax.ppermute(even, AXES, neighbour_swaps(layers, cores, 0))  3.7 us
    pallas_call x1, Pallas kernels, body(): pl.pallas_call(functools.partial(first_kernel, side, blocks, cores), out_...  2.86 us
    pallas_call x1, Pallas kernels, body(): pl.pallas_call(functools.partial(rim_kernel, side, blocks, cores, layers)...  1.24 us
    pallas_call x1, Pallas kernels, body(): pl.pallas_call(functools.partial(pack_kernel, side, blocks, cores, layers...  1.17 us
    pallas_call x1, Pallas kernels, body(): pl.pallas_call(functools.partial(second_kernel, side, blocks, cores), out...  0.95 us
    ppermute x1, starting transfers between devices, body(): other = lax.ppermute(own, AXES, owners)  0.52 us
    ppermute x1, starting transfers between devices, body(): passed_on = lax.ppermute(arrived, AXES, owners)  0.41 us
  transfers between devices with their start and end apart: 4, of which 1 were waited for; matrix products, arithmetic and copies ran while one was open for 0% of the time, Pallas kernels for 33%

profile of v5, /device:TPU:0, one launch (start us, length us, event | category | flops | bytes accessed | tf_op | source)
XLA Modules:
  0.0 11.7 jit_solution(12937914608374388609)
XLA Ops:
  0.6 1.2 %shard_map.85 = (f32[3,2,2,8,128]{4,3,2,1,0:T(8,128)S(1)}, f32[3,2,2,8,128]{4,3,2,1,0:T(8,128)S(1)}, f32[3,2,256,128]{3,2,1,0:T(8,128)S(1)}, s32[14,8,128]{2,1,0:T(8,128)S(1)}, f32[12,8,128]{2,1,0:T(8,128)S(1)}) custom-call(f32[2,256,128]{2,1,0:T(8,128)} %bitcast.35, f32[2,256,128]{2,1,0:T(8,128)} %bitcast.36, f32[2,256,128]{2,1,0:T(8,128)} %bitcast.37, ...), custom_call_target="tpu_custom_call" | custom-call | bytes 1000000 | tf_op jit(solution)/shard_map/pallas_call | solution.py:430
  1.8 0.5 %collective-permute-start = (f32[3,2,256,128]{3,2,1,0:T(8,128)S(1)}, f32[3,2,256,128]{3,2,1,0:T(8,128)S(1)}, u32[]{:S(2)}, u32[]{:S(2)}) collective-permute-start(f32[3,2,256,128]{3,2,1,0:T(8,128)S(1)} %get-tuple-element.21.refs_0_), channel_id=1, source_target_pairs={{0,1},{1,0},{2,3},{3,2},{4,5},{5,4},{6,7},{7,6},{8,9},{9,8},{10,11... | collective-permute-start | bytes 2359304 | tf_op jit(solution)/shard_map/ppermute | solution.py:440
  2.3 0.1 collective-permute-start.1
  2.4 3.7 %collective-permute-start.2 = (f32[3,2,2,8,128]{4,3,2,1,0:T(8,128)S(1)}, f32[3,2,2,8,128]{4,3,2,1,0:T(8,128)S(1)}, u32[]{:S(2)}, u32[]{:S(2)}) collective-permute-start(f32[3,2,2,8,128]{4,3,2,1,0:T(8,128)S(1)} %get-tuple-element.26), channel_id=1, source_target_pairs={{0,3},{1,2},{2,1},{3,0},{4,7},{5,6},{6,5},{7,4},{8,11},{9,10},{10,... | collective-permute-start | bytes 147464 | tf_op jit(solution)/shard_map/ppermute | solution.py:442
  6.1 0.0 collective-permute-done.refs_1_
  6.1 2.9 %shard_map.86 = (f32[3,4,32,8,128]{4,3,2,1,0:T(8,128)S(1)}, f32[3,4,32,8,128]{4,3,2,1,0:T(8,128)S(1)}, f32[3,4,32,8,128]{4,3,2,1,0:T(8,128)S(1)}, f32[3,4,32,8,1...) custom-call(f32[3,2,256,128]{3,2,1,0:T(8,128)S(1)} %get-tuple-element.21.refs_0_, ...), custom_call_target="tpu_custom_call" | custom-call | bytes 10000000 | tf_op jit(solution)/shard_map/pallas_call | solution.py:445
  9.0 0.0 collective-permute-done.1
  9.0 0.1 collective-permute-done.2
  9.1 0.4 %collective-permute-start.3 = (f32[2,3,2,2,8,128]{5,4,3,2,1,0:T(8,128)S(1)}, f32[2,3,2,2,8,128]{5,4,3,2,1,0:T(8,128)S(1)}, u32[]{:S(2)}, u32[]{:S(2)}) collective-permute-start(f32[2,3,2,2,8,128]{5,4,3,2,1,0:T(8,128)S(1)} %pad_maximum_fusion.refs_7_), channel_id=1, source_target_pairs={{0,1},{1,0},{2,3},{3,2},{4,5},{5,4},{6,7},{7,6},{8,9},{9,8},{10,11... | collective-permute-start | bytes 294920 | tf_op jit(solution)/shard_map/ppermute | solution.py:457
  9.5 0.9 %shard_map.87 = (f32[3,2,256,128]{3,2,1,0:T(8,128)S(1)}, f32[5,2,2,8,128]{4,3,2,1,0:T(8,128)S(1)}) custom-call(f32[3,4,32,8,128]{4,3,2,1,0:T(8,128)S(1)} %get-tuple-element.28.refs_0_.refs_1_, f32[3,4,32,8,128]{4,3,2,1,0:T(8,128)S(1)} %get-tuple-element.29.refs_1_, f32[3,4,32,8,128]{4,3,2,1,0:T(8,128)S(1)} %get-tuple-element.30.refs_2_, ...), custom_call_target="tpu_custom_call" | custom-call | bytes 10000000 | tf_op jit(solution)/shard_map/pallas_call | solution.py:458
  10.5 0.0 collective-permute-done.3.refs_8_
  10.5 1.2 %shard_map.88 = (f32[2,256,128]{2,1,0:T(8,128)}, f32[2,256,128]{2,1,0:T(8,128)}, f32[2,256,128]{2,1,0:T(8,128)}) custom-call(f32[3,4,32,8,128]{4,3,2,1,0:T(8,128)S(1)} %get-tuple-element.24.refs_0_, f32[3,4,32,8,128]{4,3,2,1,0:T(8,128)S(1)} %get-tuple-element.28.refs_0_.refs_1_, f32[3,2,256,128]{3,2,1,0:T(8,128)S(1)} %get-tuple-element.31.refs_2_, ...), custom_call_target="tpu_custom_call" | custom-call | bytes 1000000 | tf_op jit(solution)/shard_map/pallas_call | solution.py:473
  (1 shorter events, 0.0 us)
Async XLA Ops:
  1.8 4.3 %collective-permute-start = (f32[3,2,256,128]{3,2,1,0:T(8,128)S(1)}, f32[3,2,256,128]{3,2,1,0:T(8,128)S(1)}, u32[]{:S(2)}, u32[]{:S(2)}) collective-permute-start(f32[3,2,256,128]{3,2,1,0:T(8,128)S(1)} %get-tuple-element.21.refs_0_), channel_id=1, source_target_pairs={{0,1},{1,0},{2,3},{3,2},{4,5},{5,4},{6,7},{7,6},{8,9},{9,8},{10,11... | collective-permute-start | bytes 2359304 | tf_op jit(solution)/shard_map/ppermute | solution.py:440
  2.3 6.6 %collective-permute-start.1 = (f32[3,2,2,8,128]{4,3,2,1,0:T(8,128)S(1)}, f32[3,2,2,8,128]{4,3,2,1,0:T(8,128)S(1)}, u32[]{:S(2)}, u32[]{:S(2)}) collective-permute-start(f32[3,2,2,8,128]{4,3,2,1,0:T(8,128)S(1)} %get-tuple-element.25), channel_id=1, source_target_pairs={{0,1},{1,0},{2,5},{3,4},{4,3},{5,2},{6,9},{7,8},{8,7},{9,6},{10,13... | collective-permute-start | bytes 147464 | tf_op jit(solution)/shard_map/ppermute | solution.py:441
  2.4 6.7 %collective-permute-start.2 = (f32[3,2,2,8,128]{4,3,2,1,0:T(8,128)S(1)}, f32[3,2,2,8,128]{4,3,2,1,0:T(8,128)S(1)}, u32[]{:S(2)}, u32[]{:S(2)}) collective-permute-start(f32[3,2,2,8,128]{4,3,2,1,0:T(8,128)S(1)} %get-tuple-element.26), channel_id=1, source_target_pairs={{0,3},{1,2},{2,1},{3,0},{4,7},{5,6},{6,5},{7,4},{8,11},{9,10},{10,... | collective-permute-start | bytes 147464 | tf_op jit(solution)/shard_map/ppermute | solution.py:442
  9.1 1.4 %collective-permute-start.3 = (f32[2,3,2,2,8,128]{5,4,3,2,1,0:T(8,128)S(1)}, f32[2,3,2,2,8,128]{5,4,3,2,1,0:T(8,128)S(1)}, u32[]{:S(2)}, u32[]{:S(2)}) collective-permute-start(f32[2,3,2,2,8,128]{5,4,3,2,1,0:T(8,128)S(1)} %pad_maximum_fusion.refs_7_), channel_id=1, source_target_pairs={{0,1},{1,0},{2,3},{3,2},{4,5},{5,4},{6,7},{7,6},{8,9},{9,8},{10,11... | collective-permute-start | bytes 294920 | tf_op jit(solution)/shard_map/ppermute | solution.py:457

commit v6 on v5

--- a/solution.py
+++ b/solution.py
@@ -18,6 +18,7 @@
 FIELDS = 3
 AXES = ("slab", "bal")
 CHUNK_FIRST = 4
+CROSSED = (1, 0)
 SHIFTED_EARLY = 2
 CHUNK_SECOND = 28
 VMEM_BYTES = 40 * 2**20
@@ -147,9 +148,11 @@
     beside = [jnp.clip(layer + 2 * end - 1, 0, layers - 1) for end in range(2)]
     listed = holders(before, layer, core, blocks, cores)
     listed += [after[core * blocks + b, layer] for b in range(blocks)]
-    for table in beside:
+    for end, table in enumerate(beside):
+        crossed = jnp.where(lax.rem(layer, 2) == 1 - end, *CROSSED)
+        sender = jnp.where(crossed == 1, cores - 1 - core, core)
         for c in range(cores):
-            slot = jnp.where(c == 0, cores - 1 - core, core) * blocks
+            slot = (sender if c == 0 else cores - 1 - sender) * blocks
             listed += [before[slot + b, table] for b in range(blocks)]
     for k, place in enumerate(listed):
         places_out[k] = jnp.full((ROWS, LANES), place, jnp.int32)
@@ -166,23 +169,30 @@
                 odd_ref[f, b, d] = jnp.where(is_even, lower, upper)
 
 
+def spread(geometry, planes, sources, raw, ups, downs):
+    for x in planes:
+        for f in range(FIELDS):
+            for place, source in sources.items():
+                for b in range(source.shape[1]):
+                    plane = source[f, b, plane_rows(x)]
+                    raw[f, place + b, x] = plane
+                    ups[f, place + b, x] = geometry.up(plane)
+                    downs[f, place + b, x] = geometry.down(plane)
+
+
+def early_kernel(side, own, raw, ups, downs):
+    @pl.when(lax.axis_index("slab") == 0)
+    def _():
+        spread(Geometry(side), range(side), {0: own}, raw, ups, downs)
+
+
 def first_kernel(side, blocks, cores, *refs):
     own, other, places_ref, rates_ref = refs[:4]
-    raw, stepped, next_ups, next_downs, face_around, ups, downs, around = refs[4:]
+    raw, ups, downs, stepped, next_ups, next_downs, face_around, around = refs[7:]
     ring = blocks * cores
     geometry = Geometry(side)
     places = [place_at(places_ref, p) for p in range(ring)]
     rates = [rates_ref[p] for p in range(ring)]
-
-    def spread(planes):
-        for x in planes:
-            for f in range(FIELDS):
-                for k in range(ring):
-                    source = own if k < blocks else other
-                    plane = source[f, k % blocks, plane_rows(x)]
-                    raw[f, k, x] = plane
-                    ups[f, k, x] = geometry.up(plane)
-                    downs[f, k, x] = geometry.down(plane)
 
     def gather(planes):
         for x in planes:
@@ -212,14 +222,19 @@
                         next_ups[f, p, x] = geometry.up(new[f])
                         next_downs[f, p, x] = geometry.down(new[f])
 
-    count = side // CHUNK_FIRST
-    spread(range(CHUNK_FIRST))
-    for c in range(count):
-        planes = range(c * CHUNK_FIRST, (c + 1) * CHUNK_FIRST)
-        gather(planes)
-        if c + 1 < count:
-            spread([x + CHUNK_FIRST for x in planes])
-        calculate([x for x in planes if 0 < x < side - 1])
+    def steps(sources):
+        count = side // CHUNK_FIRST
+        spread(geometry, range(CHUNK_FIRST), sources, raw, ups, downs)
+        for c in range(count):
+            planes = range(c * CHUNK_FIRST, (c + 1) * CHUNK_FIRST)
+            gather(planes)
+            if c + 1 < count:
+                spread(geometry, [x + CHUNK_FIRST for x in planes], sources, raw, ups, downs)
+            calculate([x for x in planes if 0 < x < side - 1])
+
+    is_early = lax.axis_index("slab") == 0
+    pl.when(is_early)(lambda: steps({blocks: other}))
+    pl.when(jnp.logical_not(is_early))(lambda: steps({0: own, blocks: other}))
 
 
 def place_at(ref, k):
@@ -404,7 +419,7 @@
         for core in range(cores):
             here = layer * cores + core
             if 0 <= partner < layers:
-                pairs.append((here, partner * cores + cores - 1 - core))
+                pairs.append((here, partner * cores + (cores - 1 - core if CROSSED[first] else core)))
             else:
                 pairs.append((here, layer * cores + cores - 1 - core))
     return pairs
@@ -439,19 +454,29 @@
     )(*in_hbm(*fields, before, after, flags))
     other = lax.ppermute(own, AXES, owners)
     odd_in = lax.ppermute(odd, AXES, neighbour_swaps(layers, cores, 1))
-    even_in = lax.ppermute(even, AXES, neighbour_swaps(layers, cores, 0))
     planes = (FIELDS, ring, side, ROWS, LANES)
     kept = FIELDS + 2
-    raw, stepped, ups, downs, face_around = pl.pallas_call(
+    three = (jax.ShapeDtypeStruct(planes, f32),) * 3
+    early = pl.pallas_call(
+        functools.partial(early_kernel, side),
+        out_shape=three,
+        in_specs=[vmem],
+        out_specs=(vmem,) * 3,
+        compiler_params=params,
+        cost_estimate=pl.CostEstimate(flops=0, bytes_accessed=10**6, transcendentals=0),
+    )(own)
+    even, *early = lax.optimization_barrier((even, *early))
+    even_in = lax.ppermute(even, AXES, neighbour_swaps(layers, cores, 0))
+    raw, _, _, stepped, ups, downs, face_around = pl.pallas_call(
         functools.partial(first_kernel, side, blocks, cores),
-        out_shape=(jax.ShapeDtypeStruct(planes, f32),) * 4
-        + (jax.ShapeDtypeStruct((kept, ring, 2, ROWS, LANES), f32),),
-        in_specs=[vmem] * 4,
-        out_specs=(vmem,) * 5,
-        scratch_shapes=[pltpu.VMEM(planes, f32)] * 2 + [pltpu.VMEM((kept, ring, side, ROWS, LANES), f32)],
+        out_shape=three * 2 + (jax.ShapeDtypeStruct((kept, ring, 2, ROWS, LANES), f32),),
+        in_specs=[vmem] * 7,
+        out_specs=(vmem,) * 7,
+        input_output_aliases={4 + k: k for k in range(3)},
+        scratch_shapes=[pltpu.VMEM((kept, ring, side, ROWS, LANES), f32)],
         compiler_params=params,
         cost_estimate=pl.CostEstimate(flops=0, bytes_accessed=10**7, transcendentals=0),
-    )(own, other, places, rates)
+    )(own, other, places, rates, *early)
     odd_in, even_in, stepped = lax.optimization_barrier((odd_in, even_in, stepped))
     arrived = jnp.stack([even_in, odd_in])
     passed_on = lax.ppermute(arrived, AXES, owners)

time: 11.9 us -> 11.8 us (level)
  waiting for transfers between devices: 0.12 us -> 0.65 us
  starting transfers between devices: 4.71 us -> 4.21 us
    pallas_call x1, Pallas kernels: 2.86 us -> 2.3 us  [body(): pl.pallas_call(functools.partial(first_kernel, side, blocks, cores), out_...]
    pallas_call x0 -> x1, Pallas kernels: none -> 0.47 us  [body(): pl.pallas_call(functools.partial(early_kernel, side), out_shape=three, in...]
    ppermute x1, waiting for transfers between devices: 0.11 us -> 0.58 us  [body(): even_in = lax.ppermute(even, AXES, neighbour_swaps(layers, cores, 0))]
    ppermute x1, starting transfers between devices: 3.7 us -> 3.27 us  [body(): even_in = lax.ppermute(even, AXES, neighbour_swaps(layers, cores, 0))]
  transfers between devices with their start and end apart: 4 -> 4, of which waited for: 1 -> 2; matrix products, arithmetic and copies ran while one was open for 0% -> 0% of each run, Pallas kernels for 33% -> 32%
where the time goes in v6:
time: 11.8 us; the launch traced here: 11.7 us
  Pallas kernels  6.12 us (52%)
  starting transfers between devices  4.21 us (36%)
  between operations  0.67 us (6%)
  waiting for transfers between devices  0.65 us (6%)
    ppermute x1, starting transfers between devices, body(): even_in = lax.ppermute(even, AXES, neighbour_swaps(layers, cores, 0))  3.27 us
    pallas_call x1, Pallas kernels, body(): pl.pallas_call(functools.partial(first_kernel, side, blocks, cores), out_...  2.3 us
    pallas_call x1, Pallas kernels, body(): pl.pallas_call(functools.partial(rim_kernel, side, blocks, cores, layers)...  1.23 us
    pallas_call x1, Pallas kernels, body(): pl.pallas_call(functools.partial(pack_kernel, side, blocks, cores, layers...  1.17 us
    pallas_call x1, Pallas kernels, body(): pl.pallas_call(functools.partial(second_kernel, side, blocks, cores), out...  0.95 us
    ppermute x1, waiting for transfers between devices, body(): even_in = lax.ppermute(even, AXES, neighbour_swaps(layers, cores, 0))  0.58 us
    ppermute x1, starting transfers between devices, body(): other = lax.ppermute(own, AXES, owners)  0.52 us
    pallas_call x1, Pallas kernels, body(): pl.pallas_call(functools.partial(early_kernel, side), out_shape=three, in...  0.47 us
  transfers between devices with their start and end apart: 4, of which 2 were waited for; matrix products, arithmetic and copies ran while one was open for 0% of the time, Pallas kernels for 32%

profile of v6, /device:TPU:0, one launch (start us, length us, event | category | flops | bytes accessed | tf_op | source)
XLA Modules:
  0.0 11.7 jit_solution(14409247276585741419)
XLA Ops:
  0.6 1.2 %shard_map.85 = (f32[3,2,2,8,128]{4,3,2,1,0:T(8,128)S(1)}, f32[3,2,2,8,128]{4,3,2,1,0:T(8,128)S(1)}, f32[3,2,256,128]{3,2,1,0:T(8,128)S(1)}, s32[14,8,128]{2,1,0:T(8,128)S(1)}, f32[12,8,128]{2,1,0:T(8,128)S(1)}) custom-call(f32[2,256,128]{2,1,0:T(8,128)} %bitcast.35, f32[2,256,128]{2,1,0:T(8,128)} %bitcast.36, f32[2,256,128]{2,1,0:T(8,128)} %bitcast.37, ...), custom_call_target="tpu_custom_call" | custom-call | bytes 1000000 | tf_op jit(solution)/shard_map/pallas_call | solution.py:445
  1.8 0.5 %collective-permute-start = (f32[3,2,256,128]{3,2,1,0:T(8,128)S(1)}, f32[3,2,256,128]{3,2,1,0:T(8,128)S(1)}, u32[]{:S(2)}, u32[]{:S(2)}) collective-permute-start(f32[3,2,256,128]{3,2,1,0:T(8,128)S(1)} %get-tuple-element.28.own.refs_0_), channel_id=1, source_target_pairs={{0,1},{1,0},{2,3},{3,2},{4,5},{5,4},{6,7},{7,6},{8,9},{9,8},{10,11... | collective-permute-start | bytes 2359304 | tf_op jit(solution)/shard_map/ppermute | solution.py:455
  2.3 0.1 collective-permute-start.1
  2.4 0.5 %shard_map.86 = (f32[3,4,32,8,128]{4,3,2,1,0:T(8,128)S(1)}, f32[3,4,32,8,128]{4,3,2,1,0:T(8,128)S(1)}, f32[3,4,32,8,128]{4,3,2,1,0:T(8,128)S(1)}) custom-call(f32[3,2,256,128]{3,2,1,0:T(8,128)S(1)} %get-tuple-element.28.own.refs_0_), custom_call_target="tpu_custom_call" | custom-call | bytes 1000000 | tf_op jit(solution)/shard_map/pallas_call | solution.py:460
  2.9 3.3 %collective-permute-start.2 = (f32[3,2,2,8,128]{4,3,2,1,0:T(8,128)S(1)}, f32[3,2,2,8,128]{4,3,2,1,0:T(8,128)S(1)}, u32[]{:S(2)}, u32[]{:S(2)}) collective-permute-start(f32[3,2,2,8,128]{4,3,2,1,0:T(8,128)S(1)} %get-tuple-element.40), channel_id=1, source_target_pairs={{0,3},{1,2},{2,1},{3,0},{4,7},{5,6},{6,5},{7,4},{8,11},{9,10},{10,... | collective-permute-start | bytes 147464 | tf_op jit(solution)/shard_map/ppermute | solution.py:469
  6.2 0.0 collective-permute-done.refs_1_
  6.2 2.3 %shard_map.87 = (f32[3,4,32,8,128]{4,3,2,1,0:T(8,128)S(1)}, f32[3,4,32,8,128]{4,3,2,1,0:T(8,128)S(1)}, f32[3,4,32,8,128]{4,3,2,1,0:T(8,128)S(1)}, f32[3,4,32,8,1...) custom-call(f32[3,2,256,128]{3,2,1,0:T(8,128)S(1)} %get-tuple-elemen, ...), custom_call_target="tpu_custom_call", output_to_operand_aliasing={{0}: (4, {}), {1}: (5, {}), {2}: (6, {})} | custom-call | bytes 10000000 | tf_op jit(solution)/shard_map/pallas_call | solution.py:470
  8.5 0.0 collective-permute-done.1
  8.5 0.6 %collective-permute-done.2 = f32[3,2,2,8,128]{4,3,2,1,0:T(8,128)S(1)} collective-permute-done((f32[3,2,2,8,128]{4,3,2,1,0:T(8,128)S(1)}, f32[3,2,2,8,128]{4,3,2,1,0:T(8,128)S(1)}, u32[]{:S(2)}, u32[]{:S(2)}) %collective-permute-start.2) | collective-permute-done | bytes 49184 | tf_op jit(solution)/shard_map/ppermute | solution.py:469
  9.1 0.3 %collective-permute-start.3 = (f32[2,3,2,2,8,128]{5,4,3,2,1,0:T(8,128)S(1)}, f32[2,3,2,2,8,128]{5,4,3,2,1,0:T(8,128)S(1)}, u32[]{:S(2)}, u32[]{:S(2)}) collective-permute-start(f32[2,3,2,2,8,128]{5,4,3,2,1,0:T(8,128)S(1)} %pad_maximum_fusion.refs_7_), channel_id=1, source_target_pairs={{0,1},{1,0},{2,3},{3,2},{4,5},{5,4},{6,7},{7,6},{8,9},{9,8},{10,11... | collective-permute-start | bytes 294920 | tf_op jit(solution)/shard_map/ppermute | solution.py:482
  9.4 1.0 %shard_map.88 = (f32[3,2,256,128]{3,2,1,0:T(8,128)S(1)}, f32[5,2,2,8,128]{4,3,2,1,0:T(8,128)S(1)}) custom-call(f32[3,4,32,8,128]{4,3,2,1,0:T(8,128)S(1)} %get-tuple-element.42.refs_0_.refs_1_, f32[3,4,32,8,128]{4,3,2,1,0:T(8,128)S(1)} %get-tuple-element.43.refs_1_, f32[3,4,32,8,128]{4,3,2,1,0:T(8,128)S(1)} %get-tuple-element.44.refs_2_, ...), custom_call_target="tpu_custom_call" | custom-call | bytes 10000000 | tf_op jit(solution)/shard_map/pallas_call | solution.py:483
  10.4 0.1 collective-permute-done.3.refs_8_
  10.4 1.2 %shard_map.89 = (f32[2,256,128]{2,1,0:T(8,128)}, f32[2,256,128]{2,1,0:T(8,128)}, f32[2,256,128]{2,1,0:T(8,128)}) custom-call(f32[3,4,32,8,128]{4,3,2,1,0:T(8,128)S(1)} %get-tuple-element.38.refs_0_, f32[3,4,32,8,128]{4,3,2,1,0:T(8,128)S(1)} %get-tuple-element.42.refs_0_.refs_1_, f32[3,2,256,128]{3,2,1,0:T(8,128)S(1)} %get-tuple-element.45.refs_2_, ...), custom_call_target="tpu_custom_call" | custom-call | bytes 1000000 | tf_op jit(solution)/shard_map/pallas_call | solution.py:498
  (1 shorter events, 0.0 us)
Async XLA Ops:
  1.8 4.3 %collective-permute-start = (f32[3,2,256,128]{3,2,1,0:T(8,128)S(1)}, f32[3,2,256,128]{3,2,1,0:T(8,128)S(1)}, u32[]{:S(2)}, u32[]{:S(2)}) collective-permute-start(f32[3,2,256,128]{3,2,1,0:T(8,128)S(1)} %get-tuple-element.28.own.refs_0_), channel_id=1, source_target_pairs={{0,1},{1,0},{2,3},{3,2},{4,5},{5,4},{6,7},{7,6},{8,9},{9,8},{10,11... | collective-permute-start | bytes 2359304 | tf_op jit(solution)/shard_map/ppermute | solution.py:455
  2.3 6.1 %collective-permute-start.1 = (f32[3,2,2,8,128]{4,3,2,1,0:T(8,128)S(1)}, f32[3,2,2,8,128]{4,3,2,1,0:T(8,128)S(1)}, u32[]{:S(2)}, u32[]{:S(2)}) collective-permute-start(f32[3,2,2,8,128]{4,3,2,1,0:T(8,128)S(1)} %get-tuple-element.39), channel_id=1, source_target_pairs={{0,1},{1,0},{2,4},{3,5},{4,2},{5,3},{6,8},{7,9},{8,6},{9,7},{10,12... | collective-permute-start | bytes 147464 | tf_op jit(solution)/shard_map/ppermute | solution.py:456
  2.9 6.2 %collective-permute-start.2 = (f32[3,2,2,8,128]{4,3,2,1,0:T(8,128)S(1)}, f32[3,2,2,8,128]{4,3,2,1,0:T(8,128)S(1)}, u32[]{:S(2)}, u32[]{:S(2)}) collective-permute-start(f32[3,2,2,8,128]{4,3,2,1,0:T(8,128)S(1)} %get-tuple-element.40), channel_id=1, source_target_pairs={{0,3},{1,2},{2,1},{3,0},{4,7},{5,6},{6,5},{7,4},{8,11},{9,10},{10,... | collective-permute-start | bytes 147464 | tf_op jit(solution)/shard_map/ppermute | solution.py:469
  9.1 1.4 %collective-permute-start.3 = (f32[2,3,2,2,8,128]{5,4,3,2,1,0:T(8,128)S(1)}, f32[2,3,2,2,8,128]{5,4,3,2,1,0:T(8,128)S(1)}, u32[]{:S(2)}, u32[]{:S(2)}) collective-permute-start(f32[2,3,2,2,8,128]{5,4,3,2,1,0:T(8,128)S(1)} %pad_maximum_fusion.refs_7_), channel_id=1, source_target_pairs={{0,1},{1,0},{2,3},{3,2},{4,5},{5,4},{6,7},{7,6},{8,9},{9,8},{10,11... | collective-permute-start | bytes 294920 | tf_op jit(solution)/shard_map/ppermute | solution.py:482

commit v7 on v6

--- a/solution.py
+++ b/solution.py
@@ -19,7 +19,7 @@
 AXES = ("slab", "bal")
 CHUNK_FIRST = 4
 CROSSED = (1, 0)
-SHIFTED_EARLY = 2
+SHIFTED_EARLY = 3
 CHUNK_SECOND = 28
 VMEM_BYTES = 40 * 2**20
 
@@ -241,8 +241,9 @@
     return ref[k][0, 0]
 
 
-def second_kernel(side, blocks, cores, *refs):
-    stepped, ups, downs, places_ref, rates_ref, result, rim_around, shifted, around = refs
+def second_kernel(side, blocks, cores, layers, *refs):
+    stepped, ups, downs, places_ref, rates_ref, raw, face_around = refs[:7]
+    result, rim_around, shifted, around, faces = refs[7:]
     ring = blocks * cores
     geometry = Geometry(side)
     places = [place_at(places_ref, ring + b) for b in range(blocks)]
@@ -290,6 +291,51 @@
         shift(1 + end * (side - 3))
     for end in range(2):
         gather(1 + end * (side - 3), rim_around, end)
+
+
+    layer = lax.axis_index("slab")
+
+    def close(end):
+        x = [d if end == 0 else side - 1 - d for d in range(3)]
+        for p in range(ring):
+            place = place_at(places_ref, p)
+            near = planes_at(raw, place, x[0])
+            new = finish(
+                near, near, planes_at(raw, place, x[1]), [face_around[k, p, end] for k in range(FIELDS + 2)], rates_ref[p]
+            )
+            for f in range(FIELDS):
+                faces[f, p] = new[f]
+        for b, (p, following, previous) in enumerate(rounds):
+            for f in range(FIELDS):
+                shifted[0, f, b, x[0]] = geometry.up(faces[f, p])
+                shifted[1, f, b, x[0]] = geometry.down(faces[f, p])
+                shifted[2, f, b, x[0]] = geometry.down(faces[f, following])
+                shifted[3, f, b, x[0]] = geometry.up(faces[f, previous])
+        for b, p in enumerate(places):
+            keep_sides(
+                geometry,
+                around,
+                b,
+                x[0],
+                lambda f: faces[f, p],
+                lambda f: shifted[0, f, b, x[0]],
+                lambda f: shifted[1, f, b, x[0]],
+                lambda f: shifted[2, f, b, x[0]],
+                lambda f: shifted[3, f, b, x[0]],
+            )
+        for b, p in enumerate(places):
+            face = [faces[f, p] for f in range(FIELDS)]
+            first, second = planes_at(stepped, p, x[1]), planes_at(stepped, p, x[2])
+            news = (
+                finish(face, face, first, [around[k, b, x[0]] for k in range(FIELDS + 2)], rates[b]),
+                finish(face, first, second, [rim_around[k, b, end] for k in range(FIELDS + 2)], rates[b]),
+            )
+            for d in range(EDGE):
+                for f in range(FIELDS):
+                    result[f, b, plane_rows(x[d])] = news[d][f]
+
+    pl.when(layer == 0)(lambda: close(0))
+    pl.when(layer == layers - 1)(lambda: close(1))
 
 
 def rim_kernel(side, blocks, cores, layers, *refs):
@@ -311,103 +357,121 @@
         copy.start()
     places = [place_at(places_ref, p) for p in range(ring)]
     targets = [place_at(places_ref, ring + b) for b in range(blocks)]
-    beside = [layer + 2 * end - 1 for end in range(2)]
-    outside = [jnp.logical_or(b < 0, b >= layers) for b in beside]
-    ends = range(2)
-
-    def at_face(end, p, d):
-        return planes_at(raw, places[p], d if end == 0 else side - 1 - d)
-
-    for end in ends:
-        message = jnp.where(parity == 1 - end, 0, 1)
-        for c in range(cores):
-            for b in range(blocks):
-                p = place_at(places_ref, ring + blocks + (end * cores + c) * blocks + b)
-                for f in range(FIELDS):
-                    for d in range(EDGE):
-                        halo[end, f, p, d] = messages[c][message, f, b, d]
-    for f in range(FIELDS):
-        for end in ends:
-            tiles[f, end] = result[f, :, pl.ds(end * (side * ROWS - rows), rows)]
-    for end in ends:
-        for p in range(ring):
+    rounds = [(p, (p + 1) & (ring - 1), (p + ring - 1) & (ring - 1)) for p in targets]
+
+    def end_rows(end):
+        return pl.ds(end * (side * ROWS - rows) if isinstance(end, int) else pl.multiple_of(end * (side * ROWS - rows), rows), rows)
+
+
+    def rim(ends, done):
+        out_copies = [pltpu.make_async_copy(result.at[f, :, end_rows(end)], outs[f].at[:, end_rows(end)], sem.at[f, end]) for end in done for f in range(FIELDS)]
+        for copy in out_copies:
+            copy.start()
+
+        def outside(end):
+            beside = layer + 2 * end - 1
+            return jnp.logical_or(beside < 0, beside >= layers)
+
+        def at_face(end, p, d):
+            return planes_at(raw, places[p], d + end * (side - 1 - 2 * d))
+
+        for end in ends:
+            message = jnp.where(parity == 1 - end, 0, 1)
+            for c in range(cores):
+                for b in range(blocks):
+                    p = place_at(places_ref, ring + blocks + (end * cores + c) * blocks + b)
+                    for f in range(FIELDS):
+                        for d in range(EDGE):
+                            halo[end, f, p, d] = messages[c][message, f, b, d]
+        for f in range(FIELDS):
+            for end in ends:
+                tiles[f, end] = result[f, :, end_rows(end)]
+        for end in ends:
+            for p in range(ring):
+                for f in range(FIELDS):
+                    near = jnp.where(outside(end), at_face(end, p, 0)[f], halo[end, f, p, 0])
+                    halo[end, f, p, 0] = near
+                    shifted[0, end, f, p] = geometry.up(near)
+                    shifted[1, end, f, p] = geometry.down(near)
+        for end in ends:
+            for p in range(ring):
+                new = finish(
+                    [halo[end, f, p, 0] for f in range(FIELDS)],
+                    at_face(end, p, 0),
+                    at_face(end, p, 1),
+                    [face_around[k, p, end] for k in range(FIELDS + 2)],
+                    rates_ref[p],
+                )
+                for f in range(FIELDS):
+                    faces[end, f, p, 1] = new[f]
+        for end in ends:
+            for p in range(ring):
+                keep_sides(
+                    geometry,
+                    around,
+                    p,
+                    end,
+                    lambda f: halo[end, f, p, 0],
+                    lambda f: shifted[0, end, f, p],
+                    lambda f: shifted[1, end, f, p],
+                    lambda f: shifted[1, end, f, (p + 1) % ring],
+                    lambda f: shifted[0, end, f, (p - 1) % ring],
+                )
+        for end in ends:
+            for b, (p, following, previous) in enumerate(rounds):
+                for f in range(FIELDS):
+                    shifted[2, end, f, 4 * b] = geometry.up(faces[end, f, p, 1])
+                    shifted[2, end, f, 4 * b + 1] = geometry.down(faces[end, f, p, 1])
+                    shifted[2, end, f, 4 * b + 2] = geometry.down(faces[end, f, following, 1])
+                    shifted[2, end, f, 4 * b + 3] = geometry.up(faces[end, f, previous, 1])
+        for end in ends:
+            for p in range(ring):
+                new = finish(
+                    [halo[end, f, p, 1] for f in range(FIELDS)],
+                    [halo[end, f, p, 0] for f in range(FIELDS)],
+                    at_face(end, p, 0),
+                    [around[k, p, end] for k in range(FIELDS + 2)],
+                    rates_ref[ring * (1 + end) + p],
+                )
+                for f in range(FIELDS):
+                    faces[end, f, p, 0] = jnp.where(outside(end), faces[end, f, p, 1], new[f])
+        for end in ends:
+            for b, (p, following, previous) in enumerate(rounds):
+                keep_sides(
+                    geometry,
+                    around,
+                    ring + b,
+                    end,
+                    lambda f: faces[end, f, p, 1],
+                    lambda f: shifted[2, end, f, 4 * b],
+                    lambda f: shifted[2, end, f, 4 * b + 1],
+                    lambda f: shifted[2, end, f, 4 * b + 2],
+                    lambda f: shifted[2, end, f, 4 * b + 3],
+                )
+        for end in ends:
+            for b, p in enumerate(targets):
+                outer, face = ([faces[end, f, p, d] for f in range(FIELDS)] for d in range(2))
+                first, second = (planes_at(inner, p, d + end * (side - 1 - 2 * d)) for d in (1, 2))
+                news = (
+                    finish(outer, face, first, [around[k, ring + b, end] for k in range(FIELDS + 2)], rates_ref[p]),
+                    finish(face, first, second, [rim_around[k, b, end] for k in range(FIELDS + 2)], rates_ref[p]),
+                )
+                for d in range(EDGE):
+                    row = d + end * (ROWS - 1 - 2 * d)
+                    for f in range(FIELDS):
+                        tiles[f, end, b, pl.ds(row, ROWS, stride=ROWS)] = news[d][f]
             for f in range(FIELDS):
-                near = jnp.where(outside[end], at_face(end, p, 0)[f], halo[end, f, p, 0])
-                halo[end, f, p, 0] = near
-                shifted[0, end, f, p] = geometry.up(near)
-                shifted[1, end, f, p] = geometry.down(near)
-    for end in ends:
-        for p in range(ring):
-            new = finish(
-                [halo[end, f, p, 0] for f in range(FIELDS)],
-                at_face(end, p, 0),
-                at_face(end, p, 1),
-                [face_around[k, p, end] for k in range(FIELDS + 2)],
-                rates_ref[p],
-            )
-            for f in range(FIELDS):
-                faces[end, f, p, 1] = new[f]
-    for end in ends:
-        for p in range(ring):
-            keep_sides(
-                geometry,
-                around,
-                p,
-                end,
-                lambda f: halo[end, f, p, 0],
-                lambda f: shifted[0, end, f, p],
-                lambda f: shifted[1, end, f, p],
-                lambda f: shifted[1, end, f, (p + 1) % ring],
-                lambda f: shifted[0, end, f, (p - 1) % ring],
-            )
-    rounds = [(p, (p + 1) & (ring - 1), (p + ring - 1) & (ring - 1)) for p in targets]
-    for end in ends:
-        for b, (p, following, previous) in enumerate(rounds):
-            for f in range(FIELDS):
-                shifted[2, end, f, 4 * b] = geometry.up(faces[end, f, p, 1])
-                shifted[2, end, f, 4 * b + 1] = geometry.down(faces[end, f, p, 1])
-                shifted[2, end, f, 4 * b + 2] = geometry.down(faces[end, f, following, 1])
-                shifted[2, end, f, 4 * b + 3] = geometry.up(faces[end, f, previous, 1])
-    for end in ends:
-        for p in range(ring):
-            new = finish(
-                [halo[end, f, p, 1] for f in range(FIELDS)],
-                [halo[end, f, p, 0] for f in range(FIELDS)],
-                at_face(end, p, 0),
-                [around[k, p, end] for k in range(FIELDS + 2)],
-                rates_ref[ring * (1 + end) + p],
-            )
-            for f in range(FIELDS):
-                faces[end, f, p, 0] = jnp.where(outside[end], faces[end, f, p, 1], new[f])
-    for end in ends:
-        for b, (p, following, previous) in enumerate(rounds):
-            keep_sides(
-                geometry,
-                around,
-                ring + b,
-                end,
-                lambda f: faces[end, f, p, 1],
-                lambda f: shifted[2, end, f, 4 * b],
-                lambda f: shifted[2, end, f, 4 * b + 1],
-                lambda f: shifted[2, end, f, 4 * b + 2],
-                lambda f: shifted[2, end, f, 4 * b + 3],
-            )
-    for end in ends:
-        for b, p in enumerate(targets):
-            outer, face = ([faces[end, f, p, d] for f in range(FIELDS)] for d in range(2))
-            first, second = (planes_at(inner, p, d if end == 0 else side - 1 - d) for d in (1, 2))
-            news = (
-                finish(outer, face, first, [around[k, ring + b, end] for k in range(FIELDS + 2)], rates_ref[p]),
-                finish(face, first, second, [rim_around[k, b, end] for k in range(FIELDS + 2)], rates_ref[p]),
-            )
-            for d in range(EDGE):
-                row = d if end == 0 else ROWS - 1 - d
-                for f in range(FIELDS):
-                    tiles[f, end, b, pl.ds(row, ROWS, stride=ROWS)] = news[d][f]
-        for f in range(FIELDS):
-            part = pl.ds(end * (side * ROWS - rows), rows)
-            copies.append(pltpu.make_async_copy(tiles.at[f, end], outs[f].at[:, part], sem.at[f, end]))
-            copies[-1].start()
+                part = end_rows(end)
+                out_copies.append(pltpu.make_async_copy(tiles.at[f, end], outs[f].at[:, part], sem.at[f, end]))
+                out_copies[-1].start()
+        for copy in out_copies:
+            copy.wait()
+
+    is_lowest, is_highest = layer == 0, layer == layers - 1
+    at_edge = jnp.logical_or(is_lowest, is_highest)
+    open_end = jnp.where(is_lowest, 1, 0)
+    pl.when(at_edge)(lambda: rim([open_end], [1 - open_end]))
+    pl.when(jnp.logical_not(at_edge))(lambda: rim([0, 1], []))
     for copy in copies:
         copy.wait()
 
@@ -481,20 +545,21 @@
     arrived = jnp.stack([even_in, odd_in])
     passed_on = lax.ppermute(arrived, AXES, owners)
     result, rim_around = pl.pallas_call(
-        functools.partial(second_kernel, side, blocks, cores),
+        functools.partial(second_kernel, side, blocks, cores, layers),
         out_shape=(
             jax.ShapeDtypeStruct((FIELDS, blocks, rows, LANES), f32),
             jax.ShapeDtypeStruct((kept, blocks, 2, ROWS, LANES), f32),
         ),
-        in_specs=[vmem] * 5,
+        in_specs=[vmem] * 7,
         out_specs=(vmem,) * 2,
         scratch_shapes=[
             pltpu.VMEM((4, FIELDS, blocks, side, ROWS, LANES), f32),
             pltpu.VMEM((kept, blocks, side, ROWS, LANES), f32),
+            pltpu.VMEM((FIELDS, ring, ROWS, LANES), f32),
         ],
         compiler_params=params,
         cost_estimate=pl.CostEstimate(flops=0, bytes_accessed=10**7, transcendentals=0),
-    )(stepped, ups, downs, places, rates)
+    )(stepped, ups, downs, places, rates, raw, face_around)
     results = pl.pallas_call(
         functools.partial(rim_kernel, side, blocks, cores, layers),
         out_shape=(jax.ShapeDtypeStruct((blocks, rows, LANES), f32),) * FIELDS,

time: 11.8 us -> 11.7 us (level)
  waiting for transfers between devices: 0.65 us -> 0.46 us
    ppermute x1, waiting for transfers between devices: 0.58 us -> 0.37 us  [body(): even_in = lax.ppermute(even, AXES, neighbour_swaps(layers, cores, 0))]
    pallas_call x1, Pallas kernels: 2.3 us -> 2.51 us  [body(): pl.pallas_call(functools.partial(first_kernel, side, blocks, cores), out_...]
  transfers between devices with their start and end apart: 4 -> 4, of which waited for: 2 -> 2; matrix products, arithmetic and copies ran while one was open for 0% -> 0% of each run, Pallas kernels for 32% -> 34%
where the time goes in v7:
time: 11.7 us; the launch traced here: 11.6 us
  Pallas kernels  6.21 us (53%)
  starting transfers between devices  4.21 us (36%)
  between operations  0.67 us (6%)
  waiting for transfers between devices  0.46 us (4%)
    ppermute x1, starting transfers between devices, body(): even_in = lax.ppermute(even, AXES, neighbour_swaps(layers, cores, 0))  3.27 us
    pallas_call x1, Pallas kernels, body(): pl.pallas_call(functools.partial(first_kernel, side, blocks, cores), out_...  2.51 us
    pallas_call x1, Pallas kernels, body(): pl.pallas_call(functools.partial(pack_kernel, side, blocks, cores, layers...  1.17 us
    pallas_call x1, Pallas kernels, body(): pl.pallas_call(functools.partial(rim_kernel, side, blocks, cores, layers)...  1.13 us
    pallas_call x1, Pallas kernels, body(): pl.pallas_call(functools.partial(second_kernel, side, blocks, cores, laye...  0.93 us
    ppermute x1, starting transfers between devices, body(): other = lax.ppermute(own, AXES, owners)  0.52 us
    pallas_call x1, Pallas kernels, body(): pl.pallas_call(functools.partial(early_kernel, side), out_shape=three, in...  0.47 us
    ppermute x1, waiting for transfers between devices, body(): even_in = lax.ppermute(even, AXES, neighbour_swaps(layers, cores, 0))  0.37 us
  transfers between devices with their start and end apart: 4, of which 2 were waited for; matrix products, arithmetic and copies ran while one was open for 0% of the time, Pallas kernels for 34%

profile of v7, /device:TPU:0, one launch (start us, length us, event | category | flops | bytes accessed | tf_op | source)
XLA Modules:
  0.0 11.6 jit_solution(13072251710030889239)
XLA Ops:
  0.6 1.2 %shard_map.85 = (f32[3,2,2,8,128]{4,3,2,1,0:T(8,128)S(1)}, f32[3,2,2,8,128]{4,3,2,1,0:T(8,128)S(1)}, f32[3,2,256,128]{3,2,1,0:T(8,128)S(1)}, s32[14,8,128]{2,1,0:T(8,128)S(1)}, f32[12,8,128]{2,1,0:T(8,128)S(1)}) custom-call(f32[2,256,128]{2,1,0:T(8,128)} %bitcast.35, f32[2,256,128]{2,1,0:T(8,128)} %bitcast.36, f32[2,256,128]{2,1,0:T(8,128)} %bitcast.37, ...), custom_call_target="tpu_custom_call" | custom-call | bytes 1000000 | tf_op jit(solution)/shard_map/pallas_call | solution.py:509
  1.8 0.5 %collective-permute-start = (f32[3,2,256,128]{3,2,1,0:T(8,128)S(1)}, f32[3,2,256,128]{3,2,1,0:T(8,128)S(1)}, u32[]{:S(2)}, u32[]{:S(2)}) collective-permute-start(f32[3,2,256,128]{3,2,1,0:T(8,128)S(1)} %get-tuple-element.28.own.refs_0_), channel_id=1, source_target_pairs={{0,1},{1,0},{2,3},{3,2},{4,5},{5,4},{6,7},{7,6},{8,9},{9,8},{10,11... | collective-permute-start | bytes 2359304 | tf_op jit(solution)/shard_map/ppermute | solution.py:519
  2.3 0.1 collective-permute-start.1
  2.4 0.5 %shard_map.86 = (f32[3,4,32,8,128]{4,3,2,1,0:T(8,128)S(1)}, f32[3,4,32,8,128]{4,3,2,1,0:T(8,128)S(1)}, f32[3,4,32,8,128]{4,3,2,1,0:T(8,128)S(1)}) custom-call(f32[3,2,256,128]{3,2,1,0:T(8,128)S(1)} %get-tuple-element.28.own.refs_0_), custom_call_target="tpu_custom_call" | custom-call | bytes 1000000 | tf_op jit(solution)/shard_map/pallas_call | solution.py:524
  2.9 3.3 %collective-permute-start.2 = (f32[3,2,2,8,128]{4,3,2,1,0:T(8,128)S(1)}, f32[3,2,2,8,128]{4,3,2,1,0:T(8,128)S(1)}, u32[]{:S(2)}, u32[]{:S(2)}) collective-permute-start(f32[3,2,2,8,128]{4,3,2,1,0:T(8,128)S(1)} %get-tuple-element.40), channel_id=1, source_target_pairs={{0,3},{1,2},{2,1},{3,0},{4,7},{5,6},{6,5},{7,4},{8,11},{9,10},{10,... | collective-permute-start | bytes 147464 | tf_op jit(solution)/shard_map/ppermute | solution.py:533
  6.2 0.0 collective-permute-done.refs_1_
  6.2 2.5 %shard_map.87 = (f32[3,4,32,8,128]{4,3,2,1,0:T(8,128)S(1)}, f32[3,4,32,8,128]{4,3,2,1,0:T(8,128)S(1)}, f32[3,4,32,8,128]{4,3,2,1,0:T(8,128)S(1)}, f32[3,4,32,8,1...) custom-call(f32[3,2,256,128]{3,2,1,0:T(8,128)S(1)} %get-tuple-elemen, ...), custom_call_target="tpu_custom_call", output_to_operand_aliasing={{0}: (4, {}), {1}: (5, {}), {2}: (6, {})} | custom-call | bytes 10000000 | tf_op jit(solution)/shard_map/pallas_call | solution.py:534
  8.7 0.0 collective-permute-done.1
  8.7 0.4 %collective-permute-done.2 = f32[3,2,2,8,128]{4,3,2,1,0:T(8,128)S(1)} collective-permute-done((f32[3,2,2,8,128]{4,3,2,1,0:T(8,128)S(1)}, f32[3,2,2,8,128]{4,3,2,1,0:T(8,128)S(1)}, u32[]{:S(2)}, u32[]{:S(2)}) %collective-permute-start.2) | collective-permute-done | bytes 49184 | tf_op jit(solution)/shard_map/ppermute | solution.py:533
  9.1 0.3 %collective-permute-start.3 = (f32[2,3,2,2,8,128]{5,4,3,2,1,0:T(8,128)S(1)}, f32[2,3,2,2,8,128]{5,4,3,2,1,0:T(8,128)S(1)}, u32[]{:S(2)}, u32[]{:S(2)}) collective-permute-start(f32[2,3,2,2,8,128]{5,4,3,2,1,0:T(8,128)S(1)} %pad_maximum_fusion.refs_7_), channel_id=1, source_target_pairs={{0,1},{1,0},{2,3},{3,2},{4,5},{5,4},{6,7},{7,6},{8,9},{9,8},{10,11... | collective-permute-start | bytes 294920 | tf_op jit(solution)/shard_map/ppermute | solution.py:546
  9.4 0.9 %shard_map.88 = (f32[3,2,256,128]{3,2,1,0:T(8,128)S(1)}, f32[5,2,2,8,128]{4,3,2,1,0:T(8,128)S(1)}) custom-call(f32[3,4,32,8,128]{4,3,2,1,0:T(8,128)S(1)} %get-tuple-element.42.refs_0_.refs_1_, f32[3,4,32,8,128]{4,3,2,1,0:T(8,128)S(1)} %get-tuple-element.43.refs_1_, f32[3,4,32,8,128]{4,3,2,1,0:T(8,128)S(1)} %get-tuple-element.44.refs_2_, ...), custom_call_target="tpu_custom_call" | custom-call | bytes 10000000 | tf_op jit(solution)/shard_map/pallas_call | solution.py:547
  10.3 0.1 collective-permute-done.3.refs_8_
  10.4 1.1 %shard_map.89 = (f32[2,256,128]{2,1,0:T(8,128)}, f32[2,256,128]{2,1,0:T(8,128)}, f32[2,256,128]{2,1,0:T(8,128)}) custom-call(f32[3,4,32,8,128]{4,3,2,1,0:T(8,128)S(1)} %get-tuple-element.38.refs_5_.refs_0_, f32[3,4,32,8,128]{4,3,2,1,0:T(8,128)S(1)} %get-tuple-element.42.refs_0_.refs_1_, f32[3,2,256,128]{3,2,1,0:T(8,128)S(1)} %get-tuple-element.46.refs_2_, ...), custom_call_target="tpu_custom_call" | custom-call | bytes 1000000 | tf_op jit(solution)/shard_map/pallas_call | solution.py:563
  (1 shorter events, 0.0 us)
Async XLA Ops:
  1.8 4.3 %collective-permute-start = (f32[3,2,256,128]{3,2,1,0:T(8,128)S(1)}, f32[3,2,256,128]{3,2,1,0:T(8,128)S(1)}, u32[]{:S(2)}, u32[]{:S(2)}) collective-permute-start(f32[3,2,256,128]{3,2,1,0:T(8,128)S(1)} %get-tuple-element.28.own.refs_0_), channel_id=1, source_target_pairs={{0,1},{1,0},{2,3},{3,2},{4,5},{5,4},{6,7},{7,6},{8,9},{9,8},{10,11... | collective-permute-start | bytes 2359304 | tf_op jit(solution)/shard_map/ppermute | solution.py:519
  2.3 6.3 %collective-permute-start.1 = (f32[3,2,2,8,128]{4,3,2,1,0:T(8,128)S(1)}, f32[3,2,2,8,128]{4,3,2,1,0:T(8,128)S(1)}, u32[]{:S(2)}, u32[]{:S(2)}) collective-permute-start(f32[3,2,2,8,128]{4,3,2,1,0:T(8,128)S(1)} %get-tuple-element.39), channel_id=1, source_target_pairs={{0,1},{1,0},{2,4},{3,5},{4,2},{5,3},{6,8},{7,9},{8,6},{9,7},{10,12... | collective-permute-start | bytes 147464 | tf_op jit(solution)/shard_map/ppermute | solution.py:520
  2.9 6.2 %collective-permute-start.2 = (f32[3,2,2,8,128]{4,3,2,1,0:T(8,128)S(1)}, f32[3,2,2,8,128]{4,3,2,1,0:T(8,128)S(1)}, u32[]{:S(2)}, u32[]{:S(2)}) collective-permute-start(f32[3,2,2,8,128]{4,3,2,1,0:T(8,128)S(1)} %get-tuple-element.40), channel_id=1, source_target_pairs={{0,3},{1,2},{2,1},{3,0},{4,7},{5,6},{6,5},{7,4},{8,11},{9,10},{10,... | collective-permute-start | bytes 147464 | tf_op jit(solution)/shard_map/ppermute | solution.py:533
  9.1 1.4 %collective-permute-start.3 = (f32[2,3,2,2,8,128]{5,4,3,2,1,0:T(8,128)S(1)}, f32[2,3,2,2,8,128]{5,4,3,2,1,0:T(8,128)S(1)}, u32[]{:S(2)}, u32[]{:S(2)}) collective-permute-start(f32[2,3,2,2,8,128]{5,4,3,2,1,0:T(8,128)S(1)} %pad_maximum_fusion.refs_7_), channel_id=1, source_target_pairs={{0,1},{1,0},{2,3},{3,2},{4,5},{5,4},{6,7},{7,6},{8,9},{9,8},{10,11... | collective-permute-start | bytes 294920 | tf_op jit(solution)/shard_map/ppermute | solution.py:546
